TPU v7x, 32 devices: a whole 2x2x4 slice. The times are simulated.
32 devices in a mesh: dp: 8 (over z, x), fsdp: 4 (over y, core).
Axes of the slice: x: 2, y: 2, z: 4, core: 2. Of those that a mesh axis runs over, the one named last changes fastest.
Arguments:
- tokens: bfloat16 [128, 256, 512], P(('dp', 'fsdp')), may hold values from -6 to 6
- cotangent: bfloat16 [128, 256, 512], P(('dp', 'fsdp')), may hold values from -6 to 6
- reveal_order: int32 [128, 256], P(('dp', 'fsdp')), may hold values from 0 to 255, each once within a row
- reveal_step: int32 [128], P(('dp', 'fsdp')), may hold values from 1 to 256
- lengths: int32 [128], P(('dp', 'fsdp')), may hold values from 224 to 256
- weight_qkv: float32 [512, 1536], P(('dp', 'fsdp')), may hold values from -0.25 to 0.25
- weight_out: float32 [512, 512], P(('dp', 'fsdp')), may hold values from -1 to 1
- weight_up: float32 [512, 2048], P(('dp', 'fsdp')), may hold values from -0.25 to 0.25
- weight_down: float32 [2048, 512], P(('dp', 'fsdp')), may hold values from -0.125 to 0.125
- vectors: float32 [5, 512], P(None, ('dp', 'fsdp')), may hold values from -4 to 4, as said below
- moment_qkv: float32 [512, 1536], P(('dp', 'fsdp')), may hold values from -64 to 64
- square_qkv: float32 [512, 1536], P(('dp', 'fsdp')), may hold values from 8.192 to 32.768
- moment_out: float32 [512, 512], P(('dp', 'fsdp')), may hold values from -20 to 20
- square_out: float32 [512, 512], P(('dp', 'fsdp')), may hold values from 0.73728 to 2.94912
- moment_up: float32 [512, 2048], P(('dp', 'fsdp')), may hold values from -32 to 32
- square_up: float32 [512, 2048], P(('dp', 'fsdp')), may hold values from 2.94912 to 11.79648
- moment_down: float32 [2048, 512], P(('dp', 'fsdp')), may hold values from -64 to 64
- square_down: float32 [2048, 512], P(('dp', 'fsdp')), may hold values from 11.79648 to 47.18592
- moment_vec: float32 [5, 512], P(None, ('dp', 'fsdp')), may hold values from -64 to 64
- square_vec: float32 [5, 512], P(None, ('dp', 'fsdp')), may hold values from 11.79648 to 47.18592
Outputs:
- block_output: bfloat16 [128, 256, 512], P(('dp', 'fsdp'))
- input_grad: float32 [128, 256, 512], P(('dp', 'fsdp'))
- new_moment_qkv: float32 [512, 1536], P(('dp', 'fsdp'))
- new_square_qkv: float32 [512, 1536], P(('dp', 'fsdp'))
- new_weight_qkv: float32 [512, 1536], P(('dp', 'fsdp'))
- new_moment_out: float32 [512, 512], P(('dp', 'fsdp'))
- new_square_out: float32 [512, 512], P(('dp', 'fsdp'))
- new_weight_out: float32 [512, 512], P(('dp', 'fsdp'))
- new_moment_up: float32 [512, 2048], P(('dp', 'fsdp'))
- new_square_up: float32 [512, 2048], P(('dp', 'fsdp'))
- new_weight_up: float32 [512, 2048], P(('dp', 'fsdp'))
- new_moment_down: float32 [2048, 512], P(('dp', 'fsdp'))
- new_square_down: float32 [2048, 512], P(('dp', 'fsdp'))
- new_weight_down: float32 [2048, 512], P(('dp', 'fsdp'))
- new_moment_vec: float32 [5, 512], P(None, ('dp', 'fsdp'))
- new_square_vec: float32 [5, 512], P(None, ('dp', 'fsdp'))
- new_vectors: float32 [5, 512], P(None, ('dp', 'fsdp'))
Inputs may be any that keep to these rules, and one draw needn't show every extreme that they name: `vectors`: rows 0 and 1 lie in 0.7 to 1.3.
All inputs are finite; a program needn't handle non-finite values.
Results may differ from a plain program's by a relative error of at most 0.0085.
The roundings to bfloat16 on the way count: a program that leaves them out, or rounds other values in their place, can miss the bound.
Values may be sent and summed in bfloat16 or wider, within the bound.
No kernel may reach another device: no remote copies, remote signals or barrier semaphores. Data moves between devices by JAX's collectives and lax.ppermute only.
A program may use at most 128 MiB of HBM per device.

v0:
```python
import jax
import jax.numpy as jnp
from jax import lax
from jax.sharding import PartitionSpec as P

D = 512
HEADS = 8
HEAD = 64
MICRO = 2
STEP = 10


norm_epsilon = 1e-05
beta_first = 0.9
beta_second = 0.999
adam_epsilon = 1e-08
weight_decay = 0.1
matrix_rate = 0.02
output_rate = 0.1
vector_rate = 0.2
masked_score = -1000000000.0


def layer_norm(values, gain, shift):
    centred = values - jnp.mean(values, axis=-1, keepdims=True)
    spread = jnp.mean(centred * centred, axis=-1, keepdims=True)
    return centred * lax.rsqrt(spread + norm_epsilon) * gain + shift


def attention_scores(qkv_split, key_valid):
    scores = jnp.einsum(
        "cqhd,ckhd->chqk",
        qkv_split[:, :, 0],
        qkv_split[:, :, 1],
        preferred_element_type=jnp.float32,
    ) * HEAD ** (-0.5)
    return jnp.where(key_valid[:, None, None, :], scores, masked_score)


def forward_pass(gathered, inputs, masked, key_valid):
    qkv_full, out_full, up_full, down_full, vec_full = gathered
    vec_wide = vec_full.astype(jnp.float32)
    span_count, seq_len = (inputs.shape[0], inputs.shape[1])
    started = jnp.where(masked[..., None], vec_wide[4], inputs.astype(jnp.float32))
    normed = layer_norm(started, vec_wide[0], vec_wide[2]).astype(jnp.bfloat16)
    projected = jnp.einsum(
        "csd,de->cse", normed, qkv_full, preferred_element_type=jnp.float32
    ).astype(jnp.bfloat16)
    qkv_split = projected.reshape(span_count, seq_len, 3, HEADS, HEAD)
    scores = attention_scores(qkv_split, key_valid)
    row_peak = jnp.max(scores, axis=-1, keepdims=True)
    exp_scores = jnp.exp(scores - row_peak)
    row_total = jnp.sum(exp_scores, axis=-1, keepdims=True)
    probability = exp_scores / row_total
    log_total = row_peak + jnp.log(row_total)
    attended = jnp.einsum(
        "chqk,ckhd->cqhd",
        probability.astype(jnp.bfloat16),
        qkv_split[:, :, 2],
        preferred_element_type=jnp.float32,
    )
    attended = attended.astype(jnp.bfloat16).reshape(span_count, seq_len, D)
    middle = started + jnp.einsum(
        "csd,de->cse", attended, out_full, preferred_element_type=jnp.float32
    )
    second = layer_norm(middle, vec_wide[1], vec_wide[3]).astype(jnp.bfloat16)
    hidden_pre = jnp.einsum("csd,df->csf", second, up_full, preferred_element_type=jnp.float32)
    activated = jax.nn.gelu(hidden_pre).astype(jnp.bfloat16)
    result = middle + jnp.einsum(
        "csf,fd->csd", activated, down_full, preferred_element_type=jnp.float32
    )
    saved_state = (
        started,
        normed,
        qkv_split,
        log_total,
        attended,
        middle,
        second,
        hidden_pre,
        activated,
    )
    return (result, saved_state)


def backward_pass(gathered, saved_state, cot_rows, masked, key_valid):
    qkv_full, out_full, up_full, down_full, vec_full = gathered
    vec_wide = vec_full.astype(jnp.float32)
    started, normed, qkv_split, log_total, attended, middle, second, hidden_pre, activated = (
        saved_state
    )
    span_count, seq_len = (cot_rows.shape[0], cot_rows.shape[1])
    upstream = cot_rows.astype(jnp.float32)
    down_grad = upstream.astype(jnp.bfloat16)
    grad_down = jnp.einsum("csf,csd->fd", activated, down_grad, preferred_element_type=jnp.float32)
    grad_act = jnp.einsum("csd,fd->csf", down_grad, down_full, preferred_element_type=jnp.float32)
    ignored, gelu_back = jax.vjp(jax.nn.gelu, hidden_pre)
    grad_pre = gelu_back(grad_act)[0].astype(jnp.bfloat16)
    grad_up = jnp.einsum("csd,csf->df", second, grad_pre, preferred_element_type=jnp.float32)
    grad_second = jnp.einsum("csf,df->csd", grad_pre, up_full, preferred_element_type=jnp.float32)
    ignored, second_back = jax.vjp(layer_norm, middle, vec_wide[1], vec_wide[3])
    grad_middle_norm, grad_gain_two, grad_shift_two = second_back(grad_second)
    grad_middle = upstream + grad_middle_norm
    mix_grad = grad_middle.astype(jnp.bfloat16)
    grad_out = jnp.einsum("csd,cse->de", attended, mix_grad, preferred_element_type=jnp.float32)
    grad_att = jnp.einsum("cse,de->csd", mix_grad, out_full, preferred_element_type=jnp.float32)
    grad_att = grad_att.astype(jnp.bfloat16).reshape(span_count, seq_len, HEADS, HEAD)
    scores = attention_scores(qkv_split, key_valid)
    probability = jnp.exp(scores - log_total)
    grad_values = jnp.einsum(
        "chqk,cqhd->ckhd",
        probability.astype(jnp.bfloat16),
        grad_att,
        preferred_element_type=jnp.float32,
    )
    grad_probs = jnp.einsum(
        "cqhd,ckhd->chqk", grad_att, qkv_split[:, :, 2], preferred_element_type=jnp.float32
    )
    grad_scores = probability * (
        grad_probs - jnp.sum(probability * grad_probs, axis=-1, keepdims=True)
    )
    grad_scores = grad_scores.astype(jnp.bfloat16)
    grad_queries = jnp.einsum(
        "chqk,ckhd->cqhd", grad_scores, qkv_split[:, :, 1], preferred_element_type=jnp.float32
    ) * HEAD ** (-0.5)
    grad_keys = jnp.einsum(
        "chqk,cqhd->ckhd", grad_scores, qkv_split[:, :, 0], preferred_element_type=jnp.float32
    ) * HEAD ** (-0.5)
    grad_split = jnp.stack([grad_queries, grad_keys, grad_values], axis=2).astype(jnp.bfloat16)
    grad_split = grad_split.reshape(span_count, seq_len, 3 * D)
    grad_qkv = jnp.einsum("csd,cse->de", normed, grad_split, preferred_element_type=jnp.float32)
    grad_normed = jnp.einsum(
        "cse,de->csd", grad_split, qkv_full, preferred_element_type=jnp.float32
    )
    ignored, first_back = jax.vjp(layer_norm, started, vec_wide[0], vec_wide[2])
    grad_started_norm, grad_gain_one, grad_shift_one = first_back(grad_normed)
    grad_started = grad_middle + grad_started_norm
    grad_mask = jnp.sum(jnp.where(masked[..., None], grad_started, 0.0), axis=(0, 1))
    input_grad = jnp.where(masked[..., None], 0.0, grad_started)
    grad_vec = jnp.stack([grad_gain_one, grad_gain_two, grad_shift_one, grad_shift_two, grad_mask])
    return (input_grad, (grad_qkv, grad_out, grad_up, grad_down, grad_vec))


def adam_update(master, gradient, moment, square, step_rate, decay_rate):
    moment_new = beta_first * moment + (1.0 - beta_first) * gradient
    square_new = beta_second * square + (1.0 - beta_second) * gradient * gradient
    corrected = (
        moment_new
        / (1.0 - beta_first**STEP)
        / (jnp.sqrt(square_new / (1.0 - beta_second**STEP)) + adam_epsilon)
    )
    return (moment_new, square_new, master - step_rate * (corrected + decay_rate * master))


def add_tuples(running, fresh_grads):
    if running is None:
        return fresh_grads
    return tuple((summed + added for summed, added in zip(running, fresh_grads)))


def local(
    tokens,
    cotangent,
    reveal_order,
    reveal_step,
    lengths,
    weight_qkv,
    weight_out,
    weight_up,
    weight_down,
    vectors,
    moment_qkv,
    square_qkv,
    moment_out,
    square_out,
    moment_up,
    square_up,
    moment_down,
    square_down,
    moment_vec,
    square_vec,
):
    qkv_half = weight_qkv.astype(jnp.bfloat16)
    out_half = weight_out.astype(jnp.bfloat16)
    up_half = weight_up.astype(jnp.bfloat16)
    down_half = weight_down.astype(jnp.bfloat16)
    vec_half = vectors.astype(jnp.bfloat16)
    batch_spans = tokens.shape[0] // MICRO
    seq_len = tokens.shape[1]
    positions = jnp.arange(seq_len, dtype=jnp.int32)
    outputs = []
    input_grads = []
    running = None
    for micro_index in range(MICRO):
        lower = micro_index * batch_spans
        upper = lower + batch_spans
        masked = reveal_order[lower:upper] >= reveal_step[lower:upper, None]
        key_valid = positions[None, :] < lengths[lower:upper, None]
        gathered = (
            lax.all_gather(qkv_half, ("dp", "fsdp"), axis=0, tiled=True),
            lax.all_gather(out_half, ("dp", "fsdp"), axis=0, tiled=True),
            lax.all_gather(up_half, ("dp", "fsdp"), axis=0, tiled=True),
            lax.all_gather(down_half, ("dp", "fsdp"), axis=0, tiled=True),
            lax.all_gather(vec_half, ("dp", "fsdp"), axis=1, tiled=True),
        )
        result, saved_state = forward_pass(gathered, tokens[lower:upper], masked, key_valid)
        outputs.append(result.astype(jnp.bfloat16))
        back_gathered = (
            lax.all_gather(qkv_half, ("dp", "fsdp"), axis=0, tiled=True),
            lax.all_gather(out_half, ("dp", "fsdp"), axis=0, tiled=True),
            lax.all_gather(up_half, ("dp", "fsdp"), axis=0, tiled=True),
            lax.all_gather(down_half, ("dp", "fsdp"), axis=0, tiled=True),
            lax.all_gather(vec_half, ("dp", "fsdp"), axis=1, tiled=True),
        )
        input_grad, fresh_grads = backward_pass(
            back_gathered, saved_state, cotangent[lower:upper], masked, key_valid
        )
        input_grads.append(input_grad)
        grad_qkv, grad_out, grad_up, grad_down, grad_vec = fresh_grads
        shares = (
            lax.psum_scatter(grad_qkv, ("dp", "fsdp"), scatter_dimension=0, tiled=True),
            lax.psum_scatter(grad_out, ("dp", "fsdp"), scatter_dimension=0, tiled=True),
            lax.psum_scatter(grad_up, ("dp", "fsdp"), scatter_dimension=0, tiled=True),
            lax.psum_scatter(grad_down, ("dp", "fsdp"), scatter_dimension=0, tiled=True),
            lax.psum_scatter(grad_vec, ("dp", "fsdp"), scatter_dimension=1, tiled=True),
        )
        running = add_tuples(running, tuple(shares))
    block_output = jnp.concatenate(outputs, axis=0)
    input_grad = jnp.concatenate(input_grads, axis=0)
    m_qkv, s_qkv, w_qkv = adam_update(
        weight_qkv, running[0], moment_qkv, square_qkv, matrix_rate, weight_decay
    )
    m_out, s_out, w_out = adam_update(
        weight_out, running[1], moment_out, square_out, output_rate, weight_decay
    )
    m_up, s_up, w_up = adam_update(
        weight_up, running[2], moment_up, square_up, matrix_rate, weight_decay
    )
    m_down, s_down, w_down = adam_update(
        weight_down, running[3], moment_down, square_down, matrix_rate, weight_decay
    )
    m_vec, s_vec, w_vec = adam_update(vectors, running[4], moment_vec, square_vec, vector_rate, 0.0)
    return (
        block_output,
        input_grad,
        m_qkv,
        s_qkv,
        w_qkv,
        m_out,
        s_out,
        w_out,
        m_up,
        s_up,
        w_up,
        m_down,
        s_down,
        w_down,
        m_vec,
        s_vec,
        w_vec,
    )


def solution(mesh):
    return jax.shard_map(
        local,
        mesh=mesh,
        in_specs=(
            P(("dp", "fsdp"), None, None),
            P(("dp", "fsdp"), None, None),
            P(("dp", "fsdp"), None),
            P(("dp", "fsdp")),
            P(("dp", "fsdp")),
            P(("dp", "fsdp"), None),
            P(("dp", "fsdp"), None),
            P(("dp", "fsdp"), None),
            P(("dp", "fsdp"), None),
            P(None, ("dp", "fsdp")),
            P(("dp", "fsdp"), None),
            P(("dp", "fsdp"), None),
            P(("dp", "fsdp"), None),
            P(("dp", "fsdp"), None),
            P(("dp", "fsdp"), None),
            P(("dp", "fsdp"), None),
            P(("dp", "fsdp"), None),
            P(("dp", "fsdp"), None),
            P(None, ("dp", "fsdp")),
            P(None, ("dp", "fsdp")),
        ),
        out_specs=(
            P(("dp", "fsdp"), None, None),
            P(("dp", "fsdp"), None, None),
            P(("dp", "fsdp"), None),
            P(("dp", "fsdp"), None),
            P(("dp", "fsdp"), None),
            P(("dp", "fsdp"), None),
            P(("dp", "fsdp"), None),
            P(("dp", "fsdp"), None),
            P(("dp", "fsdp"), None),
            P(("dp", "fsdp"), None),
            P(("dp", "fsdp"), None),
            P(("dp", "fsdp"), None),
            P(("dp", "fsdp"), None),
            P(("dp", "fsdp"), None),
            P(None, ("dp", "fsdp")),
            P(None, ("dp", "fsdp")),
            P(None, ("dp", "fsdp")),
        ),
        check_vma=False,
    )
```

profile of v0, /device:TPU:0, one launch (start us, length us, event | category | flops | bytes accessed | tf_op | source)
XLA Modules:
  0.0 910.3 jit_solution(10841099295102615427)
XLA Ops:
  13.7 43.5 %all-gather = bf16[32,16,5]{1,2,0:T(8,128)(2,1)S(1)} all-gather(bf16[1,16,5]{1,2,0:T(8,128)(2,1)S(1)} %convert_bitcast_fusion), channel_id=1, replica_groups=mesh['dp'=8,'fsdp'=4] {'dp','fsdp'}, dimensions={0}, use_global_device_ids=true | all-gather | bytes 5280 | tf_op jit(solution)/shard_map/all_gather | solution.py:204
  62.8 38.2 %all_gather.12 = bf16[512,512]{1,0:T(8,128)(2,1)S(1)} all-gather(bf16[16,512]{1,0:T(8,128)(2,1)S(1)} %convert_element_type.132), channel_id=1, replica_groups=mesh['dp'=8,'fsdp'=4] {'dp','fsdp'}, dimensions={0}, use_global_device_ids=true | all-gather | bytes 540672 | tf_op jit(solution)/shard_map/all_gather | solution.py:201
  101.0 4.1 convolution_convert_fusion
  107.6 3.7 convolution_convert_fusion.1
  111.3 2.8 copy.131
  125.0 3.4 all-gather.7.cloned.1.call-done
  128.3 3.0 fusion.35
  137.8 4.0 bitcast_add_fusion
  141.9 140.2 %reduce-scatter.14.cloned.1.call-done = f32[64,512]{1,0:T(8,128)} async-done(((f32[2048,512]{1,0:T(8,128)}), f32[64,512]{1,0:T(8,128)}) %reduce-scatter.14.cloned.1.call-update) | async-done | bytes 131088 | tf_op jit(solution)/shard_map/reduce_scatter | solution.py:224
  284.3 53.5 %all-gather.9.cloned.1.call-done = bf16[2048,512]{1,0:T(8,128)(2,1)} async-done(((bf16[64,512]{1,0:T(8,128)(2,1)}), bf16[2048,512]{1,0:T(8,128)(2,1)}) %all-gather.9.cloned.1.call-update) | async-done | bytes 2097168 | tf_op jit(solution)/shard_map/all_gather | solution.py:203
  337.8 6.4 fusion.13
  344.2 3.5 fusion.6
  358.3 4.1 fusion.76
  372.1 3.3 fusion.79
  391.1 3.0 fusion.47
  394.2 2.8 convolution_bitcast_fusion
  397.0 3.0 fusion.16
  400.3 3.2 fusion.109
  403.5 3.5 bitcast_add_fusion.1
  407.0 4.5 fusion.60
  416.1 107.4 %reduce-scatter.16.cloned.1.call-done = f32[16,5]{1,0:T(8,128)} async-done(((f32[512,5]{1,0:T(8,128)}), f32[16,5]{1,0:T(8,128)}) %reduce-scatter.16.cloned.1.call-update) | async-done | bytes 336
  524.9 131.5 %reduce-scatter.10.cloned.1.call-done = f32[16,512]{1,0:T(8,128)} async-done(((f32[512,512]{1,0:T(8,128)}), f32[16,512]{1,0:T(8,128)}) %reduce-scatter.10.cloned.1.call-update) | async-done | bytes 32784 | tf_op jit(solution)/shard_map/reduce_scatter | solution.py:222
  657.8 101.5 %reduce-scatter.8.cloned.1.call-done = f32[16,1536]{1,0:T(8,128)} async-done(((f32[512,1536]{1,0:T(8,128)}), f32[16,1536]{1,0:T(8,128)}) %reduce-scatter.8.cloned.1.call-update) | async-done | bytes 98320 | tf_op jit(solution)/shard_map/reduce_scatter | solution.py:221
  760.9 140.7 %reduce-scatter.12.cloned.1.call-done = f32[16,2048]{1,0:T(8,128)} async-done(((f32[512,2048]{1,0:T(8,128)}), f32[16,2048]{1,0:T(8,128)}) %reduce-scatter.12.cloned.1.call-update) | async-done | bytes 131088 | tf_op jit(solution)/shard_map/reduce_scatter | solution.py:223
  (234 shorter events, 80.7 us)
Async XLA Ops:
  7.2 93.8 %all-gather.5.cloned.1.call-start = ((), (), s32[]{:S(2)}) async-start(), calls=%async_computation.5 | async-start | bytes 1622016 | tf_op jit(solution)/shard_map/all_gather | solution.py:200
  8.8 119.5 %all-gather.7.cloned.1.call-start = ((), (), s32[]{:S(2)}) async-start(), calls=%async_computation.6 | async-start | bytes 2162688 | tf_op jit(solution)/shard_map/all_gather | solution.py:202
  10.4 271.8 %reduce-scatter.14.cloned.1.call-start = ((), (), s32[]{:S(2)}) async-start(), calls=%async_computation.11 | async-start | bytes 4325376 | tf_op jit(solution)/shard_map/reduce_scatter | solution.py:224
  57.5 50.2 %copy-start.58 = (f32[1,512]{1,0:T(1,128)}, f32[1,512]{1,0:T(1,128)S(1)}, u32[]{:S(2)}) copy-start(f32[1,512]{1,0:T(1,128)S(1)} %get-tuple-element.63) | copy-start | bytes 6148
  62.8 44.9 %copy-start.55 = (f32[2,256]{1,0:T(2,128)}, f32[2,256]{1,0:T(2,128)S(1)}, u32[]{:S(2)}) copy-start(f32[2,256]{1,0:T(2,128)S(1)} %fusion.113) | copy-start | bytes 6148
  141.8 140.3 %copy-start.44 = (f32[64,512]{1,0:T(8,128)S(1)}, f32[64,512]{1,0:T(8,128)}, u32[]{:S(2)}) copy-start(f32[64,512]{1,0:T(8,128)} %param.28) | copy-start | bytes 393220
  141.8 140.3 %copy-start.45 = (f32[64,512]{1,0:T(8,128)S(1)}, f32[64,512]{1,0:T(8,128)}, u32[]{:S(2)}) copy-start(f32[64,512]{1,0:T(8,128)} %param.37) | copy-start | bytes 393220
  141.9 195.9 %all-gather.9.cloned.1.call-start = ((), (), s32[]{:S(2)}) async-start(), calls=%async_computation.7 | async-start | bytes 2162688 | tf_op jit(solution)/shard_map/all_gather | solution.py:203
  284.0 239.5 %reduce-scatter.16.cloned.1.call-start = ((), (), s32[]{:S(2)}) async-start(), calls=%async_computation.12 | async-start | bytes 270336
  391.1 265.3 %reduce-scatter.10.cloned.1.call-start = ((), (), s32[]{:S(2)}) async-start(), calls=%async_computation.9 | async-start | bytes 1081344 | tf_op jit(solution)/shard_map/reduce_scatter | solution.py:222
  394.1 365.2 %reduce-scatter.8.cloned.1.call-start = ((), (), s32[]{:S(2)}) async-start(), calls=%async_computation.8 | async-start | bytes 3244032 | tf_op jit(solution)/shard_map/reduce_scatter | solution.py:221
  400.1 501.5 %reduce-scatter.12.cloned.1.call-start = ((), (), s32[]{:S(2)}) async-start(), calls=%async_computation.10 | async-start | bytes 4325376 | tf_op jit(solution)/shard_map/reduce_scatter | solution.py:223
  414.3 110.0 %copy-start.57 = (f32[5,16]{1,0:T(8,128)S(1)}, f32[5,16]{1,0:T(8,128)}, u32[]{:S(2)}) copy-start(f32[5,16]{1,0:T(8,128)} %param.29) | copy-start | bytes 964
  414.3 110.0 %copy-start.60 = (f32[5,16]{1,0:T(8,128)S(1)}, f32[5,16]{1,0:T(8,128)}, u32[]{:S(2)}) copy-start(f32[5,16]{1,0:T(8,128)} %param.39) | copy-start | bytes 964
  414.3 242.1 %copy-start.48 = (f32[16,512]{1,0:T(8,128)S(1)}, f32[16,512]{1,0:T(8,128)}, u32[]{:S(2)}) copy-start(f32[16,512]{1,0:T(8,128)} %param.26) | copy-start | bytes 98308
  414.3 345.0 %copy-start.43 = (f32[16,1536]{1,0:T(8,128)S(1)}, f32[16,1536]{1,0:T(8,128)}, u32[]{:S(2)}) copy-start(f32[16,1536]{1,0:T(8,128)} %param.25) | copy-start | bytes 294916
  414.3 487.3 %copy-start.39 = (f32[16,2048]{1,0:T(8,128)S(1)}, f32[16,2048]{1,0:T(8,128)}, u32[]{:S(2)}) copy-start(f32[16,2048]{1,0:T(8,128)} %param.27) | copy-start | bytes 393220
  414.3 487.3 %copy-start.46 = (f32[16,2048]{1,0:T(8,128)S(1)}, f32[16,2048]{1,0:T(8,128)}, u32[]{:S(2)}) copy-start(f32[16,2048]{1,0:T(8,128)} %param.35) | copy-start | bytes 393220
  414.6 109.7 %copy-start.61 = (f32[5,16]{1,0:T(8,128)S(1)}, f32[5,16]{1,0:T(8,128)}, u32[]{:S(2)}) copy-start(f32[5,16]{1,0:T(8,128)} %param.38) | copy-start | bytes 964
  414.6 241.8 %copy-start.51 = (f32[16,512]{1,0:T(8,128)S(1)}, f32[16,512]{1,0:T(8,128)}, u32[]{:S(2)}) copy-start(f32[16,512]{1,0:T(8,128)} %param.33) | copy-start | bytes 98308
  414.6 241.8 %copy-start.52 = (f32[16,512]{1,0:T(8,128)S(1)}, f32[16,512]{1,0:T(8,128)}, u32[]{:S(2)}) copy-start(f32[16,512]{1,0:T(8,128)} %param.32) | copy-start | bytes 98308
  414.6 344.7 %copy-start.49 = (f32[16,1536]{1,0:T(8,128)S(1)}, f32[16,1536]{1,0:T(8,128)}, u32[]{:S(2)}) copy-start(f32[16,1536]{1,0:T(8,128)} %param.31) | copy-start | bytes 294916
  414.6 344.7 %copy-start.50 = (f32[16,1536]{1,0:T(8,128)S(1)}, f32[16,1536]{1,0:T(8,128)}, u32[]{:S(2)}) copy-start(f32[16,1536]{1,0:T(8,128)} %param.30) | copy-start | bytes 294916
  414.6 487.0 %copy-start.47 = (f32[16,2048]{1,0:T(8,128)S(1)}, f32[16,2048]{1,0:T(8,128)}, u32[]{:S(2)}) copy-start(f32[16,2048]{1,0:T(8,128)} %param.34) | copy-start | bytes 393220
  (49 other events, 169.8 us)
Sparse Core Ops, SparseCore 0:
  11.5 57.7 all-gather.4
  72.7 55.5 all-gather.6
  142.0 140.1 reduce-scatter.13
  285.4 52.2 all-gather.8
  391.2 132.2 reduce-scatter.15
  525.7 130.6 reduce-scatter.9
  661.8 97.4 reduce-scatter.7
  761.6 139.9 reduce-scatter.11
where the time goes:
time: 916 us; the launch traced here: 910 us
  waiting for transfers between devices  678 us (74%)
  matrix products  81.9 us (9%)
  blocking collectives  81.7 us (9%)
  other arithmetic  30.7 us (3%)
  local copies, waits for them, and re-layouts  22 us (2%)
  between operations  15.2 us (2%)
    reduce_scatter x1, waiting for transfers between devices, local(): lax.psum_scatter(grad_up, ('dp', 'fsdp'), scatter_dimension=0, tiled=True)  141 us
    reduce_scatter x1, waiting for transfers between devices, local(): lax.psum_scatter(grad_down, ('dp', 'fsdp'), scatter_dimension=0, tiled=True)  140 us
    reduce_scatter x1, waiting for transfers between devices, local(): lax.psum_scatter(grad_out, ('dp', 'fsdp'), scatter_dimension=0, tiled=True)  131 us
    unnamed x9, waiting for transfers between devices  108 us
    reduce_scatter x1, waiting for transfers between devices, local(): lax.psum_scatter(grad_qkv, ('dp', 'fsdp'), scatter_dimension=0, tiled=True)  101 us
    all_gather x1, waiting for transfers between devices, local(): lax.all_gather(down_half, ('dp', 'fsdp'), axis=0, tiled=True)  53.5 us
    all_gather x1, blocking collectives, local(): lax.all_gather(vec_half, ('dp', 'fsdp'), axis=1, tiled=True)  43.5 us
    all_gather x1, blocking collectives, local(): lax.all_gather(out_half, ('dp', 'fsdp'), axis=0, tiled=True)  38.2 us
  transfers between devices with their start and end apart: 8, of which 7 were waited for; matrix products, arithmetic and copies ran while one was open for 7% of the time, Pallas kernels for 0%

commit v1 on v0

--- a/solution.py
+++ b/solution.py
@@ -1,12 +1,15 @@
+import functools
+
 import jax
 import jax.numpy as jnp
 from jax import lax
+from jax.experimental import pallas as pl
+from jax.experimental.pallas import tpu as pltpu
 from jax.sharding import PartitionSpec as P
 
 D = 512
 HEADS = 8
 HEAD = 64
-MICRO = 2
 STEP = 10
 
 
@@ -152,10 +155,142 @@
     return (moment_new, square_new, master - step_rate * (corrected + decay_rate * master))
 
 
-def add_tuples(running, fresh_grads):
-    if running is None:
-        return fresh_grads
-    return tuple((summed + added for summed, added in zip(running, fresh_grads)))
+AXES = ("dp", "fsdp")
+LANES = 128
+
+
+def device_count(mesh):
+    return mesh.shape["dp"] * mesh.shape["fsdp"]
+
+
+def far_masks(count):
+    masks = []
+    bit = 8
+    while bit < count:
+        masks.append(bit)
+        bit *= 2
+    return masks
+
+
+def exchange(values, count, even_mask, odd_mask):
+    pairs = [(i, i ^ (odd_mask if i % 2 else even_mask)) for i in range(count)]
+    return lax.ppermute(values, AXES, pairs)
+
+
+def far_offsets(count):
+    offsets = [0]
+    for mask in far_masks(count):
+        offsets = offsets + [old + mask for old in offsets]
+    return offsets
+
+
+def block_device(me, core, place, far):
+    quarter = len(far)
+    first = jnp.where(core == 0, 4, 2)
+    second = 6 - first
+    group = place // quarter
+    near = (0, first, second, first + second)[group]
+    return me ^ near ^ far[place % quarter]
+
+
+def gather_stack(shard, count):
+    far = far_offsets(count)
+    stack = [shard] + [exchange(shard, count, offset, offset) for offset in far[1:]]
+    stack = jnp.concatenate(stack, axis=0)
+    stack = jnp.concatenate([stack, exchange(stack, count, 4, 2)], axis=0)
+    late = exchange(stack, count, 2, 4)
+    return (stack, late, exchange(stack, count, 1, 1), exchange(late, count, 1, 1))
+
+
+def assemble_kernel(me_ref, own_ref, late_ref, other_ref, other_late_ref, full_ref, *, far, rows):
+    me = me_ref[0]
+    core = me & 1
+    half = len(far) * 2
+    for place in range(half):
+        for stream, refs in ((0, (own_ref, late_ref)), (1, (other_ref, other_late_ref))):
+            for upper in range(2):
+                device = block_device(me ^ stream, core ^ stream, place + upper * half, far)
+                start = pl.multiple_of(device * rows, rows)
+                full_ref[pl.ds(start, rows), :] = refs[upper][pl.ds(place * rows, rows), :]
+
+
+def whole_vmem():
+    return pl.BlockSpec(memory_space=pltpu.VMEM)
+
+
+def assemble(me, stacks, count):
+    half, columns = stacks[0].shape
+    far = far_offsets(count)
+    rows = half // (2 * len(far))
+    return pl.pallas_call(
+        functools.partial(assemble_kernel, far=far, rows=rows),
+        out_shape=jax.ShapeDtypeStruct((rows * count, columns), stacks[0].dtype),
+        in_specs=[pl.BlockSpec(memory_space=pltpu.SMEM)] + [whole_vmem()] * 4,
+        out_specs=whole_vmem(),
+        name="assemble",
+    )(me, *stacks)
+
+
+def arrange_kernel(me_ref, full_ref, keep_ref, send_ref, *, far, rows):
+    me = me_ref[0]
+    core = me & 1
+    for place in range(len(far) * 4):
+        here = pl.ds(place * rows, rows)
+        device = block_device(me, core, place, far)
+        keep_ref[here, :] = full_ref[pl.ds(pl.multiple_of(device * rows, rows), rows), :]
+        device = block_device(me ^ 1, core ^ 1, place, far)
+        taken = full_ref[pl.ds(pl.multiple_of(device * rows, rows), rows), :]
+        send_ref[here, :] = taken.astype(jnp.bfloat16)
+
+
+def arrange(me, full, count):
+    total, columns = full.shape
+    return pl.pallas_call(
+        functools.partial(arrange_kernel, far=far_offsets(count), rows=total // count),
+        out_shape=(
+            jax.ShapeDtypeStruct((total // 2, columns), jnp.float32),
+            jax.ShapeDtypeStruct((total // 2, columns), jnp.bfloat16),
+        ),
+        in_specs=[pl.BlockSpec(memory_space=pltpu.SMEM), whole_vmem()],
+        out_specs=(whole_vmem(), whole_vmem()),
+        name="arrange",
+    )(me, full)
+
+
+def low(values):
+    return values.astype(jnp.bfloat16)
+
+
+def wide(values):
+    return values.astype(jnp.float32)
+
+
+def scatter_stack(keep, send, count):
+    total = keep + wide(exchange(send, count, 1, 1))
+    half = total.shape[0] // 2
+    total = total[:half] + wide(exchange(low(total[half:]), count, 2, 4))
+    half = half // 2
+    total = total[:half] + wide(exchange(low(total[half:]), count, 4, 2))
+    far = far_offsets(count)
+    rows = half // len(far)
+    own = total[:rows]
+    for place in range(1, len(far)):
+        part = low(total[place * rows : (place + 1) * rows])
+        own = own + wide(exchange(part, count, far[place], far[place]))
+    return own
+
+
+def gather_rows(me, shard, count):
+    if shard.shape[0] % 16 == 0:
+        return assemble(me, gather_stack(shard, count), count)
+    return lax.all_gather(shard, AXES, axis=0, tiled=True)
+
+
+def scatter_rows(me, full, count):
+    if (full.shape[0] // count) % 16 == 0:
+        keep, send = arrange(me, full, count)
+        return scatter_stack(keep, send, count)
+    return lax.psum_scatter(full, AXES, scatter_dimension=0, tiled=True)
 
 
 def local(
@@ -180,53 +315,37 @@
     moment_vec,
     square_vec,
 ):
-    qkv_half = weight_qkv.astype(jnp.bfloat16)
-    out_half = weight_out.astype(jnp.bfloat16)
-    up_half = weight_up.astype(jnp.bfloat16)
-    down_half = weight_down.astype(jnp.bfloat16)
-    vec_half = vectors.astype(jnp.bfloat16)
-    batch_spans = tokens.shape[0] // MICRO
-    seq_len = tokens.shape[1]
-    positions = jnp.arange(seq_len, dtype=jnp.int32)
-    outputs = []
-    input_grads = []
-    running = None
-    for micro_index in range(MICRO):
-        lower = micro_index * batch_spans
-        upper = lower + batch_spans
-        masked = reveal_order[lower:upper] >= reveal_step[lower:upper, None]
-        key_valid = positions[None, :] < lengths[lower:upper, None]
-        gathered = (
-            lax.all_gather(qkv_half, ("dp", "fsdp"), axis=0, tiled=True),
-            lax.all_gather(out_half, ("dp", "fsdp"), axis=0, tiled=True),
-            lax.all_gather(up_half, ("dp", "fsdp"), axis=0, tiled=True),
-            lax.all_gather(down_half, ("dp", "fsdp"), axis=0, tiled=True),
-            lax.all_gather(vec_half, ("dp", "fsdp"), axis=1, tiled=True),
-        )
-        result, saved_state = forward_pass(gathered, tokens[lower:upper], masked, key_valid)
-        outputs.append(result.astype(jnp.bfloat16))
-        back_gathered = (
-            lax.all_gather(qkv_half, ("dp", "fsdp"), axis=0, tiled=True),
-            lax.all_gather(out_half, ("dp", "fsdp"), axis=0, tiled=True),
-            lax.all_gather(up_half, ("dp", "fsdp"), axis=0, tiled=True),
-            lax.all_gather(down_half, ("dp", "fsdp"), axis=0, tiled=True),
-            lax.all_gather(vec_half, ("dp", "fsdp"), axis=1, tiled=True),
-        )
-        input_grad, fresh_grads = backward_pass(
-            back_gathered, saved_state, cotangent[lower:upper], masked, key_valid
-        )
-        input_grads.append(input_grad)
-        grad_qkv, grad_out, grad_up, grad_down, grad_vec = fresh_grads
-        shares = (
-            lax.psum_scatter(grad_qkv, ("dp", "fsdp"), scatter_dimension=0, tiled=True),
-            lax.psum_scatter(grad_out, ("dp", "fsdp"), scatter_dimension=0, tiled=True),
-            lax.psum_scatter(grad_up, ("dp", "fsdp"), scatter_dimension=0, tiled=True),
-            lax.psum_scatter(grad_down, ("dp", "fsdp"), scatter_dimension=0, tiled=True),
-            lax.psum_scatter(grad_vec, ("dp", "fsdp"), scatter_dimension=1, tiled=True),
-        )
-        running = add_tuples(running, tuple(shares))
-    block_output = jnp.concatenate(outputs, axis=0)
-    input_grad = jnp.concatenate(input_grads, axis=0)
+    me = (lax.axis_index("dp") * lax.axis_size("fsdp") + lax.axis_index("fsdp")).astype(jnp.int32)[None]
+    count = lax.axis_size("dp") * lax.axis_size("fsdp")
+    vector_rows = jnp.pad(low(vectors).T, ((0, 0), (0, LANES - vectors.shape[0])))
+    first = gather_rows(me, jnp.concatenate([low(weight_qkv), vector_rows], axis=1), count)
+    second = gather_rows(me, jnp.concatenate([low(weight_out), low(weight_up)], axis=1), count)
+    down_full = gather_rows(me, low(weight_down), count)
+    gathered = (
+        first[:, : 3 * D],
+        second[:, :D],
+        second[:, D:],
+        down_full,
+        first[:, 3 * D : 3 * D + vectors.shape[0]].T,
+    )
+    positions = jnp.arange(tokens.shape[1], dtype=jnp.int32)
+    masked = reveal_order >= reveal_step[:, None]
+    key_valid = positions[None, :] < lengths[:, None]
+    result, saved_state = forward_pass(gathered, tokens, masked, key_valid)
+    block_output = low(result)
+    input_grad, fresh_grads = backward_pass(gathered, saved_state, cotangent, masked, key_valid)
+    grad_qkv, grad_out, grad_up, grad_down, grad_vec = fresh_grads
+    share_down = scatter_rows(me, grad_down, count)
+    share_second = scatter_rows(me, jnp.concatenate([grad_out, grad_up], axis=1), count)
+    vec_columns = jnp.pad(grad_vec.T, ((0, 0), (0, LANES - vectors.shape[0])))
+    share_first = scatter_rows(me, jnp.concatenate([grad_qkv, vec_columns], axis=1), count)
+    running = (
+        share_first[:, : 3 * D],
+        share_second[:, :D],
+        share_second[:, D:],
+        share_down,
+        share_first[:, 3 * D : 3 * D + vectors.shape[0]].T,
+    )
     m_qkv, s_qkv, w_qkv = adam_update(
         weight_qkv, running[0], moment_qkv, square_qkv, matrix_rate, weight_decay
     )

time: 916 us -> 227 us (0.25)
  waiting for transfers between devices: 678 us -> 32.5 us
  blocking collectives: 81.7 us -> 0 us
  starting transfers between devices: 0.72 us -> 46.4 us
  Pallas kernels: 0 us -> 21.7 us
  matrix products: 81.9 us -> 61.9 us
  between operations: 15.2 us -> 1.76 us
    reduce_scatter x4 -> x0, waiting for transfers between devices: 514 us -> none  [the longest x1 141 us: local(): lax.psum_scatter(grad_up, ('dp', 'fsdp'), scatter_dimension=0, tiled=True)]
    unnamed x9 -> x0, waiting for transfers between devices: 108 us -> none
    all_gather x2 -> x0, blocking collectives: 81.7 us -> none  [the longest x1 43.5 us: local(): lax.all_gather(vec_half, ('dp', 'fsdp'), axis=1, tiled=True)]
    all_gather x3 -> x0, waiting for transfers between devices: 56.8 us -> none  [the longest x1 53.5 us: local(): lax.all_gather(down_half, ('dp', 'fsdp'), axis=0, tiled=True)]
    ppermute x0 -> x39, starting transfers between devices: none -> 46.4 us  [exchange(): return lax.ppermute(values, AXES, pairs)]
    ppermute x0 -> x39, waiting for transfers between devices: none -> 32.5 us  [exchange(): return lax.ppermute(values, AXES, pairs)]
    pallas_call x0 -> x6, Pallas kernels: none -> 21.7 us  [the longest x3 12.7 us: arrange(): pl.pallas_call(functools.partial(arrange_kernel, far=far_offsets(count),...]
  transfers between devices with their start and end apart: 8 -> 39, of which waited for: 7 -> 11; matrix products, arithmetic and copies ran while one was open for 7% -> 25% of each run, Pallas kernels for 0% -> 6%
where the time goes in v1:
time: 227 us; the launch traced here: 223 us
  matrix products  61.9 us (27%)
  starting transfers between devices  46.4 us (20%)
  other arithmetic  35.5 us (16%)
  waiting for transfers between devices  32.5 us (14%)
  local copies, waits for them, and re-layouts  23.3 us (10%)
  Pallas kernels  21.7 us (10%)
    ppermute x39, starting transfers between devices, exchange(): return lax.ppermute(values, AXES, pairs)  46.4 us
    ppermute x39, waiting for transfers between devices, exchange(): return lax.ppermute(values, AXES, pairs)  32.5 us
    unnamed x107, local copies, waits for them, and re-layouts  13.8 us
    pallas_call x3, Pallas kernels, arrange(): pl.pallas_call(functools.partial(arrange_kernel, far=far_offsets(count),...  12.7 us
    pallas_call x3, Pallas kernels, assemble(): pl.pallas_call(functools.partial(assemble_kernel, far=far, rows=rows), ou...  9.05 us
    dot_general x1, matrix products, backward_pass(): jnp.einsum('csd,fd->csf', down_grad, down_full, preferred_element_type=jn...  7.38 us
    dot_general x1, matrix products, backward_pass(): jnp.einsum('chqk,cqhd->ckhd', probability.astype(jnp.bfloat16), grad_att,...  5.69 us
    dot_general x1, matrix products, backward_pass(): jnp.einsum('cqhd,ckhd->chqk', grad_att, qkv_split[:, :, 2], preferred_ele...  5.51 us
  transfers between devices with their start and end apart: 39, of which 11 were waited for; matrix products, arithmetic and copies ran while one was open for 25% of the time, Pallas kernels for 6%

profile of v1, /device:TPU:0, one launch (start us, length us, event | category | flops | bytes accessed | tf_op | source)
XLA Modules:
  0.0 223.1 jit_solution(678006244191217637)
XLA Ops:
  2.4 4.1 %collective-permute-start.1 = (bf16[16,1664]{1,0:T(8,128)(2,1)S(1)}, bf16[16,1664]{1,0:T(8,128)(2,1)S(1)}, u32[]{:S(2)}, u32[]{:S(2)}) collective-permute-start(bf16[16,1664]{1,0:T(8,128)(2,1)S(1)} %get-tuple-element.147), channel_id=1, source_target_pairs={{0,16},{1,17},{2,18},{3,19},{4,20},{5,21},{6,22},{7,23},{8,24},{9,... | collective-permute-start | bytes 159752 | tf_op jit(solution)/shard_map/ppermute | solution.py:177
  9.7 3.8 %collective-permute-start.16 = (bf16[64,512]{1,0:T(8,128)(2,1)S(1)}, bf16[64,512]{1,0:T(8,128)(2,1)S(1)}, u32[]{:S(2)}, u32[]{:S(2)}) collective-permute-start(bf16[64,512]{1,0:T(8,128)(2,1)S(1)} %get-tuple-element.135), channel_id=1, source_target_pairs={{0,24},{1,25},{2,26},{3,27},{4,28},{5,29},{6,30},{7,31},{8,16},{9,... | collective-permute-start | bytes 196616 | tf_op jit(solution)/shard_map/ppermute | solution.py:177
  32.4 5.5 %collective-permute-done.10 = bf16[64,2560]{1,0:T(8,128)(2,1)S(1)} collective-permute-done((bf16[64,2560]{1,0:T(8,128)(2,1)S(1)}, bf16[64,2560]{1,0:T(8,128)(2,1)S(1)}, u32[]{:S(2)}, u32[]{:S(2)}) %collective-permute-start.10) | collective-permute-done | bytes 327712 | tf_op jit(solution)/shard_map/ppermute | solution.py:177
  44.2 11.0 %collective-permute-done.18.late_ref = bf16[512,512]{1,0:T(8,128)(2,1)} collective-permute-done((bf16[512,512]{1,0:T(8,128)(2,1)}, bf16[512,512]{1,0:T(8,128)(2,1)}, u32[]{:S(2)}, u32[]{:S(2)}) %collective-permute-start.18) | collective-permute-done | bytes 524320 | tf_op jit(solution)/shard_map/ppermute | solution.py:177
  62.1 4.0 %convolution_convert_fusion = bf16[4,256,1536]{2,1,0:T(8,128)(2,1)} fusion(bf16[512,1664]{1,0:T(8,128)(2,1)S(1)} %copy-done.19, bf16[4,256,512]{2,1,0:T(8,128)(2,1)S(1)} %copy-done.5, f32[512]{0:T(512)S(1)} %get-tuple-element.106, f32[512]{0:T(512)S(1)} %get-tuple-element.107, f32[4,256]{1,0:T(4,128)S(1)} %fusion.53, ...), kind=kOutput, calls=%fused_computation.27 | convolution fusion | flops 1615855616 | bytes 5782528 | tf_op jit(solution)/shard_map/csd,de->cse/dot_general | solution.py:49
  66.1 3.2 %copy.125 = bf16[4,256,1536]{1,2,0:T(8,128)(2,1)S(1)} copy(bf16[4,256,1536]{2,1,0:T(8,128)(2,1)} %convolution_convert_fusion) | data formatting | bytes 6291456 | tf_op jit(solution)/shard_map/convert_element_type | solution.py:51
  74.8 3.3 %fusion.28 = bf16[4,8,64,256]{3,2,1,0:T(8,128)(2,1)} fusion(f32[4,8,256]{2,1,0:T(8,128)S(1)} %fusion.10, f32[4,8,256]{2,1,0:T(8,128)S(1)} %get-tuple-element.149, f32[4,8,256,256]{2,3,1,0:T(8,128)S(1)} %get-tuple-element.150, pred[4,256]{1,0:T(4,128)(4,1)S(1)} %iota_compare_fusion.1, bf16[4,256,3,8,64]{1,4,3,2,0:T(8,128)(2,1)S(1)} %bitcast.123), kind=kOutput, calls=%fused_computation.66 | convolution fusion | flops 279445504 | bytes 10552320 | tf_op jit(solution)/shard_map/chqk,ckhd->cqhd/dot_general | solution.py:59
  78.1 3.0 %assemble.5 = bf16[2048,512]{1,0:T(8,128)(2,1)} custom-call(s32[1]{0:T(128)} %bitcast.me_ref, bf16[512,512]{1,0:T(8,128)(2,1)} %constant_dynamic-update-slice_fusion.10.own_ref, bf16[512,512]{1,0:T(8,128)(2,1)} %collective-permute-done.18.late_ref, bf16[512,512]{1,0:T(8,128)(2,1)} %collective-permute-done.19.other_ref, ...), custom_call_target="tpu_custom_call" | custom-call | tf_op jit(solution)/shard_map/assemble/pallas_call | solution.py:225
  81.1 3.4 %assemble.4 = bf16[512,2560]{1,0:T(8,128)(2,1)} custom-call(s32[1]{0:T(128)} %bitcast.me_ref, bf16[128,2560]{1,0:T(8,128)(2,1)} %constant_dynamic-update-slice_fusion.5.own_ref, bf16[128,2560]{1,0:T(8,128)(2,1)} %collective-permute-done.11.late_ref, bf16[128,2560]{1,0:T(8,128)(2,1)} %collective-permute-done.12.other_ref, ...), custom_call_target="tpu_custom_call" | custom-call | tf_op jit(solution)/shard_map/assemble/pallas_call | solution.py:225
  90.1 3.8 %add_convert_fusion = bf16[4,256,512]{2,1,0:T(8,128)(2,1)} fusion(f32[4,256,512]{2,1,0:T(8,128)S(1)} %get-tuple-element.152, bf16[2048,512]{1,0:T(8,128)(2,1)S(1)} %copy-done.18, f32[4,256,2048]{2,1,0:T(8,128)S(1)} %fusion.25), kind=kOutput, calls=%fused_computation.52 | convolution fusion | flops 2167406592 | bytes 13631488 | tf_op jit(solution)/shard_map/csf,fd->csd/dot_general | solution.py:72
  93.9 7.4 %fusion.6 = bf16[4,256,2048]{2,1,0:T(8,128)(2,1)S(1)} fusion(f32[4,256,2048]{2,1,0:T(8,128)S(1)} %fusion.25, bf16[4,256,512]{2,1,0:T(8,128)(2,1)S(1)} %copy-done.13, bf16[2048,512]{1,0:T(8,128)(2,1)S(1)} %copy-done.18), kind=kOutput, calls=%fused_computation.8 | convolution fusion | flops 2189426688 | bytes 15728640 | tf_op jit(solution)/shard_map/csd,fd->csf/dot_general | solution.py:99
  101.3 4.9 %convolution_bitcast_fusion.1.full_ref = f32[2048,512]{1,0:T(8,128)} fusion(bf16[4,256,512]{2,1,0:T(8,128)(2,1)S(1)} %copy-done.13, f32[4,256,2048]{2,1,0:T(8,128)S(1)} %fusion.25), kind=kOutput, calls=%fused_computation.32 | convolution fusion | flops 2166358016 | bytes 13631488 | tf_op jit(solution)/shard_map/csf,csd->fd/dot_general | solution.py:98
  106.2 2.9 %multiply_reduce_fusion.1 = (f32[512]{0:T(512)S(1)}, f32[4,256]{1,0:T(4,128)S(1)}, f32[512]{0:T(512)S(1)}, f32[4,256,512]{2,1,0:T(8,128)S(1)}) fusion(f32[4,256,512]{2,1,0:T(8,128)S(1)} %get-tuple-element.152, f32[4,256]{1,0:T(4,128)S(1)} %fusion.54, f32[4,256]{1,0:T(4,128)S(1)} %broadcast_multiply_fusion, f32[512]{0:T(512)S(1)} %get-tuple-element.104, ...), kind=kOutput, calls=%fused_computation.44 | convolution fusion | flops 2151675904 | bytes 10504192 | tf_op jit(solution)/shard_map/csf,df->csd/dot_general | solution.py:103
  116.6 5.7 %fusion.34 = bf16[4,256,1,8,64]{1,4,3,0,2:T(8,128)(2,1)S(1)} fusion(bf16[4,256,8,64]{1,3,2,0:T(8,128)(2,1)} %bitcast.127, f32[4,8,256]{2,1,0:T(8,128)S(1)} %log_add_fusion, f32[4,8,256,256]{2,3,1,0:T(8,128)} %copy-done, pred[4,256]{1,0:T(4,128)(4,1)S(1)} %iota_compare_fusion.1), kind=kOutput, calls=%fused_computation.72 | convolution fusion | flops 277348352 | bytes 10519552 | tf_op jit(solution)/shard_map/chqk,cqhd->ckhd/dot_general | solution.py:113
  122.4 5.5 %multiply_reduce_fusion = (f32[4,8,256]{2,1,0:T(8,128)S(1)}, f32[4,8,256,256]{2,3,1,0:T(8,128)S(1)}) fusion(f32[4,8,256]{2,1,0:T(8,128)S(1)} %log_add_fusion, f32[4,8,256,256]{2,3,1,0:T(8,128)} %copy-done, pred[4,256]{1,0:T(4,128)(4,1)S(1)} %iota_compare_fusion.1, bf16[4,256,8,64]{1,3,2,0:T(8,128)(2,1)S(1)} %bitcast.128, ...), kind=kOutput, calls=%fused_computation.15 | convolution fusion | flops 278913024 | bytes 18940928 | tf_op jit(solution)/shard_map/cqhd,ckhd->chqk/dot_general | solution.py:119
  137.4 4.0 %convolution_bitcast_fusion = f32[512,1536]{1,0:T(8,128)} fusion(bf16[4,256,1536]{1,2,0:T(8,128)(2,1)S(1)} %bitcast.130, bf16[4,256,512]{2,1,0:T(8,128)(2,1)S(1)} %copy-done.6, f32[512]{0:T(512)S(1)} %get-tuple-element.106, f32[512]{0:T(512)S(1)} %get-tuple-element.107, f32[4,256]{1,0:T(4,128)S(1)} %fusion.53, f32[4,256]{1,0:T(4,128)S(1)} %broadcast_multiply_fusion.1, ...), kind=kOutput, calls=%fused_computation.31 | convolution fusion | flops 1614282752 | bytes 7355392 | tf_op jit(solution)/shard_map/csd,cse->de/dot_general | solution.py:134
  141.4 4.1 %arrange.5 = (f32[1024,512]{1,0:T(8,128)}, bf16[1024,512]{1,0:T(8,128)(2,1)}) custom-call(s32[1]{0:T(128)} %bitcast.me_ref, f32[2048,512]{1,0:T(8,128)} %convolution_bitcast_fusion.1.full_ref), custom_call_target="tpu_custom_call" | custom-call | tf_op jit(solution)/shard_map/arrange/pallas_call | solution.py:248
  150.0 3.9 %select_maximum_fusion.full_ref = f32[512,1664]{1,0:T(8,128)} fusion(f32[512,5]{1,0:T(8,128)S(1)} %bitcast.131, f32[512,1536]{1,0:T(8,128)} %convolution_bitcast_fusion), kind=kLoop, calls=%fused_computation.29 | loop fusion | flops 2555904 | bytes 6563840 | tf_op jit(solution)/shard_map/concatenate | solution.py:341
  153.9 3.8 %arrange.3 = (f32[256,1664]{1,0:T(8,128)}, bf16[256,1664]{1,0:T(8,128)(2,1)}) custom-call(s32[1]{0:T(128)} %bitcast.me_ref, f32[512,1664]{1,0:T(8,128)} %select_maximum_fusion.full_ref), custom_call_target="tpu_custom_call" | custom-call | tf_op jit(solution)/shard_map/arrange/pallas_call | solution.py:248
  159.6 4.9 %convolution_bitcast_fusion.2 = f32[512,2048]{1,0:T(8,128)S(1)} fusion(bf16[4,256,2048]{2,1,0:T(8,128)(2,1)} %copy-done.12, f32[4,256,512]{2,1,0:T(8,128)S(1)} %copy-done.2, f32[512]{0:T(512)S(1)} %get-tuple-element.105, f32[512]{0:T(512)S(1)} %get-tuple-element.104, f32[4,256]{1,0:T(4,128)S(1)} %fusion.54, f32[4,256]{1,0:T(4,128)S(1)} %broadcast_multiply_fusion), kind=kOutput, calls=%fused_computation.33 | convolution fusion | flops 2150105088 | bytes 10498048 | tf_op jit(solution)/shard_map/csd,csf->df/dot_general | solution.py:102
  170.2 4.9 %arrange.4 = (f32[256,2560]{1,0:T(8,128)}, bf16[256,2560]{1,0:T(8,128)(2,1)}) custom-call(s32[1]{0:T(128)} %bitcast.me_ref, f32[512,2560]{1,0:T(8,128)} %pad_maximum_fusion.full_ref), custom_call_target="tpu_custom_call" | custom-call | tf_op jit(solution)/shard_map/arrange/pallas_call | solution.py:248
  183.9 4.9 %collective-permute-start.26 = (bf16[16,1664]{1,0:T(8,128)(2,1)S(1)}, bf16[16,1664]{1,0:T(8,128)(2,1)S(1)}, u32[]{:S(2)}, u32[]{:S(2)}) collective-permute-start(bf16[16,1664]{1,0:T(8,128)(2,1)S(1)} %get-tuple-element.143), channel_id=1, source_target_pairs={{0,24},{1,25},{2,26},{3,27},{4,28},{5,29},{6,30},{7,31},{8,16},{9,... | collective-permute-start | bytes 159752 | tf_op jit(solution)/shard_map/ppermute | solution.py:177
  211.6 3.3 %collective-permute-start.32 = (bf16[16,2560]{1,0:T(8,128)(2,1)S(1)}, bf16[16,2560]{1,0:T(8,128)(2,1)S(1)}, u32[]{:S(2)}, u32[]{:S(2)}) collective-permute-start(bf16[16,2560]{1,0:T(8,128)(2,1)S(1)} %get-tuple-element.137), channel_id=1, source_target_pairs={{0,24},{1,25},{2,26},{3,27},{4,28},{5,29},{6,30},{7,31},{8,16},{9,... | collective-permute-start | bytes 245768 | tf_op jit(solution)/shard_map/ppermute | solution.py:177
  218.3 2.9 %collective-permute-done.31 = bf16[16,2560]{1,0:T(8,128)(2,1)S(1)} collective-permute-done((bf16[16,2560]{1,0:T(8,128)(2,1)S(1)}, bf16[16,2560]{1,0:T(8,128)(2,1)S(1)}, u32[]{:S(2)}, u32[]{:S(2)}) %collective-permute-start.31) | collective-permute-done | bytes 81952 | tf_op jit(solution)/shard_map/ppermute | solution.py:177
  (257 shorter events, 113.3 us)
Async XLA Ops:
  2.4 13.9 %collective-permute-start.1 = (bf16[16,1664]{1,0:T(8,128)(2,1)S(1)}, bf16[16,1664]{1,0:T(8,128)(2,1)S(1)}, u32[]{:S(2)}, u32[]{:S(2)}) collective-permute-start(bf16[16,1664]{1,0:T(8,128)(2,1)S(1)} %get-tuple-element.147), channel_id=1, source_target_pairs={{0,16},{1,17},{2,18},{3,19},{4,20},{5,21},{6,22},{7,23},{8,24},{9,... | collective-permute-start | bytes 159752 | tf_op jit(solution)/shard_map/ppermute | solution.py:177
  6.5 9.3 %collective-permute-start = (bf16[16,1664]{1,0:T(8,128)(2,1)S(1)}, bf16[16,1664]{1,0:T(8,128)(2,1)S(1)}, u32[]{:S(2)}, u32[]{:S(2)}) collective-permute-start(bf16[16,1664]{1,0:T(8,128)(2,1)S(1)} %get-tuple-element.147), channel_id=1, source_target_pairs={{0,8},{1,9},{2,10},{3,11},{4,12},{5,13},{6,14},{7,15},{8,0},{9,1},... | collective-permute-start | bytes 159752 | tf_op jit(solution)/shard_map/ppermute | solution.py:177
  8.1 10.7 %collective-permute-start.2 = (bf16[16,1664]{1,0:T(8,128)(2,1)S(1)}, bf16[16,1664]{1,0:T(8,128)(2,1)S(1)}, u32[]{:S(2)}, u32[]{:S(2)}) collective-permute-start(bf16[16,1664]{1,0:T(8,128)(2,1)S(1)} %get-tuple-element.147), channel_id=1, source_target_pairs={{0,24},{1,25},{2,26},{3,27},{4,28},{5,29},{6,30},{7,31},{8,16},{9,... | collective-permute-start | bytes 159752 | tf_op jit(solution)/shard_map/ppermute | solution.py:177
  9.7 11.3 %collective-permute-start.16 = (bf16[64,512]{1,0:T(8,128)(2,1)S(1)}, bf16[64,512]{1,0:T(8,128)(2,1)S(1)}, u32[]{:S(2)}, u32[]{:S(2)}) collective-permute-start(bf16[64,512]{1,0:T(8,128)(2,1)S(1)} %get-tuple-element.135), channel_id=1, source_target_pairs={{0,24},{1,25},{2,26},{3,27},{4,28},{5,29},{6,30},{7,31},{8,16},{9,... | collective-permute-start | bytes 196616 | tf_op jit(solution)/shard_map/ppermute | solution.py:177
  16.4 8.1 %collective-permute-start.8 = (bf16[16,2560]{1,0:T(8,128)(2,1)S(1)}, bf16[16,2560]{1,0:T(8,128)(2,1)S(1)}, u32[]{:S(2)}, u32[]{:S(2)}) collective-permute-start(bf16[16,2560]{1,0:T(8,128)(2,1)S(1)} %get-tuple-element.145), channel_id=1, source_target_pairs={{0,16},{1,17},{2,18},{3,19},{4,20},{5,21},{6,22},{7,23},{8,24},{9,... | collective-permute-start | bytes 245768 | tf_op jit(solution)/shard_map/ppermute | solution.py:177
  21.0 9.7 %collective-permute-start.3 = (bf16[64,1664]{1,0:T(8,128)(2,1)S(1)}, bf16[64,1664]{1,0:T(8,128)(2,1)S(1)}, u32[]{:S(2)}, u32[]{:S(2)}) collective-permute-start(bf16[64,1664]{1,0:T(8,128)(2,1)S(1)} %pad_maximum_fusion.4), channel_id=1, source_target_pairs={{0,4},{1,3},{2,6},{3,1},{4,0},{5,7},{6,2},{7,5},{8,12},{9,11},{10,... | collective-permute-start | bytes 638984 | tf_op jit(solution)/shard_map/ppermute | solution.py:177
  22.8 18.1 %collective-permute-start.17 = (bf16[256,512]{1,0:T(8,128)(2,1)S(1)}, bf16[256,512]{1,0:T(8,128)(2,1)S(1)}, u32[]{:S(2)}, u32[]{:S(2)}) collective-permute-start(bf16[256,512]{1,0:T(8,128)(2,1)S(1)} %pad_maximum_fusion.3), channel_id=1, source_target_pairs={{0,4},{1,3},{2,6},{3,1},{4,0},{5,7},{6,2},{7,5},{8,12},{9,11},{10,... | collective-permute-start | bytes 786440 | tf_op jit(solution)/shard_map/ppermute | solution.py:177
  27.3 10.7 %collective-permute-start.10 = (bf16[64,2560]{1,0:T(8,128)(2,1)S(1)}, bf16[64,2560]{1,0:T(8,128)(2,1)S(1)}, u32[]{:S(2)}, u32[]{:S(2)}) collective-permute-start(bf16[64,2560]{1,0:T(8,128)(2,1)S(1)} %pad_maximum_fusion.2), channel_id=1, source_target_pairs={{0,4},{1,3},{2,6},{3,1},{4,0},{5,7},{6,2},{7,5},{8,12},{9,11},{10,... | collective-permute-start | bytes 983048 | tf_op jit(solution)/shard_map/ppermute | solution.py:177
  30.8 11.5 %collective-permute-start.4 = (bf16[128,1664]{1,0:T(8,128)(2,1)S(1)}, bf16[128,1664]{1,0:T(8,128)(2,1)S(1)}, u32[]{:S(2)}, u32[]{:S(2)}) collective-permute-start(bf16[128,1664]{1,0:T(8,128)(2,1)S(1)} %constant_dynamic-update-slice_fusion.own_ref), channel_id=1, source_target_pairs={{0,2},{1,5},{2,0},{3,7},{4,6},{5,1},{6,4},{7,3},{8,10},{9,13},{10,... | collective-permute-start | bytes 1277960 | tf_op jit(solution)/shard_map/ppermute | solution.py:177
  38.7 16.5 %collective-permute-start.11 = (bf16[128,2560]{1,0:T(8,128)(2,1)}, bf16[128,2560]{1,0:T(8,128)(2,1)}, u32[]{:S(2)}, u32[]{:S(2)}) collective-permute-start(bf16[128,2560]{1,0:T(8,128)(2,1)} %constant_dynamic-update-slice_fusion.5.own_ref), channel_id=1, source_target_pairs={{0,2},{1,5},{2,0},{3,7},{4,6},{5,1},{6,4},{7,3},{8,10},{9,13},{10,... | collective-permute-start | bytes 1966088 | tf_op jit(solution)/shard_map/ppermute | solution.py:177
  41.6 13.6 %collective-permute-start.18 = (bf16[512,512]{1,0:T(8,128)(2,1)}, bf16[512,512]{1,0:T(8,128)(2,1)}, u32[]{:S(2)}, u32[]{:S(2)}) collective-permute-start(bf16[512,512]{1,0:T(8,128)(2,1)} %constant_dynamic-update-slice_fusion.10.own_ref), channel_id=1, source_target_pairs={{0,2},{1,5},{2,0},{3,7},{4,6},{5,1},{6,4},{7,3},{8,10},{9,13},{10,... | collective-permute-start | bytes 1572872 | tf_op jit(solution)/shard_map/ppermute | solution.py:177
  42.4 13.4 %collective-permute-start.6 = (bf16[128,1664]{1,0:T(8,128)(2,1)S(1)}, bf16[128,1664]{1,0:T(8,128)(2,1)S(1)}, u32[]{:S(2)}, u32[]{:S(2)}) collective-permute-start(bf16[128,1664]{1,0:T(8,128)(2,1)S(1)} %collective-permute-done.4.late_ref), channel_id=1, source_target_pairs={{0,1},{1,0},{2,3},{3,2},{4,5},{5,4},{6,7},{7,6},{8,9},{9,8},{10,11... | collective-permute-start | bytes 1277960 | tf_op jit(solution)/shard_map/ppermute | solution.py:177
  43.0 35.1 %collective-permute-start.19 = (bf16[512,512]{1,0:T(8,128)(2,1)}, bf16[512,512]{1,0:T(8,128)(2,1)}, u32[]{:S(2)}, u32[]{:S(2)}) collective-permute-start(bf16[512,512]{1,0:T(8,128)(2,1)} %constant_dynamic-update-slice_fusion.10.own_ref), channel_id=1, source_target_pairs={{0,1},{1,0},{2,3},{3,2},{4,5},{5,4},{6,7},{7,6},{8,9},{9,8},{10,11... | collective-permute-start | bytes 1572872 | tf_op jit(solution)/shard_map/ppermute | solution.py:177
  44.1 37.0 %collective-permute-start.12 = (bf16[128,2560]{1,0:T(8,128)(2,1)}, bf16[128,2560]{1,0:T(8,128)(2,1)}, u32[]{:S(2)}, u32[]{:S(2)}) collective-permute-start(bf16[128,2560]{1,0:T(8,128)(2,1)} %constant_dynamic-update-slice_fusion.5.own_ref), channel_id=1, source_target_pairs={{0,1},{1,0},{2,3},{3,2},{4,5},{5,4},{6,7},{7,6},{8,9},{9,8},{10,11... | collective-permute-start | bytes 1966088 | tf_op jit(solution)/shard_map/ppermute | solution.py:177
  55.2 22.9 %collective-permute-start.20 = (bf16[512,512]{1,0:T(8,128)(2,1)}, bf16[512,512]{1,0:T(8,128)(2,1)}, u32[]{:S(2)}, u32[]{:S(2)}) collective-permute-start(bf16[512,512]{1,0:T(8,128)(2,1)} %collective-permute-done.18.late_ref), channel_id=1, source_target_pairs={{0,1},{1,0},{2,3},{3,2},{4,5},{5,4},{6,7},{7,6},{8,9},{9,8},{10,11... | collective-permute-start | bytes 1572872 | tf_op jit(solution)/shard_map/ppermute | solution.py:177
  55.2 25.9 %collective-permute-start.13 = (bf16[128,2560]{1,0:T(8,128)(2,1)}, bf16[128,2560]{1,0:T(8,128)(2,1)}, u32[]{:S(2)}, u32[]{:S(2)}) collective-permute-start(bf16[128,2560]{1,0:T(8,128)(2,1)} %collective-permute-done.11.late_ref), channel_id=1, source_target_pairs={{0,1},{1,0},{2,3},{3,2},{4,5},{5,4},{6,7},{7,6},{8,9},{9,8},{10,11... | collective-permute-start | bytes 1966088 | tf_op jit(solution)/shard_map/ppermute | solution.py:177
  145.5 33.4 %collective-permute-start.33 = (bf16[1024,512]{1,0:T(8,128)(2,1)}, bf16[1024,512]{1,0:T(8,128)(2,1)}, u32[]{:S(2)}, u32[]{:S(2)}) collective-permute-start(bf16[1024,512]{1,0:T(8,128)(2,1)} %get-tuple-element.28), channel_id=1, source_target_pairs={{0,1},{1,0},{2,3},{3,2},{4,5},{5,4},{6,7},{7,6},{8,9},{9,8},{10,11... | collective-permute-start | bytes 3145736 | tf_op jit(solution)/shard_map/ppermute | solution.py:177
  166.0 10.8 %collective-permute-start.22 = (bf16[128,1664]{1,0:T(8,128)(2,1)S(1)}, bf16[128,1664]{1,0:T(8,128)(2,1)S(1)}, u32[]{:S(2)}, u32[]{:S(2)}) collective-permute-start(bf16[128,1664]{1,0:T(8,128)(2,1)S(1)} %slice.290), channel_id=1, source_target_pairs={{0,2},{1,5},{2,0},{3,7},{4,6},{5,1},{6,4},{7,3},{8,10},{9,13},{10,... | collective-permute-start | bytes 1277960 | tf_op jit(solution)/shard_map/ppermute | solution.py:177
  175.1 14.3 %collective-permute-start.27 = (bf16[256,2560]{1,0:T(8,128)(2,1)}, bf16[256,2560]{1,0:T(8,128)(2,1)S(1)}, u32[]{:S(2)}, u32[]{:S(2)}) collective-permute-start(bf16[256,2560]{1,0:T(8,128)(2,1)} %get-tuple-element.26), channel_id=1, source_target_pairs={{0,1},{1,0},{2,3},{3,2},{4,5},{5,4},{6,7},{7,6},{8,9},{9,8},{10,11... | collective-permute-start | bytes 3932168 | tf_op jit(solution)/shard_map/ppermute | solution.py:177
  181.3 16.4 %collective-permute-start.34 = (bf16[512,512]{1,0:T(8,128)(2,1)}, bf16[512,512]{1,0:T(8,128)(2,1)}, u32[]{:S(2)}, u32[]{:S(2)}) collective-permute-start(bf16[512,512]{1,0:T(8,128)(2,1)} %slice.289), channel_id=1, source_target_pairs={{0,2},{1,5},{2,0},{3,7},{4,6},{5,1},{6,4},{7,3},{8,10},{9,13},{10,... | collective-permute-start | bytes 1572872 | tf_op jit(solution)/shard_map/ppermute | solution.py:177
  189.8 11.0 %collective-permute-start.28 = (bf16[128,2560]{1,0:T(8,128)(2,1)S(1)}, bf16[128,2560]{1,0:T(8,128)(2,1)}, u32[]{:S(2)}, u32[]{:S(2)}) collective-permute-start(bf16[128,2560]{1,0:T(8,128)(2,1)S(1)} %slice.288), channel_id=1, source_target_pairs={{0,2},{1,5},{2,0},{3,7},{4,6},{5,1},{6,4},{7,3},{8,10},{9,13},{10,... | collective-permute-start | bytes 1966088 | tf_op jit(solution)/shard_map/ppermute | solution.py:177
  205.8 9.1 %collective-permute-start.36 = (bf16[64,512]{1,0:T(8,128)(2,1)S(1)}, bf16[64,512]{1,0:T(8,128)(2,1)S(1)}, u32[]{:S(2)}, u32[]{:S(2)}) collective-permute-start(bf16[64,512]{1,0:T(8,128)(2,1)S(1)} %get-tuple-element.139), channel_id=1, source_target_pairs={{0,8},{1,9},{2,10},{3,11},{4,12},{5,13},{6,14},{7,15},{8,0},{9,1},... | collective-permute-start | bytes 196616 | tf_op jit(solution)/shard_map/ppermute | solution.py:177
  209.4 8.0 %collective-permute-start.37 = (bf16[64,512]{1,0:T(8,128)(2,1)S(1)}, bf16[64,512]{1,0:T(8,128)(2,1)S(1)}, u32[]{:S(2)}, u32[]{:S(2)}) collective-permute-start(bf16[64,512]{1,0:T(8,128)(2,1)S(1)} %get-tuple-element.141), channel_id=1, source_target_pairs={{0,16},{1,17},{2,18},{3,19},{4,20},{5,21},{6,22},{7,23},{8,24},{9,... | collective-permute-start | bytes 196616 | tf_op jit(solution)/shard_map/ppermute | solution.py:177
  209.5 8.7 %collective-permute-start.30 = (bf16[16,2560]{1,0:T(8,128)(2,1)S(1)}, bf16[16,2560]{1,0:T(8,128)(2,1)S(1)}, u32[]{:S(2)}, u32[]{:S(2)}) collective-permute-start(bf16[16,2560]{1,0:T(8,128)(2,1)S(1)} %get-tuple-element.136), channel_id=1, source_target_pairs={{0,8},{1,9},{2,10},{3,11},{4,12},{5,13},{6,14},{7,15},{8,0},{9,1},... | collective-permute-start | bytes 245768 | tf_op jit(solution)/shard_map/ppermute | solution.py:177
  (61 other events, 673.0 us)

commit v2 on v0

v2 whole, which is shorter than its diff:
```python
import functools

import jax
import jax.numpy as jnp
from jax import lax
from jax.experimental import pallas as pl
from jax.experimental.pallas import tpu as pltpu
from jax.sharding import PartitionSpec as P

D = 512
HEADS = 8
HEAD = 64
FF = 2048
HALF_FF = FF // 2
LANES = 128
ROWS = 16
STEP = 10
AXES = ("dp", "fsdp")
PARTS = 2
VMEM_BYTES = 48 * 1024 * 1024

norm_epsilon = 1e-05
beta_first = 0.9
beta_second = 0.999
adam_epsilon = 1e-08
weight_decay = 0.1
matrix_rate = 0.02
output_rate = 0.1
vector_rate = 0.2
masked_score = -1000000000.0
gelu_scale = 0.7978845608028654
gelu_cubic = 0.044715
FIRST_PAD = 224


def low(values):
    return values.astype(jnp.bfloat16)


def wide(values):
    return values.astype(jnp.float32)


def dot(left, right):
    return lax.dot_general(left, right, (((1,), (0,)), ((), ())), preferred_element_type=jnp.float32)


def dot_rows(left, right):
    return lax.dot_general(left, right, (((1,), (1,)), ((), ())), preferred_element_type=jnp.float32)


def dot_columns(left, right):
    return lax.dot_general(left, right, (((0,), (0,)), ((), ())), preferred_element_type=jnp.float32)


def whole():
    return pl.BlockSpec(memory_space=pltpu.VMEM)


def scalars():
    return pl.BlockSpec(memory_space=pltpu.SMEM)


def row_block(rows, columns):
    return pl.BlockSpec((rows, columns), lambda i: (i, 0))


def fixed_block(rows, columns):
    return pl.BlockSpec((rows, columns), lambda i: (0, 0))


FAR = (0, 8, 16, 24)


def block_device(me, core, place):
    first = jnp.where(core == 0, 4, 2)
    near = (0, first, 6 - first, 6)[place // len(FAR)]
    return me ^ near ^ FAR[place % len(FAR)]


def assemble(me, stacks, targets):
    for stream in range(2):
        for upper in range(2):
            stack = stacks[2 * stream + upper]
            for place in range(8):
                device = block_device(me ^ stream, (me & 1) ^ stream, place + upper * 8)
                here = pl.ds(place * ROWS, ROWS)
                for ref, column, columns, groups in targets:
                    for group in range(groups):
                        start = pl.multiple_of(device * (ROWS * groups) + group * ROWS, ROWS)
                        ref[pl.ds(start, ROWS), :] = stack[here, pl.ds(column + group * columns, columns)]


def arrange(me, sources, keep_ref, send_ref):
    for place in range(16):
        here = pl.ds(place * ROWS, ROWS)
        for stream, out in ((0, keep_ref), (1, send_ref)):
            device = block_device(me ^ stream, (me & 1) ^ stream, place)
            for ref, column, columns, groups in sources:
                for group in range(groups):
                    start = pl.multiple_of(device * (ROWS * groups) + group * ROWS, ROWS)
                    taken = ref[pl.ds(start, ROWS), :]
                    out[here, pl.ds(column + group * columns, columns)] = taken.astype(out.dtype)


def arranged(columns):
    return (
        jax.ShapeDtypeStruct((16 * ROWS, columns), jnp.float32),
        jax.ShapeDtypeStruct((16 * ROWS, columns), jnp.bfloat16),
    )


def centre(values):
    centred = values - jnp.mean(values, axis=-1, keepdims=True)
    scale = lax.rsqrt(jnp.mean(centred * centred, axis=-1, keepdims=True) + norm_epsilon)
    return centred * scale, scale


def norm_back(grad, gain, hat, scale):
    inner = grad * gain
    return scale * (
        inner - jnp.mean(inner, axis=-1, keepdims=True) - hat * jnp.mean(inner * hat, axis=-1, keepdims=True)
    )


def masked_rows(order_row, step):
    seq = order_row.shape[1]
    flags = jnp.where(order_row >= step, 1.0, 0.0)
    column = jnp.transpose(jnp.broadcast_to(flags, (LANES, seq)))
    return jnp.concatenate([column] * (D // LANES), axis=1) > 0.5


def pair_split(pair, scale=None):
    lane = lax.broadcasted_iota(jnp.int32, pair.shape, 1)
    values = wide(pair)
    if scale is not None:
        values = values * scale
    return jnp.concatenate([low(jnp.where(lane < HEAD, values, 0.0)), low(jnp.where(lane < HEAD, 0.0, values))], axis=0)


def key_scores(keys, both_queries, length):
    scores = dot_rows(keys, both_queries)
    seq = scores.shape[0]
    tail = scores[FIRST_PAD:]
    row = lax.broadcasted_iota(jnp.int32, tail.shape, 0) + FIRST_PAD
    return jnp.concatenate([scores[:FIRST_PAD], jnp.where(row < length, tail, masked_score)], axis=0)


def load_input(tokens_ref, order_ref, step, vec_ref):
    masked = masked_rows(order_ref[0], step)
    return masked, jnp.where(masked, vec_ref[4:5, :], wide(tokens_ref[...]))


def attention_kernel(
    me_ref, step_ref, length_ref, order_ref, tokens_ref, own_ref, late_ref, other_ref, other_late_ref,
    p_ref, l_ref, o_ref, weight_ref, vec_ref, columns_ref,
):
    span = pl.program_id(0)

    @pl.when(span == 0)
    def _():
        targets = ((weight_ref, 0, 3 * D, 1), (columns_ref, 3 * D, LANES, 1))
        assemble(me_ref[0], (own_ref, late_ref, other_ref, other_late_ref), targets)
        vec_ref[...] = jnp.transpose(wide(columns_ref[...]))[:8]

    started = load_input(tokens_ref, order_ref, step_ref[span], vec_ref)[1]
    normed = low(centre(started)[0] * vec_ref[0:1, :] + vec_ref[2:3, :])
    p_ref[...] = low(dot(normed, weight_ref[...]))
    seq = started.shape[0]
    for pair in range(D // LANES):
        lanes = pl.ds(pair * LANES, LANES)
        queries = pair_split(p_ref[:, lanes], HEAD**-0.5)
        scores = key_scores(p_ref[:, pl.ds(D + pair * LANES, LANES)], queries, length_ref[span])
        peak = jnp.max(scores, axis=0, keepdims=True)
        exped = jnp.exp(scores - peak)
        total = jnp.sum(exped, axis=0, keepdims=True)
        probability = low(exped / total)
        l_ref[0, pair : pair + 1, :] = peak + jnp.log(total)
        values = jnp.transpose(p_ref[:, pl.ds(2 * D + pair * LANES, LANES)])
        attended = jnp.concatenate(
            [dot(values[:HEAD], probability[:, :seq]), dot(values[HEAD:], probability[:, seq:])], axis=0
        )
        o_ref[:, lanes] = jnp.transpose(low(attended))


def span_specs(seq):
    return [pl.BlockSpec((1, 1, seq), lambda i: (i, 0, 0)), row_block(seq, D)]


def pair_block(seq):
    return pl.BlockSpec((1, D // LANES, 2 * seq), lambda i: (i, 0, 0))


def attention(me, steps, lengths, order, tokens, stacks):
    spans, seq = order.shape[0], order.shape[2]
    return pl.pallas_call(
        attention_kernel,
        grid=(spans,),
        out_shape=(
            jax.ShapeDtypeStruct((spans * seq, 3 * D), jnp.bfloat16),
            jax.ShapeDtypeStruct((spans, D // LANES, 2 * seq), jnp.float32),
            jax.ShapeDtypeStruct((spans * seq, D), jnp.bfloat16),
            jax.ShapeDtypeStruct((D, 3 * D), jnp.bfloat16),
            jax.ShapeDtypeStruct((8, D), jnp.float32),
        ),
        in_specs=[scalars()] * 3 + span_specs(seq) + [whole()] * 4,
        out_specs=(
            row_block(seq, 3 * D),
            pair_block(seq),
            row_block(seq, D),
            fixed_block(D, 3 * D),
            fixed_block(8, D),
        ),
        scratch_shapes=[pltpu.VMEM((D, LANES), jnp.bfloat16)],
        compiler_params=pltpu.CompilerParams(vmem_limit_bytes=VMEM_BYTES),
        name="attention",
    )(me, steps, lengths, order, tokens, *stacks)


def add_into(ref, index, value, start):
    @pl.when(start)
    def _():
        ref[index] = value

    @pl.when(jnp.logical_not(start))
    def _():
        ref[index] += value


def hidden_half(normed, upstream, up_ref, down_ref, grad_up_ref, grad_down_ref, start):
    width = HALF_FF // PARTS
    branch = 0.0
    grad_normed = 0.0
    for part in range(PARTS):
        units = pl.ds(part * width, width)
        hidden = dot(normed, up_ref[:, units])
        grad_act = dot_rows(upstream, down_ref[units, :])
        squared = hidden * hidden
        tilt = jnp.tanh(hidden * (gelu_scale + (gelu_scale * gelu_cubic) * squared))
        gate = 0.5 + 0.5 * tilt
        active = hidden * gate
        slope = gate + active * (1.0 - tilt) * (gelu_scale + (3.0 * gelu_scale * gelu_cubic) * squared)
        active = low(active)
        grad_hidden = low(grad_act * slope)
        branch = branch + dot(active, down_ref[units, :])
        grad_normed = grad_normed + dot_rows(grad_hidden, up_ref[:, units])
        add_into(grad_up_ref, (slice(None), units), dot_columns(normed, grad_hidden), start)
        add_into(grad_down_ref, (units, slice(None)), dot_columns(active, upstream), start)
    return branch, grad_normed


def first_half_kernel(
    me_ref, step_ref, order_ref, tokens_ref, cot_ref, vec_ref, o_ref, own_ref, late_ref, other_ref, other_late_ref,
    middle_ref, normed_ref, branch_ref, back_ref, out_ref, keep_ref, send_ref,
    up_ref, down_ref, grad_up_ref, grad_down_ref,
):
    span = pl.program_id(0)

    @pl.when(span == 0)
    def _():
        targets = ((up_ref, 0, HALF_FF, 1), (down_ref, HALF_FF, D, 2), (out_ref, 2 * HALF_FF, D, 1))
        assemble(me_ref[0], (own_ref, late_ref, other_ref, other_late_ref), targets)

    started = load_input(tokens_ref, order_ref, step_ref[span], vec_ref)[1]
    middle = started + dot(o_ref[...], out_ref[...])
    middle_ref[...] = middle
    normed = low(centre(middle)[0] * vec_ref[1:2, :] + vec_ref[3:4, :])
    normed_ref[...] = normed
    branch, back = hidden_half(normed, cot_ref[...], up_ref, down_ref, grad_up_ref, grad_down_ref, span == 0)
    branch_ref[...] = middle + branch
    back_ref[...] = back

    @pl.when(span == pl.num_programs(0) - 1)
    def _():
        sources = ((grad_up_ref, 0, HALF_FF, 1), (grad_down_ref, HALF_FF, D, 2))
        arrange(me_ref[0], sources, keep_ref, send_ref)


def half_scratch():
    return [
        pltpu.VMEM((D, HALF_FF), jnp.bfloat16),
        pltpu.VMEM((HALF_FF, D), jnp.bfloat16),
        pltpu.VMEM((D, HALF_FF), jnp.float32),
        pltpu.VMEM((HALF_FF, D), jnp.float32),
    ]


def first_half(me, steps, order, tokens, cotangent, vec, attended, stacks):
    spans, seq = order.shape[0], order.shape[2]
    tall = jax.ShapeDtypeStruct((spans * seq, D), jnp.float32)
    keep, send = arranged(2 * HALF_FF)
    return pl.pallas_call(
        first_half_kernel,
        grid=(spans,),
        out_shape=(
            tall,
            jax.ShapeDtypeStruct((spans * seq, D), jnp.bfloat16),
            tall,
            tall,
            jax.ShapeDtypeStruct((D, D), jnp.bfloat16),
            keep,
            send,
        ),
        in_specs=[scalars()] * 2
        + span_specs(seq)
        + [row_block(seq, D), fixed_block(8, D), row_block(seq, D)]
        + [whole()] * 4,
        out_specs=(
            row_block(seq, D),
            row_block(seq, D),
            row_block(seq, D),
            row_block(seq, D),
            fixed_block(D, D),
            fixed_block(*keep.shape),
            fixed_block(*send.shape),
        ),
        scratch_shapes=half_scratch(),
        compiler_params=pltpu.CompilerParams(vmem_limit_bytes=VMEM_BYTES),
        name="first_half",
    )(me, steps, order, tokens, cotangent, vec, attended, *stacks)


def second_half_kernel(
    me_ref, cot_ref, vec_ref, o_ref, middle_ref, normed_ref, branch_ref, back_ref, out_ref,
    own_ref, late_ref, other_ref, other_late_ref,
    result_ref, dmiddle_ref, dattended_ref, dvec_ref, keep_ref, send_ref,
    up_ref, down_ref, grad_up_ref, grad_down_ref, grad_out_ref,
):
    span = pl.program_id(0)
    start = span == 0

    @pl.when(start)
    def _():
        targets = ((up_ref, 0, HALF_FF, 1), (down_ref, HALF_FF, D, 2))
        assemble(me_ref[0], (own_ref, late_ref, other_ref, other_late_ref), targets)
        dvec_ref[...] = jnp.zeros_like(dvec_ref)

    upstream = cot_ref[...]
    branch, back = hidden_half(normed_ref[...], upstream, up_ref, down_ref, grad_up_ref, grad_down_ref, start)
    result_ref[...] = low(branch_ref[...] + branch)
    back = back_ref[...] + back
    hat, scale = centre(middle_ref[...])
    dmiddle = wide(upstream) + norm_back(back, vec_ref[1:2, :], hat, scale)
    dmiddle_ref[...] = dmiddle
    dvec_ref[1:2, :] += jnp.sum(back * hat, axis=0, keepdims=True)
    dvec_ref[3:4, :] += jnp.sum(back, axis=0, keepdims=True)
    mixed = low(dmiddle)
    dattended_ref[...] = low(dot_rows(mixed, out_ref[...]))
    add_into(grad_out_ref, Ellipsis, dot_columns(o_ref[...], mixed), start)

    @pl.when(span == pl.num_programs(0) - 1)
    def _():
        sources = ((grad_up_ref, 0, HALF_FF, 1), (grad_down_ref, HALF_FF, D, 2), (grad_out_ref, 2 * HALF_FF, D, 1))
        arrange(me_ref[0], sources, keep_ref, send_ref)


def second_half(me, cotangent, vec, attended, middle, normed, branch, back, out_full, stacks, seq):
    total = middle.shape[0]
    keep, send = arranged(2 * HALF_FF + D)
    rows = row_block(seq, D)
    return pl.pallas_call(
        second_half_kernel,
        grid=(total // seq,),
        out_shape=(
            jax.ShapeDtypeStruct((total, D), jnp.bfloat16),
            jax.ShapeDtypeStruct((total, D), jnp.float32),
            jax.ShapeDtypeStruct((total, D), jnp.bfloat16),
            jax.ShapeDtypeStruct((8, D), jnp.float32),
            keep,
            send,
        ),
        in_specs=[scalars(), rows, fixed_block(8, D), rows, rows, rows, rows, rows, fixed_block(D, D)] + [whole()] * 4,
        out_specs=(rows, rows, rows, fixed_block(8, D), fixed_block(*keep.shape), fixed_block(*send.shape)),
        scratch_shapes=half_scratch() + [pltpu.VMEM((D, D), jnp.float32)],
        compiler_params=pltpu.CompilerParams(vmem_limit_bytes=VMEM_BYTES),
        name="second_half",
    )(me, cotangent, vec, attended, middle, normed, branch, back, out_full, *stacks)


def attention_back_kernel(
    me_ref, step_ref, length_ref, order_ref, tokens_ref, vec_ref, p_ref, l_ref, dattended_ref, dmiddle_ref, weight_ref,
    dvec_in_ref, grad_ref, keep_ref, send_ref, dp_ref, grad_qkv_ref, dvec_ref, columns_ref,
):
    span = pl.program_id(0)
    start = span == 0

    @pl.when(start)
    def _():
        dvec_ref[...] = jnp.zeros_like(dvec_ref)
        dvec_ref[:8, :] = dvec_in_ref[...]

    seq = p_ref.shape[0]
    for pair in range(D // LANES):
        lanes = pl.ds(pair * LANES, LANES)
        key_lanes = pl.ds(D + pair * LANES, LANES)
        value_lanes = pl.ds(2 * D + pair * LANES, LANES)
        queries = pair_split(p_ref[:, lanes], HEAD**-0.5)
        dattended = pair_split(dattended_ref[:, lanes])
        keys = p_ref[:, key_lanes]
        scores = key_scores(keys, queries, length_ref[span])
        probability = jnp.exp(scores - l_ref[0, pair : pair + 1, :])
        dprobability = dot_rows(p_ref[:, value_lanes], dattended)
        inner = jnp.sum(probability * dprobability, axis=0, keepdims=True)
        dscores = low(probability * (dprobability - inner))
        dp_ref[:, value_lanes] = low(dot(low(probability), dattended))
        dp_ref[:, key_lanes] = low(dot(dscores, queries))
        keys = jnp.transpose(low(wide(keys) * HEAD**-0.5))
        dqueries = jnp.concatenate([dot(keys[:HEAD], dscores[:, :seq]), dot(keys[HEAD:], dscores[:, seq:])], axis=0)
        dp_ref[:, lanes] = jnp.transpose(low(dqueries))

    masked, started = load_input(tokens_ref, order_ref, step_ref[span], vec_ref)
    hat, scale = centre(started)
    normed = low(hat * vec_ref[0:1, :] + vec_ref[2:3, :])
    add_into(grad_qkv_ref, Ellipsis, dot_columns(normed, dp_ref[...]), start)
    back = dot_rows(dp_ref[...], weight_ref[...])
    dstarted = dmiddle_ref[...] + norm_back(back, vec_ref[0:1, :], hat, scale)
    dvec_ref[0:1, :] += jnp.sum(back * hat, axis=0, keepdims=True)
    dvec_ref[2:3, :] += jnp.sum(back, axis=0, keepdims=True)
    dvec_ref[4:5, :] += jnp.sum(jnp.where(masked, dstarted, 0.0), axis=0, keepdims=True)
    grad_ref[...] = jnp.where(masked, 0.0, dstarted)

    @pl.when(span == pl.num_programs(0) - 1)
    def _():
        columns_ref[...] = jnp.transpose(dvec_ref[...])
        arrange(me_ref[0], ((grad_qkv_ref, 0, 3 * D, 1), (columns_ref, 3 * D, LANES, 1)), keep_ref, send_ref)


def attention_back(me, steps, lengths, order, tokens, vec, projected, logs, dattended, dmiddle, weight, dvec):
    spans, seq = order.shape[0], order.shape[2]
    keep, send = arranged(3 * D + LANES)
    return pl.pallas_call(
        attention_back_kernel,
        grid=(spans,),
        out_shape=(jax.ShapeDtypeStruct((spans * seq, D), jnp.float32), keep, send),
        in_specs=[scalars()] * 3
        + span_specs(seq)
        + [
            fixed_block(8, D),
            row_block(seq, 3 * D),
            pair_block(seq),
            row_block(seq, D),
            row_block(seq, D),
            fixed_block(D, 3 * D),
            fixed_block(8, D),
        ],
        out_specs=(row_block(seq, D), fixed_block(*keep.shape), fixed_block(*send.shape)),
        scratch_shapes=[
            pltpu.VMEM((seq, 3 * D), jnp.bfloat16),
            pltpu.VMEM((D, 3 * D), jnp.float32),
            pltpu.VMEM((LANES, D), jnp.float32),
            pltpu.VMEM((D, LANES), jnp.float32),
        ],
        compiler_params=pltpu.CompilerParams(vmem_limit_bytes=VMEM_BYTES),
        name="attention_back",
    )(me, steps, lengths, order, tokens, vec, projected, logs, dattended, dmiddle, weight, dvec)


def exchange(values, count, even_mask, odd_mask):
    pairs = [(i, i ^ (odd_mask if i % 2 else even_mask)) for i in range(count)]
    return lax.ppermute(values, AXES, pairs)


def gather_stacks(shard, count):
    stack = [shard] + [exchange(shard, count, offset, offset) for offset in FAR[1:]]
    stack = jnp.concatenate(stack, axis=0)
    stack = jnp.concatenate([stack, exchange(stack, count, 4, 2)], axis=0)
    late = exchange(stack, count, 2, 4)
    return (stack, late, exchange(stack, count, 1, 1), exchange(late, count, 1, 1))


def scatter_stack(keep, send, count):
    total = keep + wide(exchange(send, count, 1, 1))
    half = 8 * ROWS
    total = total[:half] + wide(exchange(low(total[half:]), count, 2, 4))
    half = half // 2
    total = total[:half] + wide(exchange(low(total[half:]), count, 4, 2))
    own = total[:ROWS]
    for place in range(1, len(FAR)):
        part = low(total[place * ROWS : (place + 1) * ROWS])
        own = own + wide(exchange(part, count, FAR[place], FAR[place]))
    return own


def split_units(up, down):
    rows, units = up.shape
    up_halves = up.reshape(rows, units // 64, 2, 32)
    down_halves = down.reshape(rows // ROWS, 2, 2, ROWS, D)
    pieces = []
    for half in range(2):
        up_part = up_halves[:, :, half].reshape(rows, units // 2)
        down_part = jnp.swapaxes(down_halves[:, half], 1, 2).reshape(rows, 2 * D)
        pieces.append(jnp.concatenate([up_part, down_part], axis=1))
    return pieces


def join_units(pieces):
    rows = pieces[0].shape[0]
    up = jnp.stack([piece[:, :HALF_FF].reshape(rows, HALF_FF // 32, 32) for piece in pieces], axis=2)
    down = [jnp.swapaxes(piece[:, HALF_FF:].reshape(rows // ROWS, ROWS, 2, D), 1, 2) for piece in pieces]
    down = jnp.stack(down, axis=1).reshape(rows * 4, D)
    return up.reshape(rows, 2 * HALF_FF), down


def stack_order(core):
    near = (0, 4, 2, 6) if core == 0 else (0, 2, 4, 6)
    return [core ^ group ^ offset for group in near for offset in FAR]


def gather_piece(piece, count):
    if piece.shape[0] == ROWS:
        return gather_stacks(piece, count)
    blocks = piece.reshape(32, ROWS, piece.shape[1])
    stacks = []
    for core in range(2):
        ordered = jnp.stack([blocks[device] for device in stack_order(core)])
        ordered = ordered.reshape(16 * ROWS, piece.shape[1])
        stacks += [ordered[: 8 * ROWS], ordered[8 * ROWS :]]
    return tuple(stacks)


def full_piece(keep, send):
    columns = keep.shape[1]
    blocks = jnp.concatenate([keep, wide(send)], axis=0).reshape(32, ROWS, columns)
    order = stack_order(0) + stack_order(1)
    return jnp.stack([blocks[order.index(device)] for device in range(32)]).reshape(32 * ROWS, columns)


def adam_update(master, gradient, moment, square, step_rate, decay_rate):
    moment_new = beta_first * moment + (1.0 - beta_first) * gradient
    square_new = beta_second * square + (1.0 - beta_second) * gradient * gradient
    corrected = (
        moment_new
        / (1.0 - beta_first**STEP)
        / (jnp.sqrt(square_new / (1.0 - beta_second**STEP)) + adam_epsilon)
    )
    return (moment_new, square_new, master - step_rate * (corrected + decay_rate * master))


def local(
    tokens,
    cotangent,
    reveal_order,
    reveal_step,
    lengths,
    weight_qkv,
    weight_out,
    weight_up,
    weight_down,
    vectors,
    moment_qkv,
    square_qkv,
    moment_out,
    square_out,
    moment_up,
    square_up,
    moment_down,
    square_down,
    moment_vec,
    square_vec,
):
    count = lax.axis_size("dp") * lax.axis_size("fsdp")
    direct = weight_qkv.shape[0] == ROWS and count == 32
    me = lax.axis_index("dp") * lax.axis_size("fsdp") + lax.axis_index("fsdp")
    me = (me if direct else 0 * me).astype(jnp.int32)[None]
    spans, seq = reveal_order.shape
    order = reveal_order.reshape(spans, 1, seq)
    flat = tokens.reshape(spans * seq, D)
    upstream = cotangent.reshape(spans * seq, D)

    halves = [low(weight_qkv), low(weight_out), low(weight_up), low(weight_down), low(vectors).T]
    if not direct:
        halves = [lax.all_gather(half, AXES, axis=0, tiled=True) for half in halves]
    qkv, out, up, down, columns = halves
    columns = jnp.pad(columns, ((0, 0), (0, LANES - columns.shape[1])))
    hidden = split_units(up, down)
    first = gather_piece(jnp.concatenate([qkv, columns], axis=1), count)
    second = gather_piece(jnp.concatenate([hidden[0], out], axis=1), count)
    third = gather_piece(hidden[1], count)

    projected, logs, attended, weight, vec = attention(me, reveal_step, lengths, order, flat, first)
    middle, normed, branch, back, out_full, keep_one, send_one = first_half(
        me, reveal_step, order, flat, upstream, vec, attended, second
    )
    result, dmiddle, dattended, dvec, keep_two, send_two = second_half(
        me, upstream, vec, attended, middle, normed, branch, back, out_full, third, seq
    )
    input_grad, keep_three, send_three = attention_back(
        me, reveal_step, lengths, order, flat, vec, projected, logs, dattended, dmiddle, weight, dvec
    )

    stacks = [(keep_one, send_one), (keep_two, send_two), (keep_three, send_three)]
    if direct:
        sums = [scatter_stack(keep, send, count) for keep, send in stacks]
    else:
        sums = [full_piece(keep, send) for keep, send in stacks]
    grad_up, grad_down = join_units([sums[0], sums[1][:, : 2 * HALF_FF]])
    grads = (
        sums[2][:, : 3 * D],
        sums[1][:, 2 * HALF_FF :],
        grad_up,
        grad_down,
        sums[2][:, 3 * D : 3 * D + vectors.shape[0]],
    )
    if not direct:
        grads = [lax.psum_scatter(grad, AXES, scatter_dimension=0, tiled=True) for grad in grads]
    m_qkv, s_qkv, w_qkv = adam_update(weight_qkv, grads[0], moment_qkv, square_qkv, matrix_rate, weight_decay)
    m_out, s_out, w_out = adam_update(weight_out, grads[1], moment_out, square_out, output_rate, weight_decay)
    m_up, s_up, w_up = adam_update(weight_up, grads[2], moment_up, square_up, matrix_rate, weight_decay)
    m_down, s_down, w_down = adam_update(weight_down, grads[3], moment_down, square_down, matrix_rate, weight_decay)
    m_vec, s_vec, w_vec = adam_update(vectors, grads[4].T, moment_vec, square_vec, vector_rate, 0.0)
    return (
        result.reshape(tokens.shape),
        input_grad.reshape(tokens.shape),
        m_qkv,
        s_qkv,
        w_qkv,
        m_out,
        s_out,
        w_out,
        m_up,
        s_up,
        w_up,
        m_down,
        s_down,
        w_down,
        m_vec,
        s_vec,
        w_vec,
    )


def solution(mesh):
    return jax.shard_map(
        local,
        mesh=mesh,
        in_specs=(
            P(("dp", "fsdp"), None, None),
            P(("dp", "fsdp"), None, None),
            P(("dp", "fsdp"), None),
            P(("dp", "fsdp")),
            P(("dp", "fsdp")),
            P(("dp", "fsdp"), None),
            P(("dp", "fsdp"), None),
            P(("dp", "fsdp"), None),
            P(("dp", "fsdp"), None),
            P(None, ("dp", "fsdp")),
            P(("dp", "fsdp"), None),
            P(("dp", "fsdp"), None),
            P(("dp", "fsdp"), None),
            P(("dp", "fsdp"), None),
            P(("dp", "fsdp"), None),
            P(("dp", "fsdp"), None),
            P(("dp", "fsdp"), None),
            P(("dp", "fsdp"), None),
            P(None, ("dp", "fsdp")),
            P(None, ("dp", "fsdp")),
        ),
        out_specs=(
            P(("dp", "fsdp"), None, None),
            P(("dp", "fsdp"), None, None),
            P(("dp", "fsdp"), None),
            P(("dp", "fsdp"), None),
            P(("dp", "fsdp"), None),
            P(("dp", "fsdp"), None),
            P(("dp", "fsdp"), None),
            P(("dp", "fsdp"), None),
            P(("dp", "fsdp"), None),
            P(("dp", "fsdp"), None),
            P(("dp", "fsdp"), None),
            P(("dp", "fsdp"), None),
            P(("dp", "fsdp"), None),
            P(("dp", "fsdp"), None),
            P(None, ("dp", "fsdp")),
            P(None, ("dp", "fsdp")),
            P(None, ("dp", "fsdp")),
        ),
        check_vma=False,
    )
```

time: 916 us -> 203 us (0.22)
  waiting for transfers between devices: 678 us -> 54.2 us
  matrix products: 81.9 us -> 0 us
  blocking collectives: 81.7 us -> 0 us
  Pallas kernels: 0 us -> 70 us
  starting transfers between devices: 0.72 us -> 46.9 us
  other arithmetic: 30.7 us -> 15.3 us
  between operations: 15.2 us -> 1.33 us
    reduce_scatter x4 -> x0, waiting for transfers between devices: 514 us -> none  [the longest x1 141 us: local(): lax.psum_scatter(grad_up, ('dp', 'fsdp'), scatter_dimension=0, tiled=True)]
    unnamed x9 -> x0, waiting for transfers between devices: 108 us -> none
    dot_general x36 -> x0, matrix products: 81.9 us -> none  [the longest x2 9.85 us: backward_pass(): jnp.einsum('csd,fd->csf', down_grad, down_full, preferred_element_type=jn...]
    all_gather x2 -> x0, blocking collectives: 81.7 us -> none  [the longest x1 43.5 us: local(): lax.all_gather(vec_half, ('dp', 'fsdp'), axis=1, tiled=True)]
    pallas_call x0 -> x4, Pallas kernels: none -> 70 us  [the longest x1 21.2 us: second_half(): pl.pallas_call(second_half_kernel, grid=(total // seq,), out_shape=(jax.S...]
    all_gather x3 -> x0, waiting for transfers between devices: 56.8 us -> none  [the longest x1 53.5 us: local(): lax.all_gather(down_half, ('dp', 'fsdp'), axis=0, tiled=True)]
    ppermute x0 -> x39, waiting for transfers between devices: none -> 54.2 us  [exchange(): return lax.ppermute(values, AXES, pairs)]
    ppermute x0 -> x39, starting transfers between devices: none -> 46.9 us  [exchange(): return lax.ppermute(values, AXES, pairs)]
  transfers between devices with their start and end apart: 8 -> 39, of which waited for: 7 -> 16; matrix products, arithmetic and copies ran while one was open for 7% -> 9% of each run, Pallas kernels for 0% -> 15%
where the time goes in v2:
time: 203 us; the launch traced here: 202 us
  Pallas kernels  70 us (34%)
  waiting for transfers between devices  54.2 us (27%)
  starting transfers between devices  46.9 us (23%)
  other arithmetic  15.3 us (8%)
  local copies, waits for them, and re-layouts  14.7 us (7%)
    ppermute x39, waiting for transfers between devices, exchange(): return lax.ppermute(values, AXES, pairs)  54.2 us
    ppermute x39, starting transfers between devices, exchange(): return lax.ppermute(values, AXES, pairs)  46.9 us
    pallas_call x1, Pallas kernels, second_half(): pl.pallas_call(second_half_kernel, grid=(total // seq,), out_shape=(jax.S...  21.2 us
    pallas_call x1, Pallas kernels, first_half(): pl.pallas_call(first_half_kernel, grid=(spans,), out_shape=(tall, jax.Sha...  18.8 us
    pallas_call x1, Pallas kernels, attention_back(): pl.pallas_call(attention_back_kernel, grid=(spans,), out_shape=(jax.Shape...  18.7 us
    pallas_call x1, Pallas kernels, attention(): pl.pallas_call(attention_kernel, grid=(spans,), out_shape=(jax.ShapeDtype...  11.3 us
    unnamed x80, local copies, waits for them, and re-layouts  9.27 us
  transfers between devices with their start and end apart: 39, of which 16 were waited for; matrix products, arithmetic and copies ran while one was open for 9% of the time, Pallas kernels for 15%

profile of v2, /device:TPU:0, one launch (start us, length us, event | category | flops | bytes accessed | tf_op | source)
XLA Modules:
  0.0 202.4 jit_solution(9256295004470897242)
XLA Ops:
  3.0 3.0 %collective-permute-start = (bf16[16,1664]{1,0:T(8,128)(2,1)S(1)}, bf16[16,1664]{1,0:T(8,128)(2,1)S(1)}, u32[]{:S(2)}, u32[]{:S(2)}) collective-permute-start(bf16[16,1664]{1,0:T(8,128)(2,1)S(1)} %get-tuple-element.133), channel_id=1, source_target_pairs={{0,8},{1,9},{2,10},{3,11},{4,12},{5,13},{6,14},{7,15},{8,0},{9,1},... | collective-permute-start | bytes 159752 | tf_op jit(solution)/shard_map/ppermute | solution.py:460
  6.0 2.6 %collective-permute-start.1 = (bf16[16,1664]{1,0:T(8,128)(2,1)S(1)}, bf16[16,1664]{1,0:T(8,128)(2,1)S(1)}, u32[]{:S(2)}, u32[]{:S(2)}) collective-permute-start(bf16[16,1664]{1,0:T(8,128)(2,1)S(1)} %get-tuple-element.133), channel_id=1, source_target_pairs={{0,16},{1,17},{2,18},{3,19},{4,20},{5,21},{6,22},{7,23},{8,24},{9,... | collective-permute-start | bytes 159752 | tf_op jit(solution)/shard_map/ppermute | solution.py:460
  13.4 3.5 %collective-permute-start.8 = (bf16[16,2560]{1,0:T(8,128)(2,1)S(1)}, bf16[16,2560]{1,0:T(8,128)(2,1)S(1)}, u32[]{:S(2)}, u32[]{:S(2)}) collective-permute-start(bf16[16,2560]{1,0:T(8,128)(2,1)S(1)} %get-tuple-element.129), channel_id=1, source_target_pairs={{0,16},{1,17},{2,18},{3,19},{4,20},{5,21},{6,22},{7,23},{8,24},{9,... | collective-permute-start | bytes 245768 | tf_op jit(solution)/shard_map/ppermute | solution.py:460
  19.1 3.9 %collective-permute-start.16 = (bf16[16,2048]{1,0:T(8,128)(2,1)S(1)}, bf16[16,2048]{1,0:T(8,128)(2,1)S(1)}, u32[]{:S(2)}, u32[]{:S(2)}) collective-permute-start(bf16[16,2048]{1,0:T(8,128)(2,1)S(1)} %get-tuple-element.135), channel_id=1, source_target_pairs={{0,24},{1,25},{2,26},{3,27},{4,28},{5,29},{6,30},{7,31},{8,16},{9,... | collective-permute-start | bytes 196616 | tf_op jit(solution)/shard_map/ppermute | solution.py:460
  27.6 2.2 %collective-permute-done.9 = bf16[16,2560]{1,0:T(8,128)(2,1)S(1)} collective-permute-done((bf16[16,2560]{1,0:T(8,128)(2,1)S(1)}, bf16[16,2560]{1,0:T(8,128)(2,1)S(1)}, u32[]{:S(2)}, u32[]{:S(2)}) %collective-permute-start.9) | collective-permute-done | bytes 81952 | tf_op jit(solution)/shard_map/ppermute | solution.py:460
  31.5 8.4 %collective-permute-done.10 = bf16[64,2560]{1,0:T(8,128)(2,1)S(1)} collective-permute-done((bf16[64,2560]{1,0:T(8,128)(2,1)S(1)}, bf16[64,2560]{1,0:T(8,128)(2,1)S(1)}, u32[]{:S(2)}, u32[]{:S(2)}) %collective-permute-start.10) | collective-permute-done | bytes 327712 | tf_op jit(solution)/shard_map/ppermute | solution.py:460
  44.8 5.7 %collective-permute-done.11.late_ref = bf16[128,2560]{1,0:T(8,128)(2,1)S(1)} collective-permute-done((bf16[128,2560]{1,0:T(8,128)(2,1)S(1)}, bf16[128,2560]{1,0:T(8,128)(2,1)S(1)}, u32[]{:S(2)}, u32[]{:S(2)}) %collective-permute-start.11) | collective-permute-done | bytes 655392 | tf_op jit(solution)/shard_map/ppermute | solution.py:460
  50.5 10.3 %collective-permute-done.4.late_ref = bf16[128,1664]{1,0:T(8,128)(2,1)} collective-permute-done((bf16[128,1664]{1,0:T(8,128)(2,1)}, bf16[128,1664]{1,0:T(8,128)(2,1)}, u32[]{:S(2)}, u32[]{:S(2)}) %collective-permute-start.4) | collective-permute-done | bytes 426016 | tf_op jit(solution)/shard_map/ppermute | solution.py:460
  62.1 2.3 %collective-permute-done.6.other_late_ref = bf16[128,1664]{1,0:T(8,128)(2,1)} collective-permute-done((bf16[128,1664]{1,0:T(8,128)(2,1)}, bf16[128,1664]{1,0:T(8,128)(2,1)}, u32[]{:S(2)}, u32[]{:S(2)}) %collective-permute-start.6) | collective-permute-done | bytes 426016 | tf_op jit(solution)/shard_map/ppermute | solution.py:460
  65.4 11.3 %attention.1 = (bf16[1024,1536]{1,0:T(8,128)(2,1)}, f32[4,4,512]{2,1,0:T(4,128)S(1)}, bf16[1024,512]{1,0:T(8,128)(2,1)S(1)}, bf16[512,1536]{1,0:T(8,128)(2,1)S(1)}, f32[8,512]{1,0:T(8,128)S(1)}) custom-call(s32[1]{0:T(128)} %bitcast.me_ref, s32[4]{0:T(128)S(1)} %copy-done.8, s32[4]{0:T(128)S(1)} %copy-done.9, s32[4,1,256]{2,1,0:T(1,128)S(1)} %reshape.74.order_ref, ...), custom_call_target="tpu_custom_call" | custom-call | tf_op jit(solution)/shard_map/attention/pallas_call | solution.py:196
  77.7 18.8 %first_half.1 = (f32[1024,512]{1,0:T(8,128)}, bf16[1024,512]{1,0:T(8,128)(2,1)S(1)}, f32[1024,512]{1,0:T(8,128)}, f32[1024,512]{1,0:T(8,128)}, bf16[512,512]{1,0...) custom-call(s32[1]{0:T(128)} %bitcast.me_ref, s32[4]{0:T(128)S(1)} %copy-done.8, ...), custom_call_target="tpu_custom_call" | custom-call | tf_op jit(solution)/shard_map/first_half/pallas_call | solution.py:292
  97.5 21.2 %second_half.1 = (bf16[1024,512]{1,0:T(8,128)(2,1)}, f32[1024,512]{1,0:T(8,128)}, bf16[1024,512]{1,0:T(8,128)(2,1)S(1)}, f32[8,512]{1,0:T(8,128)S(1)}, f32[256,2560]{1,0:T(8,128)}, /*index=5*/bf16[256,2560]{1,0:T(8,128)(2,1)}) custom-call(s32[1]{0:T(128)} %bitcast.me_ref, bf16[1024,512]{1,0:T(8,128)(2,1)S(1)} %bitcast.44, ...), custom_call_target="tpu_custom_call" | custom-call | tf_op jit(solution)/shard_map/second_half/pallas_call | solution.py:361
  118.8 18.7 %attention_back.1 = (f32[1024,512]{1,0:T(8,128)}, f32[256,1664]{1,0:T(8,128)}, bf16[256,1664]{1,0:T(8,128)(2,1)S(1)}) custom-call(s32[1]{0:T(128)} %bitcast.me_ref, s32[4]{0:T(128)S(1)} %copy-done.8, s32[4]{0:T(128)S(1)} %copy-done.9, s32[4,1,256]{2,1,0:T(1,128)S(1)} %reshape.74.order_ref, bf16[1024,512]{1,0:T(8,128)(2,1)S(1)} %bitcast.42, ...), custom_call_target="tpu_custom_call" | custom-call | tf_op jit(solution)/shard_map/attention_back/pallas_call | solution.py:431
  138.0 1.9 collective-permute-done.21
  144.6 6.3 %collective-permute-done.22 = bf16[128,1664]{1,0:T(8,128)(2,1)S(1)} collective-permute-done((bf16[128,1664]{1,0:T(8,128)(2,1)S(1)}, bf16[128,1664]{1,0:T(8,128)(2,1)S(1)}, u32[]{:S(2)}, u32[]{:S(2)}) %collective-permute-start.22) | collective-permute-done | bytes 426016 | tf_op jit(solution)/shard_map/ppermute | solution.py:460
  159.5 3.1 %collective-permute-start.26 = (bf16[16,1664]{1,0:T(8,128)(2,1)S(1)}, bf16[16,1664]{1,0:T(8,128)(2,1)S(1)}, u32[]{:S(2)}, u32[]{:S(2)}) collective-permute-start(bf16[16,1664]{1,0:T(8,128)(2,1)S(1)} %get-tuple-element.123), channel_id=1, source_target_pairs={{0,24},{1,25},{2,26},{3,27},{4,28},{5,29},{6,30},{7,31},{8,16},{9,... | collective-permute-start | bytes 159752 | tf_op jit(solution)/shard_map/ppermute | solution.py:460
  163.1 2.3 %collective-permute-start.28 = (bf16[128,2560]{1,0:T(8,128)(2,1)S(1)}, bf16[128,2560]{1,0:T(8,128)(2,1)}, u32[]{:S(2)}, u32[]{:S(2)}) collective-permute-start(bf16[128,2560]{1,0:T(8,128)(2,1)S(1)} %slice.231), channel_id=1, source_target_pairs={{0,2},{1,5},{2,0},{3,7},{4,6},{5,1},{6,4},{7,3},{8,10},{9,13},{10,... | collective-permute-start | bytes 1966088 | tf_op jit(solution)/shard_map/ppermute | solution.py:460
  171.4 4.1 %collective-permute-done.35 = bf16[64,2048]{1,0:T(8,128)(2,1)S(1)} collective-permute-done((bf16[64,2048]{1,0:T(8,128)(2,1)S(1)}, bf16[64,2048]{1,0:T(8,128)(2,1)S(1)}, u32[]{:S(2)}, u32[]{:S(2)}) %collective-permute-start.35) | collective-permute-done | bytes 262176 | tf_op jit(solution)/shard_map/ppermute | solution.py:460
  175.7 3.7 %collective-permute-start.37 = (bf16[16,2048]{1,0:T(8,128)(2,1)S(1)}, bf16[16,2048]{1,0:T(8,128)(2,1)S(1)}, u32[]{:S(2)}, u32[]{:S(2)}) collective-permute-start(bf16[16,2048]{1,0:T(8,128)(2,1)S(1)} %get-tuple-element.121), channel_id=1, source_target_pairs={{0,16},{1,17},{2,18},{3,19},{4,20},{5,21},{6,22},{7,23},{8,24},{9,... | collective-permute-start | bytes 196616 | tf_op jit(solution)/shard_map/ppermute | solution.py:460
  183.4 2.0 %collective-permute-done.38 = bf16[16,2048]{1,0:T(8,128)(2,1)S(1)} collective-permute-done((bf16[16,2048]{1,0:T(8,128)(2,1)S(1)}, bf16[16,2048]{1,0:T(8,128)(2,1)S(1)}, u32[]{:S(2)}, u32[]{:S(2)}) %collective-permute-start.38) | collective-permute-done | bytes 65568 | tf_op jit(solution)/shard_map/ppermute | solution.py:460
  185.4 3.0 %collective-permute-done.29 = bf16[64,2560]{1,0:T(8,128)(2,1)S(1)} collective-permute-done((bf16[64,2560]{1,0:T(8,128)(2,1)S(1)}, bf16[64,2560]{1,0:T(8,128)(2,1)S(1)}, u32[]{:S(2)}, u32[]{:S(2)}) %collective-permute-start.29) | collective-permute-done | bytes 327712 | tf_op jit(solution)/shard_map/ppermute | solution.py:460
  188.6 3.7 %collective-permute-start.31 = (bf16[16,2560]{1,0:T(8,128)(2,1)S(1)}, bf16[16,2560]{1,0:T(8,128)(2,1)S(1)}, u32[]{:S(2)}, u32[]{:S(2)}) collective-permute-start(bf16[16,2560]{1,0:T(8,128)(2,1)S(1)} %get-tuple-element.118), channel_id=1, source_target_pairs={{0,16},{1,17},{2,18},{3,19},{4,20},{5,21},{6,22},{7,23},{8,24},{9,... | collective-permute-start | bytes 245768 | tf_op jit(solution)/shard_map/ppermute | solution.py:460
  193.2 3.0 %collective-permute-done.31 = bf16[16,2560]{1,0:T(8,128)(2,1)S(1)} collective-permute-done((bf16[16,2560]{1,0:T(8,128)(2,1)S(1)}, bf16[16,2560]{1,0:T(8,128)(2,1)S(1)}, u32[]{:S(2)}, u32[]{:S(2)}) %collective-permute-start.31) | collective-permute-done | bytes 81952 | tf_op jit(solution)/shard_map/ppermute | solution.py:460
  196.3 2.3 %collective-permute-done.32 = bf16[16,2560]{1,0:T(8,128)(2,1)S(1)} collective-permute-done((bf16[16,2560]{1,0:T(8,128)(2,1)S(1)}, bf16[16,2560]{1,0:T(8,128)(2,1)S(1)}, u32[]{:S(2)}, u32[]{:S(2)}) %collective-permute-start.32) | collective-permute-done | bytes 81952 | tf_op jit(solution)/shard_map/ppermute | solution.py:460
  (197 shorter events, 53.7 us)
Async XLA Ops:
  3.0 14.1 %collective-permute-start = (bf16[16,1664]{1,0:T(8,128)(2,1)S(1)}, bf16[16,1664]{1,0:T(8,128)(2,1)S(1)}, u32[]{:S(2)}, u32[]{:S(2)}) collective-permute-start(bf16[16,1664]{1,0:T(8,128)(2,1)S(1)} %get-tuple-element.133), channel_id=1, source_target_pairs={{0,8},{1,9},{2,10},{3,11},{4,12},{5,13},{6,14},{7,15},{8,0},{9,1},... | collective-permute-start | bytes 159752 | tf_op jit(solution)/shard_map/ppermute | solution.py:460
  6.0 11.9 %collective-permute-start.1 = (bf16[16,1664]{1,0:T(8,128)(2,1)S(1)}, bf16[16,1664]{1,0:T(8,128)(2,1)S(1)}, u32[]{:S(2)}, u32[]{:S(2)}) collective-permute-start(bf16[16,1664]{1,0:T(8,128)(2,1)S(1)} %get-tuple-element.133), channel_id=1, source_target_pairs={{0,16},{1,17},{2,18},{3,19},{4,20},{5,21},{6,22},{7,23},{8,24},{9,... | collective-permute-start | bytes 159752 | tf_op jit(solution)/shard_map/ppermute | solution.py:460
  8.6 10.4 %collective-permute-start.2 = (bf16[16,1664]{1,0:T(8,128)(2,1)S(1)}, bf16[16,1664]{1,0:T(8,128)(2,1)S(1)}, u32[]{:S(2)}, u32[]{:S(2)}) collective-permute-start(bf16[16,1664]{1,0:T(8,128)(2,1)S(1)} %get-tuple-element.133), channel_id=1, source_target_pairs={{0,24},{1,25},{2,26},{3,27},{4,28},{5,29},{6,30},{7,31},{8,16},{9,... | collective-permute-start | bytes 159752 | tf_op jit(solution)/shard_map/ppermute | solution.py:460
  12.4 15.2 %collective-permute-start.7 = (bf16[16,2560]{1,0:T(8,128)(2,1)S(1)}, bf16[16,2560]{1,0:T(8,128)(2,1)S(1)}, u32[]{:S(2)}, u32[]{:S(2)}) collective-permute-start(bf16[16,2560]{1,0:T(8,128)(2,1)S(1)} %get-tuple-element.129), channel_id=1, source_target_pairs={{0,8},{1,9},{2,10},{3,11},{4,12},{5,13},{6,14},{7,15},{8,0},{9,1},... | collective-permute-start | bytes 245768 | tf_op jit(solution)/shard_map/ppermute | solution.py:460
  13.4 14.2 %collective-permute-start.8 = (bf16[16,2560]{1,0:T(8,128)(2,1)S(1)}, bf16[16,2560]{1,0:T(8,128)(2,1)S(1)}, u32[]{:S(2)}, u32[]{:S(2)}) collective-permute-start(bf16[16,2560]{1,0:T(8,128)(2,1)S(1)} %get-tuple-element.129), channel_id=1, source_target_pairs={{0,16},{1,17},{2,18},{3,19},{4,20},{5,21},{6,22},{7,23},{8,24},{9,... | collective-permute-start | bytes 245768 | tf_op jit(solution)/shard_map/ppermute | solution.py:460
  19.1 7.9 %collective-permute-start.16 = (bf16[16,2048]{1,0:T(8,128)(2,1)S(1)}, bf16[16,2048]{1,0:T(8,128)(2,1)S(1)}, u32[]{:S(2)}, u32[]{:S(2)}) collective-permute-start(bf16[16,2048]{1,0:T(8,128)(2,1)S(1)} %get-tuple-element.135), channel_id=1, source_target_pairs={{0,24},{1,25},{2,26},{3,27},{4,28},{5,29},{6,30},{7,31},{8,16},{9,... | collective-permute-start | bytes 196616 | tf_op jit(solution)/shard_map/ppermute | solution.py:460
  25.5 16.6 %collective-permute-start.3 = (bf16[64,1664]{1,0:T(8,128)(2,1)S(1)}, bf16[64,1664]{1,0:T(8,128)(2,1)S(1)}, u32[]{:S(2)}, u32[]{:S(2)}) collective-permute-start(bf16[64,1664]{1,0:T(8,128)(2,1)S(1)} %pad_maximum_fusion.3), channel_id=1, source_target_pairs={{0,4},{1,3},{2,6},{3,1},{4,0},{5,7},{6,2},{7,5},{8,12},{9,11},{10,... | collective-permute-start | bytes 638984 | tf_op jit(solution)/shard_map/ppermute | solution.py:460
  27.0 14.5 %collective-permute-start.17 = (bf16[64,2048]{1,0:T(8,128)(2,1)S(1)}, bf16[64,2048]{1,0:T(8,128)(2,1)S(1)}, u32[]{:S(2)}, u32[]{:S(2)}) collective-permute-start(bf16[64,2048]{1,0:T(8,128)(2,1)S(1)} %pad_maximum_fusion.2), channel_id=1, source_target_pairs={{0,4},{1,3},{2,6},{3,1},{4,0},{5,7},{6,2},{7,5},{8,12},{9,11},{10,... | collective-permute-start | bytes 786440 | tf_op jit(solution)/shard_map/ppermute | solution.py:460
  29.9 10.0 %collective-permute-start.10 = (bf16[64,2560]{1,0:T(8,128)(2,1)S(1)}, bf16[64,2560]{1,0:T(8,128)(2,1)S(1)}, u32[]{:S(2)}, u32[]{:S(2)}) collective-permute-start(bf16[64,2560]{1,0:T(8,128)(2,1)S(1)} %pad_maximum_fusion.1), channel_id=1, source_target_pairs={{0,4},{1,3},{2,6},{3,1},{4,0},{5,7},{6,2},{7,5},{8,12},{9,11},{10,... | collective-permute-start | bytes 983048 | tf_op jit(solution)/shard_map/ppermute | solution.py:460
  39.9 10.7 %collective-permute-start.11 = (bf16[128,2560]{1,0:T(8,128)(2,1)S(1)}, bf16[128,2560]{1,0:T(8,128)(2,1)S(1)}, u32[]{:S(2)}, u32[]{:S(2)}) collective-permute-start(bf16[128,2560]{1,0:T(8,128)(2,1)S(1)} %constant_dynamic-update-slice_fusion.5.own_ref), channel_id=1, source_target_pairs={{0,2},{1,5},{2,0},{3,7},{4,6},{5,1},{6,4},{7,3},{8,10},{9,13},{10,... | collective-permute-start | bytes 1966088 | tf_op jit(solution)/shard_map/ppermute | solution.py:460
  41.5 19.3 %collective-permute-start.18 = (bf16[128,2048]{1,0:T(8,128)(2,1)S(1)}, bf16[128,2048]{1,0:T(8,128)(2,1)}, u32[]{:S(2)}, u32[]{:S(2)}) collective-permute-start(bf16[128,2048]{1,0:T(8,128)(2,1)S(1)} %constant_dynamic-update-slice_fusion.12.own_ref), channel_id=1, source_target_pairs={{0,2},{1,5},{2,0},{3,7},{4,6},{5,1},{6,4},{7,3},{8,10},{9,13},{10,... | collective-permute-start | bytes 1572872 | tf_op jit(solution)/shard_map/ppermute | solution.py:460
  42.7 18.1 %collective-permute-start.4 = (bf16[128,1664]{1,0:T(8,128)(2,1)}, bf16[128,1664]{1,0:T(8,128)(2,1)}, u32[]{:S(2)}, u32[]{:S(2)}) collective-permute-start(bf16[128,1664]{1,0:T(8,128)(2,1)} %constant_dynamic-update-slice_fusion.own_ref), channel_id=1, source_target_pairs={{0,2},{1,5},{2,0},{3,7},{4,6},{5,1},{6,4},{7,3},{8,10},{9,13},{10,... | collective-permute-start | bytes 1277960 | tf_op jit(solution)/shard_map/ppermute | solution.py:460
  44.3 17.1 %collective-permute-start.5 = (bf16[128,1664]{1,0:T(8,128)(2,1)}, bf16[128,1664]{1,0:T(8,128)(2,1)S(1)}, u32[]{:S(2)}, u32[]{:S(2)}) collective-permute-start(bf16[128,1664]{1,0:T(8,128)(2,1)} %constant_dynamic-update-slice_fusion.own_ref), channel_id=1, source_target_pairs={{0,1},{1,0},{2,3},{3,2},{4,5},{5,4},{6,7},{7,6},{8,9},{9,8},{10,11... | collective-permute-start | bytes 1277960 | tf_op jit(solution)/shard_map/ppermute | solution.py:460
  44.3 33.5 %collective-permute-start.12 = (bf16[128,2560]{1,0:T(8,128)(2,1)S(1)}, bf16[128,2560]{1,0:T(8,128)(2,1)S(1)}, u32[]{:S(2)}, u32[]{:S(2)}) collective-permute-start(bf16[128,2560]{1,0:T(8,128)(2,1)S(1)} %constant_dynamic-update-slice_fusion.5.own_ref), channel_id=1, source_target_pairs={{0,1},{1,0},{2,3},{3,2},{4,5},{5,4},{6,7},{7,6},{8,9},{9,8},{10,11... | collective-permute-start | bytes 1966088 | tf_op jit(solution)/shard_map/ppermute | solution.py:460
  50.5 27.2 %collective-permute-start.13 = (bf16[128,2560]{1,0:T(8,128)(2,1)S(1)}, bf16[128,2560]{1,0:T(8,128)(2,1)}, u32[]{:S(2)}, u32[]{:S(2)}) collective-permute-start(bf16[128,2560]{1,0:T(8,128)(2,1)S(1)} %collective-permute-done.11.late_ref), channel_id=1, source_target_pairs={{0,1},{1,0},{2,3},{3,2},{4,5},{5,4},{6,7},{7,6},{8,9},{9,8},{10,11... | collective-permute-start | bytes 1966088 | tf_op jit(solution)/shard_map/ppermute | solution.py:460
  60.8 36.7 %collective-permute-start.19 = (bf16[128,2048]{1,0:T(8,128)(2,1)S(1)}, bf16[128,2048]{1,0:T(8,128)(2,1)}, u32[]{:S(2)}, u32[]{:S(2)}) collective-permute-start(bf16[128,2048]{1,0:T(8,128)(2,1)S(1)} %constant_dynamic-update-slice_fusion.12.own_ref), channel_id=1, source_target_pairs={{0,1},{1,0},{2,3},{3,2},{4,5},{5,4},{6,7},{7,6},{8,9},{9,8},{10,11... | collective-permute-start | bytes 1572872 | tf_op jit(solution)/shard_map/ppermute | solution.py:460
  60.8 36.7 %collective-permute-start.20 = (bf16[128,2048]{1,0:T(8,128)(2,1)}, bf16[128,2048]{1,0:T(8,128)(2,1)}, u32[]{:S(2)}, u32[]{:S(2)}) collective-permute-start(bf16[128,2048]{1,0:T(8,128)(2,1)} %collective-permute-done.18.late_ref), channel_id=1, source_target_pairs={{0,1},{1,0},{2,3},{3,2},{4,5},{5,4},{6,7},{7,6},{8,9},{9,8},{10,11... | collective-permute-start | bytes 1572872 | tf_op jit(solution)/shard_map/ppermute | solution.py:460
  137.6 16.2 %collective-permute-start.33 = (bf16[256,2048]{1,0:T(8,128)(2,1)S(1)}, bf16[256,2048]{1,0:T(8,128)(2,1)S(1)}, u32[]{:S(2)}, u32[]{:S(2)}) collective-permute-start(bf16[256,2048]{1,0:T(8,128)(2,1)S(1)} %get-tuple-element.58), channel_id=1, source_target_pairs={{0,1},{1,0},{2,3},{3,2},{4,5},{5,4},{6,7},{7,6},{8,9},{9,8},{10,11... | collective-permute-start | bytes 3145736 | tf_op jit(solution)/shard_map/ppermute | solution.py:460
  142.7 8.2 %collective-permute-start.22 = (bf16[128,1664]{1,0:T(8,128)(2,1)S(1)}, bf16[128,1664]{1,0:T(8,128)(2,1)S(1)}, u32[]{:S(2)}, u32[]{:S(2)}) collective-permute-start(bf16[128,1664]{1,0:T(8,128)(2,1)S(1)} %slice.233), channel_id=1, source_target_pairs={{0,2},{1,5},{2,0},{3,7},{4,6},{5,1},{6,4},{7,3},{8,10},{9,13},{10,... | collective-permute-start | bytes 1277960 | tf_op jit(solution)/shard_map/ppermute | solution.py:460
  144.6 18.1 %collective-permute-start.27 = (bf16[256,2560]{1,0:T(8,128)(2,1)}, bf16[256,2560]{1,0:T(8,128)(2,1)S(1)}, u32[]{:S(2)}, u32[]{:S(2)}) collective-permute-start(bf16[256,2560]{1,0:T(8,128)(2,1)} %get-tuple-element.56), channel_id=1, source_target_pairs={{0,1},{1,0},{2,3},{3,2},{4,5},{5,4},{6,7},{7,6},{8,9},{9,8},{10,11... | collective-permute-start | bytes 3932168 | tf_op jit(solution)/shard_map/ppermute | solution.py:460
  156.5 11.0 %collective-permute-start.34 = (bf16[128,2048]{1,0:T(8,128)(2,1)}, bf16[128,2048]{1,0:T(8,128)(2,1)}, u32[]{:S(2)}, u32[]{:S(2)}) collective-permute-start(bf16[128,2048]{1,0:T(8,128)(2,1)} %slice.232), channel_id=1, source_target_pairs={{0,2},{1,5},{2,0},{3,7},{4,6},{5,1},{6,4},{7,3},{8,10},{9,13},{10,... | collective-permute-start | bytes 1572872 | tf_op jit(solution)/shard_map/ppermute | solution.py:460
  163.1 17.0 %collective-permute-start.28 = (bf16[128,2560]{1,0:T(8,128)(2,1)S(1)}, bf16[128,2560]{1,0:T(8,128)(2,1)}, u32[]{:S(2)}, u32[]{:S(2)}) collective-permute-start(bf16[128,2560]{1,0:T(8,128)(2,1)S(1)} %slice.231), channel_id=1, source_target_pairs={{0,2},{1,5},{2,0},{3,7},{4,6},{5,1},{6,4},{7,3},{8,10},{9,13},{10,... | collective-permute-start | bytes 1966088 | tf_op jit(solution)/shard_map/ppermute | solution.py:460
  175.7 7.7 %collective-permute-start.37 = (bf16[16,2048]{1,0:T(8,128)(2,1)S(1)}, bf16[16,2048]{1,0:T(8,128)(2,1)S(1)}, u32[]{:S(2)}, u32[]{:S(2)}) collective-permute-start(bf16[16,2048]{1,0:T(8,128)(2,1)S(1)} %get-tuple-element.121), channel_id=1, source_target_pairs={{0,16},{1,17},{2,18},{3,19},{4,20},{5,21},{6,22},{7,23},{8,24},{9,... | collective-permute-start | bytes 196616 | tf_op jit(solution)/shard_map/ppermute | solution.py:460
  188.6 7.6 %collective-permute-start.31 = (bf16[16,2560]{1,0:T(8,128)(2,1)S(1)}, bf16[16,2560]{1,0:T(8,128)(2,1)S(1)}, u32[]{:S(2)}, u32[]{:S(2)}) collective-permute-start(bf16[16,2560]{1,0:T(8,128)(2,1)S(1)} %get-tuple-element.118), channel_id=1, source_target_pairs={{0,16},{1,17},{2,18},{3,19},{4,20},{5,21},{6,22},{7,23},{8,24},{9,... | collective-permute-start | bytes 245768 | tf_op jit(solution)/shard_map/ppermute | solution.py:460
  (45 other events, 406.5 us)

commit v3 on v0

v3 whole, which is shorter than its diff:
```python
import functools

import jax
import jax.numpy as jnp
from jax import lax
from jax.experimental import pallas as pl
from jax.experimental.pallas import tpu as pltpu
from jax.sharding import PartitionSpec as P

D = 512
HEADS = 8
HEAD = 64
FF = 2048
QUARTER = FF // 4
LANES = 128
PAIRS = D // LANES
ROWS = 16
STEP = 10
AXES = ("dp", "fsdp")
VMEM_BYTES = 28 * 1024 * 1024

norm_epsilon = 1e-05
beta_first = 0.9
beta_second = 0.999
adam_epsilon = 1e-08
weight_decay = 0.1
matrix_rate = 0.02
output_rate = 0.1
vector_rate = 0.2
masked_score = -1000000000.0
gelu_scale = 0.7978845608028654
gelu_cubic = 0.044715
FIRST_PAD = 224


def low(values):
    return values.astype(jnp.bfloat16)


def wide(values):
    return values.astype(jnp.float32)


def dot(left, right):
    return lax.dot_general(left, right, (((1,), (0,)), ((), ())), preferred_element_type=jnp.float32)


def dot_rows(left, right):
    return lax.dot_general(left, right, (((1,), (1,)), ((), ())), preferred_element_type=jnp.float32)


def dot_columns(left, right):
    return lax.dot_general(left, right, (((0,), (0,)), ((), ())), preferred_element_type=jnp.float32)


def cost(micros):
    return pl.CostEstimate(flops=int(micros * 1.15e9), bytes_accessed=0, transcendentals=0)


class Refs:
    pass


def call(body, name, grid, micros, ins, outs, scratch=(), continued=None):
    aliases = {}
    if continued is not None:
        for n, entry in enumerate(outs):
            aliases[len(ins)] = n
            ins = ins + [("old_" + entry[0], getattr(continued, entry[0]), pl.BlockSpec(memory_space=pl.ANY))]
    names = [entry[0] for entry in ins] + [entry[0] for entry in outs] + [entry[0] for entry in scratch]

    def kernel(*refs):
        named = Refs()
        for entry, ref in zip(names, refs):
            setattr(named, entry, ref)
        body(named)

    results = pl.pallas_call(
        kernel,
        grid=grid,
        out_shape=[jax.ShapeDtypeStruct(shape, kind) for _, shape, kind, _ in outs],
        in_specs=[spec for _, _, spec in ins],
        out_specs=[spec for _, _, _, spec in outs],
        scratch_shapes=[pltpu.VMEM(shape, kind) for _, shape, kind in scratch],
        compiler_params=pltpu.CompilerParams(vmem_limit_bytes=VMEM_BYTES),
        cost_estimate=cost(micros),
        input_output_aliases=aliases,
        name=name,
    )(*[array for _, array, _ in ins])
    out = Refs()
    for entry, value in zip(outs, results):
        setattr(out, entry[0], value)
    return out


def whole():
    return pl.BlockSpec(memory_space=pltpu.VMEM)


def scalars():
    return pl.BlockSpec(memory_space=pltpu.SMEM)


def row_block(rows, columns, at=0):
    return pl.BlockSpec((rows, columns), lambda i: (i, at))


def fixed_block(rows, columns, at=0):
    return pl.BlockSpec((rows, columns), lambda i: (0, at))


FAR = (0, 8, 16, 24)


def block_device(me, core, place):
    first = jnp.where(core == 0, 4, 2)
    near = (0, first, 6 - first, 6)[place // len(FAR)]
    return me ^ near ^ FAR[place % len(FAR)]


def assemble(me, stacks, targets):
    for stream in range(2):
        for upper in range(2):
            stack = stacks[2 * stream + upper]
            for place in range(8):
                device = block_device(me ^ stream, (me & 1) ^ stream, place + upper * 8)
                rows = pl.ds(pl.multiple_of(device * ROWS, ROWS), ROWS)
                for ref, column in targets:
                    ref[rows, :] = stack[pl.ds(place * ROWS, ROWS), pl.ds(column, ref.shape[1])]


def arrange(me, sources, keep_ref, send_ref):
    for place in range(16):
        here = pl.ds(place * ROWS, ROWS)
        for stream, out in ((0, keep_ref), (1, send_ref)):
            device = block_device(me ^ stream, (me & 1) ^ stream, place)
            rows = pl.ds(pl.multiple_of(device * ROWS, ROWS), ROWS)
            column = 0
            for ref in sources:
                out[here, pl.ds(column, ref.shape[1])] = ref[rows, :].astype(out.dtype)
                column += ref.shape[1]


def arranged(columns):
    shape = (16 * ROWS, columns)
    return [("keep", shape, jnp.float32, fixed_block(*shape)), ("send", shape, jnp.bfloat16, fixed_block(*shape))]


def centre(values):
    centred = values - jnp.mean(values, axis=-1, keepdims=True)
    scale = lax.rsqrt(jnp.mean(centred * centred, axis=-1, keepdims=True) + norm_epsilon)
    return centred * scale, scale


def norm_back(grad, gain, hat, scale):
    inner = grad * gain
    return scale * (
        inner - jnp.mean(inner, axis=-1, keepdims=True) - hat * jnp.mean(inner * hat, axis=-1, keepdims=True)
    )


def masked_rows(order_row, step):
    seq = order_row.shape[1]
    flags = jnp.where(order_row >= step, 1.0, 0.0)
    column = jnp.transpose(jnp.broadcast_to(flags, (LANES, seq)))
    return jnp.concatenate([column] * (D // LANES), axis=1) > 0.5


def pair_split(pair, scale=None):
    lane = lax.broadcasted_iota(jnp.int32, pair.shape, 1)
    values = wide(pair)
    if scale is not None:
        values = values * scale
    return jnp.concatenate([low(jnp.where(lane < HEAD, values, 0.0)), low(jnp.where(lane < HEAD, 0.0, values))], axis=0)


def key_scores(keys, both_queries, length):
    scores = dot_rows(keys, both_queries)
    seq = scores.shape[0]
    tail = scores[FIRST_PAD:]
    row = lax.broadcasted_iota(jnp.int32, tail.shape, 0) + FIRST_PAD
    return jnp.concatenate([scores[:FIRST_PAD], jnp.where(row < length, tail, masked_score)], axis=0)


def load_input(tokens_ref, order_ref, step, vec_ref):
    masked = masked_rows(order_ref[0], step)
    return masked, jnp.where(masked, vec_ref[4:5, :], wide(tokens_ref[...]))


def add_into(ref, index, value, start):
    @pl.when(start)
    def _():
        ref[index] = value

    @pl.when(jnp.logical_not(start))
    def _():
        ref[index] += value


def span_inputs(order, tokens, seq):
    return [
        ("order", order, pl.BlockSpec((1, 1, seq), lambda i: (i, 0, 0))),
        ("tokens", tokens, row_block(seq, D)),
    ]


def attention(scalar, order, tokens, first, spans, front=None):
    count, _, seq = order.shape
    fresh = front is None

    def body(r):
        span = pl.program_id(0)
        at = span + spans[0]
        if fresh:

            @pl.when(span == 0)
            def _():
                stacks = (r.stack0, r.stack1, r.stack2, r.stack3)
                assemble(r.me[0], stacks, ((r.weight, 0), (r.columns, 3 * D)))
                r.vec[...] = jnp.transpose(wide(r.columns[...]))[:8]

        started = load_input(r.tokens, r.order, r.step[at], r.vec)[1]
        normed = low(centre(started)[0] * r.vec[0:1, :] + r.vec[2:3, :])
        r.normed[...] = normed
        r.p[...] = low(dot(normed, r.weight[...]))
        for pair in range(PAIRS):
            lanes = pl.ds(pair * LANES, LANES)
            queries = pair_split(r.p[:, lanes], HEAD**-0.5)
            scores = key_scores(r.p[:, pl.ds(D + pair * LANES, LANES)], queries, r.length[at])
            peak = jnp.max(scores, axis=0, keepdims=True)
            exped = jnp.exp(scores - peak)
            total = jnp.sum(exped, axis=0, keepdims=True)
            probability = low(exped / total)
            r.logs[0, pair : pair + 1, :] = peak + jnp.log(total)
            values = jnp.transpose(r.p[:, pl.ds(2 * D + pair * LANES, LANES)])
            attended = jnp.concatenate(
                [dot(values[:HEAD], probability[:, :seq]), dot(values[HEAD:], probability[:, seq:])], axis=0
            )
            r.attended[:, lanes] = jnp.transpose(low(attended))

    ins = [(name, array, scalars()) for name, array in scalar.items()]
    ins += [
        ("order", order, pl.BlockSpec((1, 1, seq), lambda i: (i + spans[0], 0, 0))),
        ("tokens", tokens, pl.BlockSpec((seq, D), lambda i: (i + spans[0], 0))),
    ]
    def placed(columns):
        return pl.BlockSpec((seq, columns), lambda i: (i + spans[0], 0))

    rows = count * seq
    outs = [
        ("normed", (rows, D), jnp.bfloat16, placed(D)),
        ("p", (rows, 3 * D), jnp.bfloat16, placed(3 * D)),
        ("attended", (rows, D), jnp.bfloat16, placed(D)),
        ("logs", (count, PAIRS, 2 * seq), jnp.float32, pl.BlockSpec((1, PAIRS, 2 * seq), lambda i: (i + spans[0], 0, 0))),
    ]
    scratch = []
    if fresh:
        ins += [("stack%d" % n, stack, whole()) for n, stack in enumerate(first)]
        outs += [
            ("weight", (D, 3 * D), jnp.bfloat16, fixed_block(D, 3 * D)),
            ("vec", (8, D), jnp.float32, fixed_block(8, D)),
        ]
        scratch = [("columns", (D, LANES), jnp.bfloat16)]
    else:
        ins += [("weight", first[0], fixed_block(D, 3 * D)), ("vec", first[1], fixed_block(8, D))]
    return call(body, "attention", (len(spans),), 3 * len(spans), ins, outs, scratch, front)


def hidden_quarter(normed, upstream, up, down):
    hidden = dot(normed, up)
    grad_act = dot_rows(upstream, down)
    squared = hidden * hidden
    tilt = jnp.tanh(hidden * (gelu_scale + (gelu_scale * gelu_cubic) * squared))
    gate = 0.5 + 0.5 * tilt
    active = hidden * gate
    slope = gate + active * (1.0 - tilt) * (gelu_scale + (3.0 * gelu_scale * gelu_cubic) * squared)
    active = low(active)
    grad_hidden = low(grad_act * slope)
    return dot(active, down), dot_rows(grad_hidden, up), dot_columns(normed, grad_hidden), dot_columns(active, upstream)


def quarter_inputs(stacks, quarter):
    ins = []
    for name, group in (("up", quarter % 2), ("down", 2 + quarter % 2)):
        ins += [("%s%d" % (name, n), stack, fixed_block(8 * ROWS, QUARTER, group)) for n, stack in enumerate(stacks)]
    return ins


def quarter_call(quarter, seq, total, scalar, cotangent, stacks, ins, outs, before, after, micros, last=None):
    def body(r):
        span = pl.program_id(0)
        start = span == 0

        @pl.when(start)
        def _():
            assemble(r.me[0], (r.up0, r.up1, r.up2, r.up3), ((r.up, 0),))
            assemble(r.me[0], (r.down0, r.down1, r.down2, r.down3), ((r.down, 0),))

        normed = before(r, span)
        branch, back, grad_up, grad_down = hidden_quarter(normed, r.cot[...], r.up[...], r.down[...])
        add_into(r.grad_up, Ellipsis, grad_up, start)
        add_into(r.grad_down, Ellipsis, grad_down, start)
        after(r, branch, back, start)
        if last is not None:

            @pl.when(span == pl.num_programs(0) - 1)
            def _():
                last(r)

    scratch = [("up", (D, QUARTER), jnp.bfloat16), ("down", (QUARTER, D), jnp.bfloat16)]
    grads = [("grad_up", (D, QUARTER), jnp.float32), ("grad_down", (QUARTER, D), jnp.float32)]
    if last is None:
        outs = outs + [(name, shape, kind, fixed_block(*shape)) for name, shape, kind in grads]
    else:
        scratch = scratch + grads
    if any(entry[0] == "out_grad" for entry in outs):
        outs = [entry for entry in outs if entry[0] != "out_grad"]
        scratch = scratch + [("out_grad", (D, D), jnp.float32)]
    ins = [("me", scalar["me"], scalars()), ("cot", cotangent, row_block(seq, D))] + ins + quarter_inputs(stacks, quarter)
    return call(body, "hidden%d" % quarter, (total // seq,), micros, ins, outs, scratch)


def tall(name, total, seq, kind=jnp.float32):
    return (name, (total, D), kind, row_block(seq, D))


def hidden_forward_back(scalar, order, tokens, cotangent, vec, attended, stacks):
    seq = order.shape[2]
    total = tokens.shape[0]
    rows = row_block(seq, D)

    def enter(r, span):
        @pl.when(span == 0)
        def _():
            assemble(r.me[0], (r.out0, r.out1, r.out2, r.out3), ((r.out_full, 0),))

        middle = load_input(r.tokens, r.order, r.step[span], r.vec)[1] + dot(r.attended[...], r.out_full[...])
        r.middle[...] = middle
        normed = low(centre(middle)[0] * r.vec[1:2, :] + r.vec[3:4, :])
        r.normed[...] = normed
        return normed

    def leave_first(r, branch, back, start):
        r.branch[...] = r.middle[...] + branch
        r.back[...] = back

    ins = [("step", scalar["step"], scalars())] + span_inputs(order, tokens, seq)
    ins += [("vec", vec, fixed_block(8, D)), ("attended", attended, rows)]
    ins += [("out%d" % n, stack, fixed_block(8 * ROWS, D, 4)) for n, stack in enumerate(stacks)]
    outs = [tall("middle", total, seq), tall("normed", total, seq, jnp.bfloat16)]
    outs += [tall("branch", total, seq), tall("back", total, seq)]
    outs += [("out_full", (D, D), jnp.bfloat16, fixed_block(D, D))]
    one = quarter_call(0, seq, total, scalar, cotangent, stacks, ins, outs, enter, leave_first, 7)

    stacks, waits = yield one
    cotangent = tie(cotangent, *waits)

    def carried(last):
        return [("normed", one.normed, rows), ("branch_in", last.branch, rows), ("back_in", last.back, rows)]

    def leave(r, branch, back, start):
        r.branch[...] = r.branch_in[...] + branch
        r.back[...] = r.back_in[...] + back

    def arrange_half(r):
        arrange(r.me[0], (r.old_up, r.grad_up, r.old_down, r.grad_down), r.keep, r.send)

    def old(grads):
        return [("old_up", grads.grad_up, fixed_block(D, QUARTER)), ("old_down", grads.grad_down, fixed_block(QUARTER, D))]

    sums = [tall("branch", total, seq), tall("back", total, seq)]
    take = lambda r, span: r.normed[...]
    two = quarter_call(
        1, seq, total, scalar, cotangent, stacks, carried(one) + old(one), sums + arranged(4 * QUARTER), take, leave, 7, arrange_half
    )
    stacks, waits = yield two
    cotangent = tie(cotangent, *waits)
    three = quarter_call(2, seq, total, scalar, cotangent, stacks, carried(two), sums, take, leave, 7)

    def leave_last(r, branch, back, start):
        @pl.when(start)
        def _():
            r.dvec[...] = jnp.zeros_like(r.dvec)

        r.result[...] = low(r.branch_in[...] + branch)
        back = r.back_in[...] + back
        hat, scale = centre(r.middle[...])
        dmiddle = wide(r.cot[...]) + norm_back(back, r.vec[1:2, :], hat, scale)
        r.dmiddle[...] = dmiddle
        r.dvec[1:2, :] += jnp.sum(back * hat, axis=0, keepdims=True)
        r.dvec[3:4, :] += jnp.sum(back, axis=0, keepdims=True)
        mixed = low(dmiddle)
        r.dattended[...] = low(dot_rows(mixed, r.out_full[...]))
        add_into(r.out_grad, Ellipsis, dot_columns(r.attended[...], mixed), start)

    def arrange_last(r):
        arrange(r.me[0], (r.old_up, r.grad_up, r.old_down, r.grad_down, r.out_grad), r.keep, r.send)

    ins = carried(three) + old(three)
    ins += [("middle", one.middle, rows), ("vec", vec, fixed_block(8, D)), ("attended", attended, rows)]
    ins += [("out_full", one.out_full, fixed_block(D, D))]
    outs = [tall("result", total, seq, jnp.bfloat16), tall("dmiddle", total, seq), tall("dattended", total, seq, jnp.bfloat16)]
    outs += [("dvec", (8, D), jnp.float32, fixed_block(8, D)), ("out_grad", None, None, None)]
    outs += arranged(4 * QUARTER + D)
    stacks, waits = yield three
    cotangent = tie(cotangent, *waits)
    yield quarter_call(3, seq, total, scalar, cotangent, stacks, ins, outs, take, leave_last, 9, arrange_last)


def attention_back_part(scalar, pairs, normed, p, logs, dattended, seq):
    width = len(pairs) * LANES
    at = pairs[0] // len(pairs)
    groups = PAIRS // len(pairs)

    def body(r):
        span = pl.program_id(0)
        pair_gradients(r, pairs, r.length[span], seq, 0)
        add_into(r.grad, Ellipsis, dot_columns(r.normed[...], r.dp[...]), span == 0)

    total = normed.shape[0]
    ins = [("length", scalar["length"], scalars()), ("normed", normed, row_block(seq, D))]
    ins += pair_inputs(p, logs, dattended, seq, width, at, groups)
    outs = [("dp", (total, 3 * width), jnp.bfloat16, row_block(seq, 3 * width))]
    outs += [("grad", (D, 3 * width), jnp.float32, fixed_block(D, 3 * width))]
    return call(body, "attention_back", (total // seq,), 4.5 * len(pairs), ins, outs)


def pair_inputs(p, logs, dattended, seq, width, at, groups):
    return [
        ("q", p, row_block(seq, width, at)),
        ("k", p, row_block(seq, width, at + groups)),
        ("v", p, row_block(seq, width, at + 2 * groups)),
        ("logs", logs, pl.BlockSpec((1, PAIRS, 2 * seq), lambda i: (i, 0, 0))),
        ("dattended", dattended, row_block(seq, width, at)),
    ]


def pair_gradients(r, pairs, length, seq, column):
    width = len(pairs) * LANES
    for n, pair in enumerate(pairs):
        lanes = pl.ds(n * LANES, LANES)
        queries = pair_split(r.q[:, lanes], HEAD**-0.5)
        dattended = pair_split(r.dattended[:, lanes])
        keys = r.k[:, lanes]
        scores = key_scores(keys, queries, length)
        probability = jnp.exp(scores - r.logs[0, pair : pair + 1, :])
        dprobability = dot_rows(r.v[:, lanes], dattended)
        inner = jnp.sum(probability * dprobability, axis=0, keepdims=True)
        dscores = low(probability * (dprobability - inner))
        r.dp[:, pl.ds(column + 2 * width + n * LANES, LANES)] = low(dot(low(probability), dattended))
        r.dp[:, pl.ds(column + width + n * LANES, LANES)] = low(dot(dscores, queries))
        keys = jnp.transpose(low(wide(keys) * HEAD**-0.5))
        dqueries = jnp.concatenate([dot(keys[:HEAD], dscores[:, :seq]), dot(keys[HEAD:], dscores[:, seq:])], axis=0)
        r.dp[:, pl.ds(column + n * LANES, LANES)] = jnp.transpose(low(dqueries))


def attention_back_last(scalar, pairs, normed, p, logs, dattended, seq, order, tokens, vec, dmiddle, weight, dvec, parts):
    width = len(pairs) * LANES
    at = pairs[0] // len(pairs)
    groups = PAIRS // len(pairs)
    total = normed.shape[0]

    def body(r):
        span = pl.program_id(0)
        start = span == 0

        @pl.when(start)
        def _():
            r.dvec[...] = jnp.zeros_like(r.dvec)
            r.dvec[:8, :] = r.dvec_in[...]

        pair_gradients(r, pairs, r.length[span], seq, 0)
        add_into(r.grad, Ellipsis, dot_columns(r.normed[...], r.dp[...]), start)
        back = 0.0
        for n, part in enumerate(parts + [None]):
            dp = r.dp if part is None else getattr(r, "dp%d" % n)
            size = dp.shape[1] // 3
            for kind in range(3):
                columns = pl.ds(kind * D + n * size, size)
                back = back + dot_rows(dp[:, pl.ds(kind * size, size)], r.weight[:, columns])
        masked, started = load_input(r.tokens, r.order, r.step[span], r.vec)
        hat, scale = centre(started)
        dstarted = r.dmiddle[...] + norm_back(back, r.vec[0:1, :], hat, scale)
        r.dvec[0:1, :] += jnp.sum(back * hat, axis=0, keepdims=True)
        r.dvec[2:3, :] += jnp.sum(back, axis=0, keepdims=True)
        r.dvec[4:5, :] += jnp.sum(jnp.where(masked, dstarted, 0.0), axis=0, keepdims=True)
        r.input_grad[...] = jnp.where(masked, 0.0, dstarted)

        @pl.when(span == pl.num_programs(0) - 1)
        def _():
            r.columns[...] = jnp.transpose(r.dvec[...])
            grads = [getattr(r, "grad%d" % n) for n in range(len(parts))]
            arrange(r.me[0], grads + [r.grad, r.columns], r.keep, r.send)

    ins = [(name, array, scalars()) for name, array in scalar.items()] + span_inputs(order, tokens, seq)
    ins += [("normed", normed, row_block(seq, D)), ("vec", vec, fixed_block(8, D)), ("dmiddle", dmiddle, row_block(seq, D))]
    ins += [("weight", weight, fixed_block(D, 3 * D)), ("dvec_in", dvec, fixed_block(8, D))]
    ins += pair_inputs(p, logs, dattended, seq, width, at, groups)
    for n, part in enumerate(parts):
        ins += [("dp%d" % n, part.dp, row_block(seq, part.dp.shape[1]))]
        ins += [("grad%d" % n, part.grad, fixed_block(*part.grad.shape))]
    outs = [tall("input_grad", total, seq)] + arranged(3 * D + LANES)
    scratch = [
        ("dp", (seq, 3 * width), jnp.bfloat16),
        ("grad", (D, 3 * width), jnp.float32),
        ("dvec", (LANES, D), jnp.float32),
        ("columns", (D, LANES), jnp.float32),
    ]
    return call(body, "attention_back_last", (total // seq,), 4.5 * len(pairs) + 4, ins, outs, scratch)


def exchange(values, count, even_mask, odd_mask):
    pairs = [(i, i ^ (odd_mask if i % 2 else even_mask)) for i in range(count)]
    return lax.ppermute(values, AXES, pairs)


def tie(value, *others):
    return lax.optimization_barrier((value, others))[0]


class Gather:
    def __init__(self, piece, count):
        self.piece, self.count, self.direct = piece, count, piece.shape[0] == ROWS

    def far(self):
        if self.direct:
            parts = [self.piece] + [exchange(self.piece, self.count, offset, offset) for offset in FAR[1:]]
            self.piece = jnp.concatenate(parts, axis=0)
        return self.piece

    def near(self, *waits):
        if self.direct:
            taken = exchange(self.piece, self.count, 4, 2)
            self.piece = jnp.concatenate([self.piece, tie(taken, *waits)], axis=0)
        return self.piece

    def middle(self):
        if self.direct:
            self.late = exchange(self.piece, self.count, 2, 4)
            self.other = exchange(self.piece, self.count, 1, 1)
            return self.other
        return self.piece

    def finish(self, *waits):
        if not self.direct:
            return ordered_stacks(self.piece)
        late = tie(self.late, *waits)
        return (self.piece, late, self.other, exchange(late, self.count, 1, 1))


class Scatter:
    def __init__(self, arranged, count, direct):
        self.total, self.send, self.count, self.direct = arranged.keep, arranged.send, count, direct

    def fold(self, even, odd):
        if self.direct:
            total = self.total + wide(exchange(self.send, self.count, even, odd))
            half = total.shape[0] // 2
            self.total, self.send = total[:half], low(total[half:])
        return self.total, self.send

    def core(self):
        return self.fold(1, 1)

    def near(self):
        return self.fold(2, 4)

    def next(self):
        if self.direct:
            self.total = self.total + wide(exchange(self.send, self.count, 4, 2))
        return self.total

    def finish(self):
        if not self.direct:
            self.own = full_piece(self.total, self.send)
            return self.own
        own = self.total[:ROWS]
        for place in range(1, len(FAR)):
            part = low(self.total[place * ROWS : (place + 1) * ROWS])
            own = own + wide(exchange(part, self.count, FAR[place], FAR[place]))
        self.own = own
        return own


def split_units(up, down):
    rows, units = up.shape
    up = up.reshape(rows, units // 64, 4, ROWS)
    down = down.reshape(rows // ROWS, 4, ROWS, D)
    ups = [up[:, :, quarter].reshape(rows, units // 4) for quarter in range(4)]
    downs = [down[:, quarter].reshape(rows, D) for quarter in range(4)]
    return [jnp.concatenate(ups[n : n + 2] + downs[n : n + 2], axis=1) for n in (0, 2)]


def join_units(pieces):
    rows = pieces[0].shape[0]
    groups = [[piece[:, n * QUARTER : (n + 1) * QUARTER] for n in range(4)] for piece in pieces]
    ups = groups[0][:2] + groups[1][:2]
    downs = groups[0][2:] + groups[1][2:]
    up = jnp.stack([group.reshape(rows, QUARTER // ROWS, ROWS) for group in ups], axis=2)
    down = jnp.stack([group.reshape(rows // ROWS, ROWS, D) for group in downs], axis=1)
    return up.reshape(rows, 4 * QUARTER), down.reshape(rows * 4, D)


def stack_order(core):
    near = (0, 4, 2, 6) if core == 0 else (0, 2, 4, 6)
    return [core ^ group ^ offset for group in near for offset in FAR]


def ordered_stacks(piece):
    blocks = piece.reshape(32, ROWS, piece.shape[1])
    stacks = []
    for core in range(2):
        ordered = jnp.stack([blocks[device] for device in stack_order(core)])
        ordered = ordered.reshape(16 * ROWS, piece.shape[1])
        stacks += [ordered[: 8 * ROWS], ordered[8 * ROWS :]]
    return tuple(stacks)


def full_piece(keep, send):
    columns = keep.shape[1]
    blocks = jnp.concatenate([keep, wide(send)], axis=0).reshape(32, ROWS, columns)
    order = stack_order(0) + stack_order(1)
    return jnp.stack([blocks[order.index(device)] for device in range(32)]).reshape(32 * ROWS, columns)


def adam_update(master, gradient, moment, square, step_rate, decay_rate):
    moment_new = beta_first * moment + (1.0 - beta_first) * gradient
    square_new = beta_second * square + (1.0 - beta_second) * gradient * gradient
    corrected = (
        moment_new
        / (1.0 - beta_first**STEP)
        / (jnp.sqrt(square_new / (1.0 - beta_second**STEP)) + adam_epsilon)
    )
    return (moment_new, square_new, master - step_rate * (corrected + decay_rate * master))


def local(
    tokens,
    cotangent,
    reveal_order,
    reveal_step,
    lengths,
    weight_qkv,
    weight_out,
    weight_up,
    weight_down,
    vectors,
    moment_qkv,
    square_qkv,
    moment_out,
    square_out,
    moment_up,
    square_up,
    moment_down,
    square_down,
    moment_vec,
    square_vec,
):
    count = lax.axis_size("dp") * lax.axis_size("fsdp")
    direct = weight_qkv.shape[0] == ROWS and count == 32
    me = lax.axis_index("dp") * lax.axis_size("fsdp") + lax.axis_index("fsdp")
    me = (me if direct else 0 * me).astype(jnp.int32)[None]
    spans, seq = reveal_order.shape
    order = reveal_order.reshape(spans, 1, seq)
    flat = tokens.reshape(spans * seq, D)
    upstream = cotangent.reshape(spans * seq, D)

    halves = [low(weight_qkv), low(weight_out), low(weight_up), low(weight_down), low(vectors).T]
    if not direct:
        halves = [lax.all_gather(half, AXES, axis=0, tiled=True) for half in halves]
    qkv, out, up, down, columns = halves
    columns = jnp.pad(columns, ((0, 0), (0, LANES - columns.shape[1])))
    hidden = split_units(up, down)
    scalar = {"me": me, "step": reveal_step, "length": lengths}

    one = Gather(jnp.concatenate([qkv, columns], axis=1), count)
    one.far()
    one.near()
    two = Gather(tie(jnp.concatenate([hidden[0], out], axis=1), one.middle()), count)
    two.far()
    first = one.finish()
    front = attention(scalar, order, flat, first, range(0, spans // 2))
    two.near(front.logs)
    three = Gather(tie(hidden[1], front.logs), count)
    three.far()
    rear = attention(
        scalar, order, tie(flat, two.piece), (front.weight, front.vec), range(spans // 2, spans), front
    )
    vec, weight = front.vec, front.weight
    two.middle()
    second = two.finish(rear.logs)
    quarters = hidden_forward_back(scalar, order, flat, tie(upstream, three.piece), vec, rear.attended, second)
    three.near(next(quarters).back)
    half_one = quarters.send((second, [three.piece]))
    three.middle()
    third = three.finish(half_one.send)
    quarters.send((third, []))
    sum_one = Scatter(half_one, count, direct)
    half_two = quarters.send((third, sum_one.core()))
    sum_two = Scatter(half_two, count, direct)

    def part(pairs, *waits):
        dattended = tie(half_two.dattended, *waits)
        return attention_back_part(scalar, pairs, rear.normed, rear.p, rear.logs, dattended, seq)

    parts = [part((0,), *sum_one.near())]
    parts += [part((1,), *sum_two.core(), sum_one.next())]
    parts += [part((2,), *sum_two.near(), sum_one.finish())]
    final = attention_back_last(
        scalar, (3,), rear.normed, rear.p, rear.logs, tie(half_two.dattended, sum_two.next()), seq,
        order, flat, vec, half_two.dmiddle, weight, half_two.dvec, parts,
    )
    sum_three = Scatter(final, count, direct)
    for step in (sum_three.core, sum_three.near, sum_three.next):
        step()
    sums = [sum_one.own, sum_two.finish(), sum_three.finish()]
    grad_up, grad_down = join_units(sums[:2])
    order = [3 * pair + kind for kind in range(3) for pair in range(PAIRS)]
    columns = [sums[2][:, n * LANES : (n + 1) * LANES] for n in order]
    grads = (
        jnp.concatenate(columns, axis=1),
        sums[1][:, 4 * QUARTER :],
        grad_up,
        grad_down,
        sums[2][:, 3 * D : 3 * D + vectors.shape[0]],
    )
    if not direct:
        grads = [lax.psum_scatter(grad, AXES, scatter_dimension=0, tiled=True) for grad in grads]
    m_qkv, s_qkv, w_qkv = adam_update(weight_qkv, grads[0], moment_qkv, square_qkv, matrix_rate, weight_decay)
    m_out, s_out, w_out = adam_update(weight_out, grads[1], moment_out, square_out, output_rate, weight_decay)
    m_up, s_up, w_up = adam_update(weight_up, grads[2], moment_up, square_up, matrix_rate, weight_decay)
    m_down, s_down, w_down = adam_update(weight_down, grads[3], moment_down, square_down, matrix_rate, weight_decay)
    m_vec, s_vec, w_vec = adam_update(vectors, grads[4].T, moment_vec, square_vec, vector_rate, 0.0)
    return (
        half_two.result.reshape(tokens.shape),
        final.input_grad.reshape(tokens.shape),
        m_qkv,
        s_qkv,
        w_qkv,
        m_out,
        s_out,
        w_out,
        m_up,
        s_up,
        w_up,
        m_down,
        s_down,
        w_down,
        m_vec,
        s_vec,
        w_vec,
    )


def solution(mesh):
    return jax.shard_map(
        local,
        mesh=mesh,
        in_specs=(
            P(("dp", "fsdp"), None, None),
            P(("dp", "fsdp"), None, None),
            P(("dp", "fsdp"), None),
            P(("dp", "fsdp")),
            P(("dp", "fsdp")),
            P(("dp", "fsdp"), None),
            P(("dp", "fsdp"), None),
            P(("dp", "fsdp"), None),
            P(("dp", "fsdp"), None),
            P(None, ("dp", "fsdp")),
            P(("dp", "fsdp"), None),
            P(("dp", "fsdp"), None),
            P(("dp", "fsdp"), None),
            P(("dp", "fsdp"), None),
            P(("dp", "fsdp"), None),
            P(("dp", "fsdp"), None),
            P(("dp", "fsdp"), None),
            P(("dp", "fsdp"), None),
            P(None, ("dp", "fsdp")),
            P(None, ("dp", "fsdp")),
        ),
        out_specs=(
            P(("dp", "fsdp"), None, None),
            P(("dp", "fsdp"), None, None),
            P(("dp", "fsdp"), None),
            P(("dp", "fsdp"), None),
            P(("dp", "fsdp"), None),
            P(("dp", "fsdp"), None),
            P(("dp", "fsdp"), None),
            P(("dp", "fsdp"), None),
            P(("dp", "fsdp"), None),
            P(("dp", "fsdp"), None),
            P(("dp", "fsdp"), None),
            P(("dp", "fsdp"), None),
            P(("dp", "fsdp"), None),
            P(("dp", "fsdp"), None),
            P(None, ("dp", "fsdp")),
            P(None, ("dp", "fsdp")),
            P(None, ("dp", "fsdp")),
        ),
        check_vma=False,
    )
```

time: 916 us -> 185 us (0.20)
  waiting for transfers between devices: 678 us -> 39.6 us
  matrix products: 81.9 us -> 0 us
  blocking collectives: 81.7 us -> 0 us
  Pallas kernels: 0 us -> 70.7 us
  starting transfers between devices: 0.72 us -> 41.1 us
  other arithmetic: 30.7 us -> 13.2 us
  between operations: 15.2 us -> 1.63 us
    reduce_scatter x4 -> x0, waiting for transfers between devices: 514 us -> none  [the longest x1 141 us: local(): lax.psum_scatter(grad_up, ('dp', 'fsdp'), scatter_dimension=0, tiled=True)]
    unnamed x9 -> x0, waiting for transfers between devices: 108 us -> none
    dot_general x36 -> x0, matrix products: 81.9 us -> none  [the longest x2 9.85 us: backward_pass(): jnp.einsum('csd,fd->csf', down_grad, down_full, preferred_element_type=jn...]
    all_gather x2 -> x0, blocking collectives: 81.7 us -> none  [the longest x1 43.5 us: local(): lax.all_gather(vec_half, ('dp', 'fsdp'), axis=1, tiled=True)]
    pallas_call x0 -> x10, Pallas kernels: none -> 70.7 us  [call(): pl.pallas_call(kernel, grid=grid, out_shape=[jax.ShapeDtypeStruct(shape,...]
    all_gather x3 -> x0, waiting for transfers between devices: 56.8 us -> none  [the longest x1 53.5 us: local(): lax.all_gather(down_half, ('dp', 'fsdp'), axis=0, tiled=True)]
    ppermute x0 -> x39, starting transfers between devices: none -> 41.1 us  [exchange(): return lax.ppermute(values, AXES, pairs)]
    ppermute x0 -> x39, waiting for transfers between devices: none -> 39.6 us  [exchange(): return lax.ppermute(values, AXES, pairs)]
  transfers between devices with their start and end apart: 8 -> 39, of which waited for: 7 -> 18; matrix products, arithmetic and copies ran while one was open for 7% -> 10% of each run, Pallas kernels for 0% -> 28%
where the time goes in v3:
time: 185 us
  Pallas kernels  70.7 us (38%)
  starting transfers between devices  41.1 us (22%)
  waiting for transfers between devices  39.6 us (21%)
  local copies, waits for them, and re-layouts  18.2 us (10%)
  other arithmetic  13.2 us (7%)
    pallas_call x10, Pallas kernels, call(): pl.pallas_call(kernel, grid=grid, out_shape=[jax.ShapeDtypeStruct(shape,...  70.7 us
    ppermute x39, starting transfers between devices, exchange(): return lax.ppermute(values, AXES, pairs)  41.1 us
    ppermute x39, waiting for transfers between devices, exchange(): return lax.ppermute(values, AXES, pairs)  39.6 us
    unnamed x116, local copies, waits for them, and re-layouts  9.25 us
    add x6, other arithmetic, fold(): total = self.total + wide(exchange(self.send, self.count, even, odd))  4.55 us
  transfers between devices with their start and end apart: 39, of which 18 were waited for; matrix products, arithmetic and copies ran while one was open for 10% of the time, Pallas kernels for 28%

profile of v3, /device:TPU:0, one launch (start us, length us, event | category | flops | bytes accessed | tf_op | source)
XLA Modules:
  0.0 184.5 jit_solution(8448418942885839359)
XLA Ops:
  2.4 4.1 %collective-permute-start.1 = (bf16[16,1664]{1,0:T(8,128)(2,1)S(1)}, bf16[16,1664]{1,0:T(8,128)(2,1)S(1)}, u32[]{:S(2)}, u32[]{:S(2)}) collective-permute-start(bf16[16,1664]{1,0:T(8,128)(2,1)S(1)} %get-tuple-element.231), channel_id=1, source_target_pairs={{0,16},{1,17},{2,18},{3,19},{4,20},{5,21},{6,22},{7,23},{8,24},{9,... | collective-permute-start | bytes 159752 | tf_op jit(solution)/shard_map/ppermute | solution.py:514
  10.3 3.0 %slice_reduce_fusion = (bf16[16,32,16]{2,1,0:T(8,128)(2,1)S(1)}, bf16[16,32,16]{2,1,0:T(8,128)(2,1)S(1)}, bf16[16,32,16]{2,1,0:T(8,128)(2,1)S(1)}, bf16[16,32,16]{2,1,0:T(8,128)(2,1)S(1)}) fusion(bf16[16,32,4,16]{3,2,1,0:T(4,128)(2,1)S(1)} %reshape.62), kind=kLoop, calls=%fused_computation.17 | loop fusion | bytes 131072 | tf_op jit(solution)/shard_map/slice | solution.py:589
  16.0 4.1 %collective-permute-done.3 = bf16[64,1664]{1,0:T(8,128)(2,1)S(1)} collective-permute-done((bf16[64,1664]{1,0:T(8,128)(2,1)S(1)}, bf16[64,1664]{1,0:T(8,128)(2,1)S(1)}, u32[]{:S(2)}, u32[]{:S(2)}) %collective-permute-start.3) | collective-permute-done | bytes 213024 | tf_op jit(solution)/shard_map/ppermute | solution.py:514
  22.1 3.7 %collective-permute-start.13 = (bf16[16,2560]{1,0:T(8,128)(2,1)S(1)}, bf16[16,2560]{1,0:T(8,128)(2,1)S(1)}, u32[]{:S(2)}, u32[]{:S(2)}) collective-permute-start(bf16[16,2560]{1,0:T(8,128)(2,1)S(1)} %constant_dynamic-update-slice_fusion.9), channel_id=1, source_target_pairs={{0,24},{1,25},{2,26},{3,27},{4,28},{5,29},{6,30},{7,31},{8,16},{9,... | collective-permute-start | bytes 245768 | tf_op jit(solution)/shard_map/ppermute | solution.py:514
  26.6 1.9 %collective-permute-done.4.refs_6_ = bf16[128,1664]{1,0:T(8,128)(2,1)S(1)} collective-permute-done((bf16[128,1664]{1,0:T(8,128)(2,1)S(1)}, bf16[128,1664]{1,0:T(8,128)(2,1)S(1)}, u32[]{:S(2)}, u32[]{:S(2)}) %collective-permute-start.4) | collective-permute-done | bytes 426016 | tf_op jit(solution)/shard_map/ppermute | solution.py:514
  29.3 2.8 %collective-permute-done.12 = bf16[16,2560]{1,0:T(8,128)(2,1)S(1)} collective-permute-done((bf16[16,2560]{1,0:T(8,128)(2,1)S(1)}, bf16[16,2560]{1,0:T(8,128)(2,1)S(1)}, u32[]{:S(2)}, u32[]{:S(2)}) %collective-permute-start.12) | collective-permute-done | bytes 81952 | tf_op jit(solution)/shard_map/ppermute | solution.py:514
  34.0 5.9 %attention.2 = (bf16[1024,512]{1,0:T(8,128)(2,1)S(1)}, bf16[1024,1536]{1,0:T(8,128)(2,1)S(1)}, bf16[1024,512]{1,0:T(8,128)(2,1)S(1)}, f32[4,4,512]{2,1,0:T(4,128...) custom-call(s32[1]{0:T(128)} %bitcast.refs_0_, s32[4]{0:T(128)S(1)} %copy-done.4, s32[4]{0:T(128)S(1)} %copy-done.5, ...), custom_call_target="tpu_custom_call" | custom-call | flops 6899999744 | tf_op jit(solution)/shard_map/attention/pallas_call | solution.py:78
  39.8 2.5 %collective-permute-start.9 = (bf16[16,2048]{1,0:T(8,128)(2,1)S(1)}, bf16[16,2048]{1,0:T(8,128)(2,1)S(1)}, u32[]{:S(2)}, u32[]{:S(2)}) collective-permute-start(bf16[16,2048]{1,0:T(8,128)(2,1)S(1)} %pad_maximum_fusion.4), channel_id=1, source_target_pairs={{0,24},{1,25},{2,26},{3,27},{4,28},{5,29},{6,30},{7,31},{8,16},{9,... | collective-permute-start | bytes 196616 | tf_op jit(solution)/shard_map/ppermute | solution.py:514
  46.0 5.4 %attention.3 = (bf16[1024,512]{1,0:T(8,128)(2,1)S(1)}, bf16[1024,1536]{1,0:T(8,128)(2,1)S(1)}, bf16[1024,512]{1,0:T(8,128)(2,1)S(1)}, f32[4,4,512]{2,1,0:T(4,128)S(1)}) custom-call(s32[1]{0:T(128)} %bitcast.refs_0_, s32[4]{0:T(128)S(1)} %copy-done.4, s32[4]{0:T(128)S(1)} %copy-done.5, ...), custom_call_target="tpu_custom_call", output_to_operand_aliasing={{0}: (7, {}), {1}: (8, {}), {2}: (9, {}), {3}: (10, {})} | custom-call | flops 6899999744 | tf_op jit(solution)/shard_map/attention/pallas_call | solution.py:78
  53.0 2.0 %collective-permute-done.15.refs_8_.refs_12_.refs_16_ = bf16[128,2560]{1,0:T(8,128)(2,1)S(1)} collective-permute-done((bf16[128,2560]{1,0:T(8,128)(2,1)S(1)}, bf16[128,2560]{1,0:T(8,128)(2,1)S(1)}, u32[]{:S(2)}, u32[]{:S(2)}) %collective-permute-start.15) | collective-permute-done | bytes 655392 | tf_op jit(solution)/shard_map/ppermute | solution.py:514
  57.2 8.8 %hidden0.1 = (f32[1024,512]{1,0:T(8,128)S(1)}, bf16[1024,512]{1,0:T(8,128)(2,1)S(1)}, f32[1024,512]{1,0:T(8,128)S(1)}, f32[1024,512]{1,0:T(8,128)S(1)}, bf16[512...) custom-call(s32[1]{0:T(128)} %bitcast.refs_0_, bf16[1024,512]{1,0:T(8,128)(2,1)S(1)} %bitcast.42, ...), custom_call_target="tpu_custom_call" | custom-call | flops 8049999872 | tf_op jit(solution)/shard_map/hidden0/pallas_call | solution.py:78
  67.4 7.6 %hidden1.1 = (f32[1024,512]{1,0:T(8,128)S(1)}, f32[1024,512]{1,0:T(8,128)S(1)}, f32[256,2048]{1,0:T(8,128)S(1)}, bf16[256,2048]{1,0:T(8,128)(2,1)}) custom-call(s32[1]{0:T(128)} %bitcast.refs_0_, bf16[1024,512]{1,0:T(8,128)(2,1)S(1)} %bitcast.43, bf16[1024,512]{1,0:T(8,128)(2,1)S(1)} %get-tuple-element.88.refs_2_, ...), custom_call_target="tpu_custom_call" | custom-call | flops 8049999872 | tf_op jit(solution)/shard_map/hidden1/pallas_call | solution.py:78
  79.7 7.4 %collective-permute-done.19.refs_6_.refs_10_.refs_12_.refs_16_ = bf16[128,2048]{1,0:T(8,128)(2,1)S(1)} collective-permute-done((bf16[128,2048]{1,0:T(8,128)(2,1)S(1)}, bf16[128,2048]{1,0:T(8,128)(2,1)S(1)}, u32[]{:S(2)}, u32[]{:S(2)}) %collective-permute-start.19) | collective-permute-done | bytes 524320 | tf_op jit(solution)/shard_map/ppermute | solution.py:514
  90.5 6.5 %hidden2.1 = (f32[1024,512]{1,0:T(8,128)S(1)}, f32[1024,512]{1,0:T(8,128)S(1)}, f32[512,512]{1,0:T(8,128)S(1)}, f32[512,512]{1,0:T(8,128)S(1)}) custom-call(s32[1]{0:T(128)} %bitcast.refs_0_, bf16[1024,512]{1,0:T(8,128)(2,1)S(1)} %bitcast.44, bf16[1024,512]{1,0:T(8,128)(2,1)S(1)} %copy-done.19, f32[1024,512]{1,0:T(8,128)S(1)} %copy-done.11, ...), custom_call_target="tpu_custom_call" | custom-call | flops 8049999872 | tf_op jit(solution)/shard_map/hidden2/pallas_call | solution.py:78
  97.0 11.3 %hidden3.1 = (bf16[1024,512]{1,0:T(8,128)(2,1)}, f32[1024,512]{1,0:T(8,128)S(1)}, bf16[1024,512]{1,0:T(8,128)(2,1)S(1)}, f32[8,512]{1,0:T(8,128)S(1)}, f32[256,2...) custom-call(s32[1]{0:T(128)} %bitcast.refs_0_, bf16[1024,512]{1,0:T(8,128)(2,1)S(1)} %bitcast.45, ...), custom_call_target="tpu_custom_call" | custom-call | flops 10350000128 | tf_op jit(solution)/shard_map/hidden3/pallas_call | solution.py:78
  110.2 4.8 %attention_back.3 = (bf16[1024,384]{1,0:T(8,128)(2,1)S(1)}, f32[512,384]{1,0:T(8,128)S(1)}) custom-call(s32[4]{0:T(128)S(1)} %copy-done.5, bf16[1024,512]{1,0:T(8,128)(2,1)S(1)} %copy-done.9, bf16[1024,1536]{1,0:T(8,128)(2,1)S(1)} %copy-done.7, bf16[1024,1536]{1,0:T(8,128)(2,1)S(1)} %copy-done.7, bf16[1024,1536]{1,0:T(8,128)(2,1)S(1)} %copy-done.7, ...), custom_call_target="tpu_custom_call" | custom-call | flops 5175000064 | tf_op jit(solution)/shard_map/attention_back/pallas_call | solution.py:78
  120.7 1.9 %collective-permute-done.29 = bf16[16,2048]{1,0:T(8,128)(2,1)S(1)} collective-permute-done((bf16[16,2048]{1,0:T(8,128)(2,1)S(1)}, bf16[16,2048]{1,0:T(8,128)(2,1)S(1)}, u32[]{:S(2)}, u32[]{:S(2)}) %collective-permute-start.29) | collective-permute-done | bytes 65568 | tf_op jit(solution)/shard_map/ppermute | solution.py:514
  122.6 2.4 %collective-permute-done.28 = bf16[16,2048]{1,0:T(8,128)(2,1)S(1)} collective-permute-done((bf16[16,2048]{1,0:T(8,128)(2,1)S(1)}, bf16[16,2048]{1,0:T(8,128)(2,1)S(1)}, u32[]{:S(2)}, u32[]{:S(2)}) %collective-permute-start.28) | collective-permute-done | bytes 65568 | tf_op jit(solution)/shard_map/ppermute | solution.py:514
  125.1 4.8 %attention_back.4 = (bf16[1024,384]{1,0:T(8,128)(2,1)S(1)}, f32[512,384]{1,0:T(8,128)S(1)}) custom-call(s32[4]{0:T(128)S(1)} %copy-done.5, bf16[1024,512]{1,0:T(8,128)(2,1)S(1)} %copy-done.9, bf16[1024,1536]{1,0:T(8,128)(2,1)S(1)} %copy-done.7, bf16[1024,1536]{1,0:T(8,128)(2,1)S(1)} %copy-done.7, bf16[1024,1536]{1,0:T(8,128)(2,1)S(1)} %copy-done.7, ...), custom_call_target="tpu_custom_call" | custom-call | flops 5175000064 | tf_op jit(solution)/shard_map/attention_back/pallas_call | solution.py:78
  130.7 4.8 %attention_back.5 = (bf16[1024,384]{1,0:T(8,128)(2,1)S(1)}, f32[512,384]{1,0:T(8,128)S(1)}) custom-call(s32[4]{0:T(128)S(1)} %copy-done.5, bf16[1024,512]{1,0:T(8,128)(2,1)S(1)} %copy-done.9, bf16[1024,1536]{1,0:T(8,128)(2,1)S(1)} %copy-done.7, bf16[1024,1536]{1,0:T(8,128)(2,1)S(1)} %copy-done.7, bf16[1024,1536]{1,0:T(8,128)(2,1)S(1)} %copy-done.7, ...), custom_call_target="tpu_custom_call" | custom-call | flops 5175000064 | tf_op jit(solution)/shard_map/attention_back/pallas_call | solution.py:78
  138.2 10.9 %attention_back_last.1 = (f32[1024,512]{1,0:T(8,128)}, f32[256,1664]{1,0:T(8,128)S(1)}, bf16[256,1664]{1,0:T(8,128)(2,1)S(1)}) custom-call(s32[1]{0:T(128)} %bitcast.refs_0_, s32[4]{0:T(128)S(1)} %copy-done.4, s32[4]{0:T(128)S(1)} %copy-done.5, s32[4,1,256]{2,1,0:T(1,128)S(1)} %reshape.64.refs_3_, bf16[1024,512]{1,0:T(8,128)(2,1)S(1)} %bitcast.49, ...), custom_call_target="tpu_custom_call" | custom-call | flops 9774999552 | tf_op jit(solution)/shard_map/attention_back_last/pallas_call | solution.py:78
  159.4 2.8 %collective-permute-done.37 = bf16[16,2560]{1,0:T(8,128)(2,1)S(1)} collective-permute-done((bf16[16,2560]{1,0:T(8,128)(2,1)S(1)}, bf16[16,2560]{1,0:T(8,128)(2,1)S(1)}, u32[]{:S(2)}, u32[]{:S(2)}) %collective-permute-start.37) | collective-permute-done | bytes 81952 | tf_op jit(solution)/shard_map/ppermute | solution.py:514
  168.6 4.5 %collective-permute-done.32 = bf16[64,1664]{1,0:T(8,128)(2,1)S(1)} collective-permute-done((bf16[64,1664]{1,0:T(8,128)(2,1)S(1)}, bf16[64,1664]{1,0:T(8,128)(2,1)S(1)}, u32[]{:S(2)}, u32[]{:S(2)}) %collective-permute-start.32) | collective-permute-done | bytes 213024 | tf_op jit(solution)/shard_map/ppermute | solution.py:514
  178.1 2.3 %collective-permute-done.35 = bf16[16,1664]{1,0:T(8,128)(2,1)S(1)} collective-permute-done((bf16[16,1664]{1,0:T(8,128)(2,1)S(1)}, bf16[16,1664]{1,0:T(8,128)(2,1)S(1)}, u32[]{:S(2)}, u32[]{:S(2)}) %collective-permute-start.35) | collective-permute-done | bytes 53280 | tf_op jit(solution)/shard_map/ppermute | solution.py:514
  (238 shorter events, 66.8 us)
Async XLA Ops:
  2.4 11.8 %collective-permute-start.1 = (bf16[16,1664]{1,0:T(8,128)(2,1)S(1)}, bf16[16,1664]{1,0:T(8,128)(2,1)S(1)}, u32[]{:S(2)}, u32[]{:S(2)}) collective-permute-start(bf16[16,1664]{1,0:T(8,128)(2,1)S(1)} %get-tuple-element.231), channel_id=1, source_target_pairs={{0,16},{1,17},{2,18},{3,19},{4,20},{5,21},{6,22},{7,23},{8,24},{9,... | collective-permute-start | bytes 159752 | tf_op jit(solution)/shard_map/ppermute | solution.py:514
  6.5 7.7 %collective-permute-start = (bf16[16,1664]{1,0:T(8,128)(2,1)S(1)}, bf16[16,1664]{1,0:T(8,128)(2,1)S(1)}, u32[]{:S(2)}, u32[]{:S(2)}) collective-permute-start(bf16[16,1664]{1,0:T(8,128)(2,1)S(1)} %get-tuple-element.231), channel_id=1, source_target_pairs={{0,8},{1,9},{2,10},{3,11},{4,12},{5,13},{6,14},{7,15},{8,0},{9,1},... | collective-permute-start | bytes 159752 | tf_op jit(solution)/shard_map/ppermute | solution.py:514
  20.3 8.2 %collective-permute-start.4 = (bf16[128,1664]{1,0:T(8,128)(2,1)S(1)}, bf16[128,1664]{1,0:T(8,128)(2,1)S(1)}, u32[]{:S(2)}, u32[]{:S(2)}) collective-permute-start(bf16[128,1664]{1,0:T(8,128)(2,1)S(1)} %constant_dynamic-update-slice_fusion.refs_5_), channel_id=1, source_target_pairs={{0,2},{1,5},{2,0},{3,7},{4,6},{5,1},{6,4},{7,3},{8,10},{9,13},{10,... | collective-permute-start | bytes 1277960 | tf_op jit(solution)/shard_map/ppermute | solution.py:514
  22.1 7.2 %collective-permute-start.13 = (bf16[16,2560]{1,0:T(8,128)(2,1)S(1)}, bf16[16,2560]{1,0:T(8,128)(2,1)S(1)}, u32[]{:S(2)}, u32[]{:S(2)}) collective-permute-start(bf16[16,2560]{1,0:T(8,128)(2,1)S(1)} %constant_dynamic-update-slice_fusion.9), channel_id=1, source_target_pairs={{0,24},{1,25},{2,26},{3,27},{4,28},{5,29},{6,30},{7,31},{8,16},{9,... | collective-permute-start | bytes 245768 | tf_op jit(solution)/shard_map/ppermute | solution.py:514
  32.3 12.0 %collective-permute-start.14 = (bf16[64,2560]{1,0:T(8,128)(2,1)S(1)}, bf16[64,2560]{1,0:T(8,128)(2,1)S(1)}, u32[]{:S(2)}, u32[]{:S(2)}) collective-permute-start(bf16[64,2560]{1,0:T(8,128)(2,1)S(1)} %pad_maximum_fusion.1), channel_id=1, source_target_pairs={{0,4},{1,3},{2,6},{3,1},{4,0},{5,7},{6,2},{7,5},{8,12},{9,11},{10,... | collective-permute-start | bytes 983048 | tf_op jit(solution)/shard_map/ppermute | solution.py:514
  39.8 15.3 %collective-permute-start.9 = (bf16[16,2048]{1,0:T(8,128)(2,1)S(1)}, bf16[16,2048]{1,0:T(8,128)(2,1)S(1)}, u32[]{:S(2)}, u32[]{:S(2)}) collective-permute-start(bf16[16,2048]{1,0:T(8,128)(2,1)S(1)} %pad_maximum_fusion.4), channel_id=1, source_target_pairs={{0,24},{1,25},{2,26},{3,27},{4,28},{5,29},{6,30},{7,31},{8,16},{9,... | collective-permute-start | bytes 196616 | tf_op jit(solution)/shard_map/ppermute | solution.py:514
  42.3 12.7 %collective-permute-start.8 = (bf16[16,2048]{1,0:T(8,128)(2,1)S(1)}, bf16[16,2048]{1,0:T(8,128)(2,1)S(1)}, u32[]{:S(2)}, u32[]{:S(2)}) collective-permute-start(bf16[16,2048]{1,0:T(8,128)(2,1)S(1)} %pad_maximum_fusion.4), channel_id=1, source_target_pairs={{0,16},{1,17},{2,18},{3,19},{4,20},{5,21},{6,22},{7,23},{8,24},{9,... | collective-permute-start | bytes 196616 | tf_op jit(solution)/shard_map/ppermute | solution.py:514
  42.9 12.1 %collective-permute-start.7 = (bf16[16,2048]{1,0:T(8,128)(2,1)S(1)}, bf16[16,2048]{1,0:T(8,128)(2,1)S(1)}, u32[]{:S(2)}, u32[]{:S(2)}) collective-permute-start(bf16[16,2048]{1,0:T(8,128)(2,1)S(1)} %pad_maximum_fusion.4), channel_id=1, source_target_pairs={{0,8},{1,9},{2,10},{3,11},{4,12},{5,13},{6,14},{7,15},{8,0},{9,1},... | collective-permute-start | bytes 196616 | tf_op jit(solution)/shard_map/ppermute | solution.py:514
  44.3 11.4 %collective-permute-start.16 = (bf16[128,2560]{1,0:T(8,128)(2,1)S(1)}, bf16[128,2560]{1,0:T(8,128)(2,1)S(1)}, u32[]{:S(2)}, u32[]{:S(2)}) collective-permute-start(bf16[128,2560]{1,0:T(8,128)(2,1)S(1)} %constant_dynamic-update-slice_fusion.14.refs_7_.refs_11_.refs_15_), channel_id=1, source_target_pairs={{0,1},{1,0},{2,3},{3,2},{4,5},{5,4},{6,7},{7,6},{8,9},{9,8},{10,11... | collective-permute-start | bytes 1966088 | tf_op jit(solution)/shard_map/ppermute | solution.py:514
  44.4 10.7 %collective-permute-start.15 = (bf16[128,2560]{1,0:T(8,128)(2,1)S(1)}, bf16[128,2560]{1,0:T(8,128)(2,1)S(1)}, u32[]{:S(2)}, u32[]{:S(2)}) collective-permute-start(bf16[128,2560]{1,0:T(8,128)(2,1)S(1)} %constant_dynamic-update-slice_fusion.14.refs_7_.refs_11_.refs_15_), channel_id=1, source_target_pairs={{0,2},{1,5},{2,0},{3,7},{4,6},{5,1},{6,4},{7,3},{8,10},{9,13},{10,... | collective-permute-start | bytes 1966088 | tf_op jit(solution)/shard_map/ppermute | solution.py:514
  55.1 12.2 %collective-permute-start.10 = (bf16[64,2048]{1,0:T(8,128)(2,1)S(1)}, bf16[64,2048]{1,0:T(8,128)(2,1)S(1)}, u32[]{:S(2)}, u32[]{:S(2)}) collective-permute-start(bf16[64,2048]{1,0:T(8,128)(2,1)S(1)} %get-tuple-element.222), channel_id=1, source_target_pairs={{0,4},{1,3},{2,6},{3,1},{4,0},{5,7},{6,2},{7,5},{8,12},{9,11},{10,... | collective-permute-start | bytes 786440 | tf_op jit(solution)/shard_map/ppermute | solution.py:514
  77.8 9.3 %collective-permute-start.18 = (bf16[256,2048]{1,0:T(8,128)(2,1)}, bf16[256,2048]{1,0:T(8,128)(2,1)}, u32[]{:S(2)}, u32[]{:S(2)}) collective-permute-start(bf16[256,2048]{1,0:T(8,128)(2,1)} %get-tuple-element.93), channel_id=1, source_target_pairs={{0,1},{1,0},{2,3},{3,2},{4,5},{5,4},{6,7},{7,6},{8,9},{9,8},{10,11... | collective-permute-start | bytes 3145736 | tf_op jit(solution)/shard_map/ppermute | solution.py:514
  77.9 9.2 %collective-permute-start.19 = (bf16[128,2048]{1,0:T(8,128)(2,1)S(1)}, bf16[128,2048]{1,0:T(8,128)(2,1)S(1)}, u32[]{:S(2)}, u32[]{:S(2)}) collective-permute-start(bf16[128,2048]{1,0:T(8,128)(2,1)S(1)} %constant_dynamic-update-slice_fusion.19.refs_5_.refs_9_.refs_11_.refs_15_), channel_id=1, source_target_pairs={{0,2},{1,5},{2,0},{3,7},{4,6},{5,1},{6,4},{7,3},{8,10},{9,13},{10,... | collective-permute-start | bytes 1572872 | tf_op jit(solution)/shard_map/ppermute | solution.py:514
  79.7 10.7 %collective-permute-start.20 = (bf16[128,2048]{1,0:T(8,128)(2,1)S(1)}, bf16[128,2048]{1,0:T(8,128)(2,1)S(1)}, u32[]{:S(2)}, u32[]{:S(2)}) collective-permute-start(bf16[128,2048]{1,0:T(8,128)(2,1)S(1)} %constant_dynamic-update-slice_fusion.19.refs_5_.refs_9_.refs_11_.refs_15_), channel_id=1, source_target_pairs={{0,1},{1,0},{2,3},{3,2},{4,5},{5,4},{6,7},{7,6},{8,9},{9,8},{10,11... | collective-permute-start | bytes 1572872 | tf_op jit(solution)/shard_map/ppermute | solution.py:514
  88.8 19.7 %collective-permute-start.25 = (bf16[128,2048]{1,0:T(8,128)(2,1)S(1)}, bf16[128,2048]{1,0:T(8,128)(2,1)S(1)}, u32[]{:S(2)}, u32[]{:S(2)}) collective-permute-start(bf16[128,2048]{1,0:T(8,128)(2,1)S(1)} %slice.348), channel_id=1, source_target_pairs={{0,2},{1,5},{2,0},{3,7},{4,6},{5,1},{6,4},{7,3},{8,10},{9,13},{10,... | collective-permute-start | bytes 1572872 | tf_op jit(solution)/shard_map/ppermute | solution.py:514
  108.3 10.4 %collective-permute-start.22 = (bf16[256,2560]{1,0:T(8,128)(2,1)S(1)}, bf16[256,2560]{1,0:T(8,128)(2,1)S(1)}, u32[]{:S(2)}, u32[]{:S(2)}) collective-permute-start(bf16[256,2560]{1,0:T(8,128)(2,1)S(1)} %get-tuple-element.111), channel_id=1, source_target_pairs={{0,1},{1,0},{2,3},{3,2},{4,5},{5,4},{6,7},{7,6},{8,9},{9,8},{10,11... | collective-permute-start | bytes 3932168 | tf_op jit(solution)/shard_map/ppermute | solution.py:514
  115.9 6.8 %collective-permute-start.29 = (bf16[16,2048]{1,0:T(8,128)(2,1)S(1)}, bf16[16,2048]{1,0:T(8,128)(2,1)S(1)}, u32[]{:S(2)}, u32[]{:S(2)}) collective-permute-start(bf16[16,2048]{1,0:T(8,128)(2,1)S(1)} %get-tuple-element.205), channel_id=1, source_target_pairs={{0,24},{1,25},{2,26},{3,27},{4,28},{5,29},{6,30},{7,31},{8,16},{9,... | collective-permute-start | bytes 196616 | tf_op jit(solution)/shard_map/ppermute | solution.py:514
  117.7 7.3 %collective-permute-start.28 = (bf16[16,2048]{1,0:T(8,128)(2,1)S(1)}, bf16[16,2048]{1,0:T(8,128)(2,1)S(1)}, u32[]{:S(2)}, u32[]{:S(2)}) collective-permute-start(bf16[16,2048]{1,0:T(8,128)(2,1)S(1)} %get-tuple-element.206), channel_id=1, source_target_pairs={{0,16},{1,17},{2,18},{3,19},{4,20},{5,21},{6,22},{7,23},{8,24},{9,... | collective-permute-start | bytes 196616 | tf_op jit(solution)/shard_map/ppermute | solution.py:514
  119.1 10.8 %collective-permute-start.23 = (bf16[128,2560]{1,0:T(8,128)(2,1)S(1)}, bf16[128,2560]{1,0:T(8,128)(2,1)S(1)}, u32[]{:S(2)}, u32[]{:S(2)}) collective-permute-start(bf16[128,2560]{1,0:T(8,128)(2,1)S(1)} %slice.347), channel_id=1, source_target_pairs={{0,2},{1,5},{2,0},{3,7},{4,6},{5,1},{6,4},{7,3},{8,10},{9,13},{10,... | collective-permute-start | bytes 1966088 | tf_op jit(solution)/shard_map/ppermute | solution.py:514
  130.1 7.1 %collective-permute-start.24 = (bf16[64,2560]{1,0:T(8,128)(2,1)S(1)}, bf16[64,2560]{1,0:T(8,128)(2,1)S(1)}, u32[]{:S(2)}, u32[]{:S(2)}) collective-permute-start(bf16[64,2560]{1,0:T(8,128)(2,1)S(1)} %slice.350), channel_id=1, source_target_pairs={{0,4},{1,3},{2,6},{3,1},{4,0},{5,7},{6,2},{7,5},{8,12},{9,11},{10,... | collective-permute-start | bytes 983048 | tf_op jit(solution)/shard_map/ppermute | solution.py:514
  150.8 7.2 %collective-permute-start.36 = (bf16[16,2560]{1,0:T(8,128)(2,1)S(1)}, bf16[16,2560]{1,0:T(8,128)(2,1)S(1)}, u32[]{:S(2)}, u32[]{:S(2)}) collective-permute-start(bf16[16,2560]{1,0:T(8,128)(2,1)S(1)} %get-tuple-element.201), channel_id=1, source_target_pairs={{0,8},{1,9},{2,10},{3,11},{4,12},{5,13},{6,14},{7,15},{8,0},{9,1},... | collective-permute-start | bytes 245768 | tf_op jit(solution)/shard_map/ppermute | solution.py:514
  152.3 7.2 %collective-permute-start.38 = (bf16[16,2560]{1,0:T(8,128)(2,1)S(1)}, bf16[16,2560]{1,0:T(8,128)(2,1)S(1)}, u32[]{:S(2)}, u32[]{:S(2)}) collective-permute-start(bf16[16,2560]{1,0:T(8,128)(2,1)S(1)} %get-tuple-element.202), channel_id=1, source_target_pairs={{0,24},{1,25},{2,26},{3,27},{4,28},{5,29},{6,30},{7,31},{8,16},{9,... | collective-permute-start | bytes 245768 | tf_op jit(solution)/shard_map/ppermute | solution.py:514
  154.1 8.1 %collective-permute-start.37 = (bf16[16,2560]{1,0:T(8,128)(2,1)S(1)}, bf16[16,2560]{1,0:T(8,128)(2,1)S(1)}, u32[]{:S(2)}, u32[]{:S(2)}) collective-permute-start(bf16[16,2560]{1,0:T(8,128)(2,1)S(1)} %get-tuple-element.203), channel_id=1, source_target_pairs={{0,16},{1,17},{2,18},{3,19},{4,20},{5,21},{6,22},{7,23},{8,24},{9,... | collective-permute-start | bytes 245768 | tf_op jit(solution)/shard_map/ppermute | solution.py:514
  156.5 9.4 %collective-permute-start.31 = (bf16[128,1664]{1,0:T(8,128)(2,1)}, bf16[128,1664]{1,0:T(8,128)(2,1)}, u32[]{:S(2)}, u32[]{:S(2)}) collective-permute-start(bf16[128,1664]{1,0:T(8,128)(2,1)} %slice.349), channel_id=1, source_target_pairs={{0,2},{1,5},{2,0},{3,7},{4,6},{5,1},{6,4},{7,3},{8,10},{9,13},{10,... | collective-permute-start | bytes 1277960 | tf_op jit(solution)/shard_map/ppermute | solution.py:514
  (57 other events, 454.3 us)
